TPU v7x, 32 devices: a whole 2x2x4 slice. The times are simulated.
32 devices in a mesh: gx: 4 (over z), gy: 8 (over y, x, core).
Axes of the slice: x: 2, y: 2, z: 4, core: 2. Of those that a mesh axis runs over, the one named last changes fastest.
Arguments:
- x_in: bfloat16 [4096, 768], P(('gx', 'gy')), may hold values from -6 to 6
- norm1_gain: float32 [768], replicated, may hold values from 0.1 to 1.9
- w_query: bfloat16 [768, 768], P('gx', 'gy'), may hold values from -0.21875 to 0.21875
- w_key: bfloat16 [768, 768], P('gx', 'gy'), may hold values from -0.21875 to 0.21875
- w_value: bfloat16 [768, 768], P('gx', 'gy'), may hold values from -0.21875 to 0.21875
- relative_bias_table: float32 [32, 12], replicated, may hold values from -4 to 4
- w_out: bfloat16 [768, 768], P('gy', 'gx'), may hold values from -1.75 to 1.75
- norm2_gain: float32 [768], P('gx'), may hold values from 0.1 to 1.9
- w_router: float32 [768, 32], P('gx'), may hold values from -0.15625 to 0.15625
- w_hidden: bfloat16 [768, 98304], P('gx', 'gy'), may hold values from -0.21875 to 0.21875
- w_back: bfloat16 [768, 98304], P('gx', 'gy'), may hold values from -6 to 6
- expert_choice: int32 [4096], replicated, may hold values from 0 to 31
- doc_ids: int32 [4096], P('gx'), may hold values from 0 to 11, as said below
- grad_out: bfloat16 [4096, 768], P(('gx', 'gy')), may hold values from -6 to 6
Outputs:
- block_out: float32 [4096, 768], P(('gx', 'gy'))
- grad_input: float32 [4096, 768], P(('gx', 'gy'))
- grad_norm1: float32 [768], replicated
- grad_query: float32 [768, 768], P('gx', 'gy')
- grad_key: float32 [768, 768], P('gx', 'gy')
- grad_value: float32 [768, 768], P('gx', 'gy')
- grad_table: float32 [32, 12], replicated
- grad_out_proj: float32 [768, 768], P('gy', 'gx')
- grad_norm2: float32 [768], P('gx')
- grad_router: float32 [768, 32], P('gx')
- grad_hidden: float32 [768, 98304], P('gx', 'gy')
- grad_back: float32 [768, 98304], P('gx', 'gy')
Inputs may be any that keep to these rules, and one draw needn't show every extreme that they name: doc_ids never fall along the tokens; each sequence of 1024 tokens holds three documents, the middle one starting within the sequence's first 128 tokens and ending within its last 128.
All inputs are finite; a program needn't handle non-finite values.
Results may differ from a plain program's by a relative error of at most 0.014.
Values may be sent and summed in bfloat16 or wider, within the bound.
A program may use at most 384 MiB of HBM per device.

v0:
```python
import math

import jax
import jax.numpy as jnp
from jax import lax
from jax.sharding import PartitionSpec as P

D = 768
HEADS = 12
HSIZE = 64
EXPERTS = 32
WINDOW = 1024


epsilon = 1e-06
far_steps = (12, 16, 23, 32, 46, 64, 91)
highest = lax.Precision.HIGHEST


def passed_along(value, axis, steps):
    count = lax.axis_size(axis)
    first, last = (max(0, -steps), min(count, count - steps))
    return lax.ppermute(value, axis, [(source, source + steps) for source in range(first, last)])


def bucket_ids(offset):
    ahead_part = (offset > 0).astype(jnp.int32) * 16
    distance = jnp.abs(offset)
    far_part = 8 + sum(((distance >= threshold).astype(jnp.int32) for threshold in far_steps))
    return ahead_part + jnp.where(distance < 8, distance, far_part)


def width_total(values):
    return lax.psum(values, "gx")


def token_rows(block_part):
    return lax.all_gather(block_part, "gy", axis=0, tiled=True)


def width_rows(block_part):
    return lax.all_gather(block_part, "gx", axis=0, tiled=True)


def width_sums(term_fn, row_number):
    return lax.psum_scatter(
        term_fn(jnp.int32(0), lax.axis_size("gx") * row_number),
        "gx",
        scatter_dimension=0,
        tiled=True,
    )


def token_sums(term_fn, row_number):
    return lax.psum_scatter(
        term_fn(jnp.int32(0), lax.axis_size("gy") * row_number),
        "gy",
        scatter_dimension=0,
        tiled=True,
    )


def collect_window(own_pair, reach):
    window_parts = []
    for offset_step in range(-reach, reach + 1):
        if offset_step == 0:
            window_parts.append(own_pair)
        else:
            window_parts.append(passed_along(own_pair, "gy", -offset_step))
    return jnp.concatenate(window_parts, axis=0)


def return_window(partials, reach, head_rows):
    combined = partials[reach * head_rows : (reach + 1) * head_rows]
    for offset_step in range(-reach, reach + 1):
        if offset_step != 0:
            start = (offset_step + reach) * head_rows
            combined = combined + passed_along(
                partials[start : start + head_rows], "gy", offset_step
            )
    return combined


def head_scores(query_heads, key_heads, bias_terms, allowed, score_scale):
    raw_scores = jnp.einsum(
        "qhd,khd->hqk", query_heads, key_heads, preferred_element_type=jnp.float32
    )
    return jnp.where(allowed[None], raw_scores * score_scale + bias_terms, -1000000000.0)


def rows_cols(blocks, width_devs, token_devs):
    grid = blocks.reshape(width_devs, token_devs, blocks.shape[1], blocks.shape[2])
    return jnp.transpose(grid, (0, 2, 1, 3)).reshape(
        width_devs * blocks.shape[1], token_devs * blocks.shape[2]
    )


def cols_rows(blocks, width_devs, token_devs):
    grid = blocks.reshape(width_devs, token_devs, blocks.shape[1], blocks.shape[2])
    return jnp.transpose(grid, (1, 2, 0, 3)).reshape(
        token_devs * blocks.shape[1], width_devs * blocks.shape[2]
    )


def grid_rows_cols(complete, width_devs, token_devs):
    row_total, col_total = complete.shape
    grid = complete.reshape(
        width_devs, row_total // width_devs, token_devs, col_total // token_devs
    )
    return jnp.transpose(grid, (0, 2, 1, 3)).reshape(
        width_devs * token_devs, row_total // width_devs, col_total // token_devs
    )


def grid_cols_rows(complete, width_devs, token_devs):
    row_total, col_total = complete.shape
    grid = complete.reshape(
        token_devs, row_total // token_devs, width_devs, col_total // width_devs
    )
    return jnp.transpose(grid, (2, 0, 1, 3)).reshape(
        width_devs * token_devs, row_total // token_devs, col_total // width_devs
    )


def spread_rows(partial_sum, column, group_count):
    picked_row = (jnp.arange(group_count, dtype=jnp.int32) == column).astype(jnp.float32)
    return picked_row.reshape((group_count,) + (1,) * partial_sum.ndim) * partial_sum[None]


def take_rows(table, index):
    return jnp.take(table, index, axis=0, mode="fill", fill_value=0)


def local(
    x_in,
    norm1_gain,
    w_query,
    w_key,
    w_value,
    relative_bias_table,
    w_out,
    norm2_gain,
    w_router,
    w_hidden,
    w_back,
    expert_choice,
    doc_ids,
    grad_out,
):
    token_devs = lax.axis_size("gy")
    width_devs = lax.axis_size("gx")
    member = lax.axis_index("gy")
    column = lax.axis_index("gx")
    local_count = x_in.shape[0]
    width_cols = w_router.shape[0]
    own_rows = local_count * width_devs
    all_tokens = own_rows * token_devs
    seq_len = local_count * token_devs
    experts = EXPERTS
    capacity = all_tokens * 5 // (4 * experts)
    score_scale = HSIZE ** (-0.5)
    reach = min((WINDOW + local_count - 2) // local_count, token_devs - 1)
    key_count = (2 * reach + 1) * local_count
    whole_weights = (
        lax.all_gather(w_query[None], ("gx", "gy"), axis=0, tiled=True),
        lax.all_gather(w_key[None], ("gx", "gy"), axis=0, tiled=True),
        lax.all_gather(w_value[None], ("gx", "gy"), axis=0, tiled=True),
        lax.all_gather(w_out[None], ("gx", "gy"), axis=0, tiled=True),
    )
    qkv_full = jnp.concatenate(
        [
            rows_cols(whole_weights[0], width_devs, token_devs),
            rows_cols(whole_weights[1], width_devs, token_devs),
            rows_cols(whole_weights[2], width_devs, token_devs),
        ],
        axis=1,
    )
    out_full = cols_rows(whole_weights[3], width_devs, token_devs)
    head_width = out_full.shape[0]
    inputs_row = x_in.astype(jnp.float32)
    scale_first = lax.rsqrt(jnp.mean(inputs_row * inputs_row, axis=-1, keepdims=True) + epsilon)
    normed_first = (inputs_row * scale_first * norm1_gain).astype(jnp.bfloat16)
    qkv_rows = jnp.dot(normed_first, qkv_full, preferred_element_type=jnp.float32).astype(
        jnp.bfloat16
    )
    query_heads = qkv_rows[:, :head_width].reshape(local_count, HEADS, HSIZE)
    pair_window = collect_window(
        qkv_rows[:, head_width:].reshape(local_count, 2, head_width), reach
    )
    key_heads = pair_window[:, 0].reshape(key_count, HEADS, HSIZE)
    value_heads = pair_window[:, 1].reshape(key_count, HEADS, HSIZE)
    query_pos = member * local_count + jnp.arange(local_count, dtype=jnp.int32)
    key_pos = (member - reach) * local_count + jnp.arange(key_count, dtype=jnp.int32)
    offset = key_pos[None, :] - query_pos[:, None]
    buckets = bucket_ids(offset)
    bias_terms = jnp.take(jnp.transpose(relative_bias_table), buckets, axis=1)
    no_doc = jnp.full((reach * local_count,), -1, jnp.int32)
    doc_padded = jnp.concatenate([no_doc, doc_ids, no_doc], axis=0)
    key_docs = lax.dynamic_slice_in_dim(doc_padded, member * local_count, key_count, 0)
    query_docs = lax.dynamic_slice_in_dim(doc_ids, member * local_count, local_count, 0)
    allowed = (jnp.abs(offset) < WINDOW) & (query_docs[:, None] == key_docs[None, :])
    attention_scores = head_scores(query_heads, key_heads, bias_terms, allowed, score_scale)
    row_peak = jnp.max(attention_scores, axis=-1, keepdims=True)
    shifted = jnp.exp(attention_scores - row_peak)
    row_sum = jnp.sum(shifted, axis=-1, keepdims=True)
    log_total = row_peak + jnp.log(row_sum)
    weights_reduced_precision = (shifted / row_sum).astype(jnp.bfloat16)
    attended = jnp.einsum(
        "hqk,khd->qhd", weights_reduced_precision, value_heads, preferred_element_type=jnp.float32
    )
    attended_low = attended.reshape(local_count, head_width).astype(jnp.bfloat16)
    attn_low = jnp.dot(attended_low, out_full, preferred_element_type=jnp.float32).astype(
        jnp.bfloat16
    )
    arrived = lax.all_to_all(
        jnp.stack([x_in, attn_low, grad_out], axis=1), "gx", split_axis=2, concat_axis=0, tiled=True
    )
    inputs = arrived[:, 0].astype(jnp.float32)
    grad_rows = arrived[:, 2].astype(jnp.float32)
    hidden_first = inputs + arrived[:, 1].astype(jnp.float32)
    scale_second = lax.rsqrt(
        width_total(jnp.sum(hidden_first * hidden_first, axis=-1)) / D + epsilon
    )[:, None]
    normed_second = hidden_first * scale_second * norm2_gain
    logits = width_total(jnp.dot(normed_second, w_router, precision=highest))
    router = jax.nn.softmax(logits, axis=-1)
    expert_iota = jnp.arange(experts, dtype=jnp.int32)
    tok_block = math.gcd(all_tokens, 128)
    block_count = all_tokens // tok_block
    chosen_rows = expert_iota[:, None] == expert_choice[None, :]
    chosen_low = chosen_rows.astype(jnp.bfloat16).reshape(experts, block_count, tok_block)
    block_iota = jnp.arange(tok_block, dtype=jnp.int32)
    upper = (block_iota[:, None] <= block_iota[None, :]).astype(jnp.bfloat16)
    inside_count = jnp.einsum("ebi,ij->ebj", chosen_low, upper, preferred_element_type=jnp.float32)
    block_totals = inside_count[:, :, tok_block - 1]
    earlier_blocks = jnp.cumsum(block_totals, axis=1) - block_totals
    counted = (inside_count + earlier_blocks[:, :, None]).reshape(experts, all_tokens)
    position = (jnp.sum(jnp.where(chosen_rows, counted, 0.0), axis=0) - 1.0).astype(jnp.int32)
    kept_all = position < capacity
    slot_all = jnp.where(kept_all, expert_choice * capacity + position, experts * capacity)
    source = (
        jnp.full((experts * capacity + 1,), all_tokens, jnp.int32)
        .at[slot_all]
        .set(jnp.arange(all_tokens, dtype=jnp.int32))[: experts * capacity]
    )
    source_seq = source // seq_len
    source_inner = source % seq_len
    source_rows = jnp.where(
        source < all_tokens,
        source_inner // local_count * own_rows
        + source_seq * local_count
        + source_inner % local_count,
        all_tokens,
    )
    row_iota = jnp.arange(all_tokens, dtype=jnp.int32)
    global_of_row = (
        row_iota // local_count % width_devs * seq_len
        + row_iota // own_rows * local_count
        + row_iota % local_count
    )
    slot_rows = jnp.take(slot_all, global_of_row)
    own_global = lax.dynamic_slice_in_dim(global_of_row, member * own_rows, own_rows, 0)
    picked_mine = jnp.take(expert_choice, own_global)[:, None] == expert_iota[None, :]
    gate_value = jnp.sum(jnp.where(picked_mine, router, 0.0), axis=-1)
    second_rows = token_rows(normed_second.astype(jnp.bfloat16))
    hidden_weight = jnp.transpose(w_hidden.reshape(width_cols, -1, experts), (2, 0, 1))
    back_weight = jnp.transpose(w_back.reshape(width_cols, -1, experts), (2, 1, 0))
    expert_rows = experts // width_devs
    slot_in = take_rows(second_rows, source_rows).reshape(experts, capacity, width_cols)

    def hidden_term(first_row, row_count):
        return jnp.einsum(
            "ecd,edf->ecf", slot_in, hidden_weight, preferred_element_type=jnp.float32
        )

    pre_block = width_sums(hidden_term, expert_rows)
    act_rows = width_rows(jax.nn.gelu(pre_block).astype(jnp.bfloat16))
    expert_out = jnp.einsum(
        "ecf,efd->ecd", act_rows, back_weight, preferred_element_type=jnp.float32
    ).reshape(experts * capacity, width_cols)

    def route_term(first_row, row_count):
        return take_rows(expert_out, slot_rows)

    routed = token_sums(route_term, own_rows)
    block_out = hidden_first + gate_value[:, None] * routed
    gate_grad = width_total(jnp.sum(grad_rows * routed, axis=-1))
    route_rows = token_rows((grad_rows * gate_value[:, None]).astype(jnp.bfloat16))
    gelu_pair = jax.vjp(jax.nn.gelu, pre_block)
    slot_grad = take_rows(route_rows, source_rows).reshape(experts, capacity, width_cols)
    back_grads = jnp.einsum("ecf,ecd->efd", act_rows, slot_grad, preferred_element_type=jnp.float32)

    def act_term(first_row, row_count):
        return jnp.einsum(
            "ecd,efd->ecf", slot_grad, back_weight, preferred_element_type=jnp.float32
        )

    act_grad = width_sums(act_term, expert_rows)
    pre_rows = width_rows(gelu_pair[1](act_grad)[0].astype(jnp.bfloat16))
    hidden_gradient_rows = jnp.einsum(
        "ecd,ecf->edf", slot_in, pre_rows, preferred_element_type=jnp.float32
    )
    slot_in_grad = jnp.einsum(
        "ecf,edf->ecd", pre_rows, hidden_weight, preferred_element_type=jnp.float32
    ).reshape(experts * capacity, width_cols)

    def back_route_term(first_row, row_count):
        return take_rows(slot_in_grad, slot_rows)

    back_routed = token_sums(back_route_term, own_rows)
    grad_hidden = jnp.transpose(hidden_gradient_rows, (1, 2, 0)).reshape(width_cols, -1)
    grad_back = jnp.transpose(back_grads, (2, 1, 0)).reshape(width_cols, -1)
    logit_grad = router * (
        gate_grad[:, None] * picked_mine.astype(jnp.float32) - (gate_value * gate_grad)[:, None]
    )
    second_grad = back_routed + jnp.einsum("re,de->rd", logit_grad, w_router, precision=highest)
    router_part = jnp.einsum("rd,re->de", normed_second, logit_grad, precision=highest)
    norm2_part = jnp.sum(second_grad * hidden_first * scale_second, axis=0)
    gained_second = second_grad * norm2_gain
    row_dot_second = width_total(jnp.sum(gained_second * hidden_first, axis=-1))[:, None]
    hidden_grad = (
        grad_rows
        + scale_second * gained_second
        - hidden_first * scale_second**3 * row_dot_second / D
    )
    out_rows, hidden_rows = (
        lax.all_to_all(block_out, "gx", split_axis=0, concat_axis=1, tiled=True),
        lax.all_to_all(hidden_grad, "gx", split_axis=0, concat_axis=1, tiled=True),
    )
    attn_grad = hidden_rows.astype(jnp.bfloat16)
    grad_out_full = jnp.einsum(
        "rf,rd->fd", attended_low, attn_grad, preferred_element_type=jnp.float32
    )
    attended_grad = (
        jnp.einsum("rd,fd->rf", attn_grad, out_full, preferred_element_type=jnp.float32)
        .astype(jnp.bfloat16)
        .reshape(local_count, HEADS, HSIZE)
    )
    scores_again = head_scores(query_heads, key_heads, bias_terms, allowed, score_scale)
    probs_again = jnp.exp(scores_again - log_total)
    value_grad = jnp.einsum(
        "hqk,qhd->khd",
        probs_again.astype(jnp.bfloat16),
        attended_grad,
        preferred_element_type=jnp.float32,
    )
    prob_grad = jnp.einsum(
        "qhd,khd->hqk", attended_grad, value_heads, preferred_element_type=jnp.float32
    )
    score_gradient = (
        probs_again * (prob_grad - jnp.sum(probs_again * prob_grad, axis=-1, keepdims=True))
    ).astype(jnp.bfloat16)
    query_grad = (
        jnp.einsum("hqk,khd->qhd", score_gradient, key_heads, preferred_element_type=jnp.float32)
        * score_scale
    ).astype(jnp.bfloat16)
    key_grad = (
        jnp.einsum("hqk,qhd->khd", score_gradient, query_heads, preferred_element_type=jnp.float32)
        * score_scale
    )
    band_low = max(0, reach * local_count - 90)
    band_high = min(key_count, reach * local_count + local_count + 90)
    bucket_iota = jnp.arange(relative_bias_table.shape[0], dtype=jnp.int32)
    band_onehot = (buckets[None, :, band_low:band_high] == bucket_iota[:, None, None]).astype(
        jnp.bfloat16
    )
    table_near = jnp.einsum(
        "ivt,zvt->zi",
        score_gradient[:, :, band_low:band_high],
        band_onehot,
        preferred_element_type=jnp.float32,
    )
    left_far = jnp.sum(score_gradient[:, :, :band_low].astype(jnp.float32), axis=(1, 2))
    right_far = jnp.sum(score_gradient[:, :, band_high:].astype(jnp.float32), axis=(1, 2))
    table_part = (
        table_near
        + (bucket_iota == 15).astype(jnp.float32)[:, None] * left_far[None, :]
        + (bucket_iota == 31).astype(jnp.float32)[:, None] * right_far[None, :]
    )
    pair_grads = return_window(
        jnp.stack(
            [key_grad.reshape(key_count, head_width), value_grad.reshape(key_count, head_width)],
            axis=1,
        ),
        reach,
        local_count,
    )
    qkv_grad = jnp.concatenate(
        [
            query_grad.reshape(local_count, head_width),
            pair_grads.astype(jnp.bfloat16).reshape(local_count, 2 * head_width),
        ],
        axis=1,
    )
    qkv_grads = jnp.einsum("rd,rc->dc", normed_first, qkv_grad, preferred_element_type=jnp.float32)
    first_grad = jnp.einsum("rc,dc->rd", qkv_grad, qkv_full, preferred_element_type=jnp.float32)
    norm1_part = jnp.sum(first_grad * inputs_row * scale_first, axis=0)
    gained_first = first_grad * norm1_gain
    row_dot_first = jnp.sum(gained_first * inputs_row, axis=-1, keepdims=True)
    input_rows = (
        hidden_rows + scale_first * gained_first - inputs_row * scale_first**3 * row_dot_first / D
    )
    summed = lax.psum(
        (
            norm1_part,
            table_part,
            spread_rows(norm2_part, column, width_devs),
            spread_rows(router_part, column, width_devs),
        ),
        ("gx", "gy"),
    )
    grad_norm1 = summed[0]
    grad_table = summed[1]
    grad_norm2 = lax.dynamic_index_in_dim(summed[2], column, 0, keepdims=False)
    grad_router = lax.dynamic_index_in_dim(summed[3], column, 0, keepdims=False)
    weight_parts = (
        lax.psum_scatter(
            grid_rows_cols(qkv_grads[:, :head_width], width_devs, token_devs),
            ("gx", "gy"),
            scatter_dimension=0,
            tiled=True,
        ),
        lax.psum_scatter(
            grid_rows_cols(qkv_grads[:, head_width : 2 * head_width], width_devs, token_devs),
            ("gx", "gy"),
            scatter_dimension=0,
            tiled=True,
        ),
        lax.psum_scatter(
            grid_rows_cols(qkv_grads[:, 2 * head_width :], width_devs, token_devs),
            ("gx", "gy"),
            scatter_dimension=0,
            tiled=True,
        ),
        lax.psum_scatter(
            grid_cols_rows(grad_out_full, width_devs, token_devs),
            ("gx", "gy"),
            scatter_dimension=0,
            tiled=True,
        ),
    )
    return (
        out_rows,
        input_rows,
        grad_norm1,
        weight_parts[0][0],
        weight_parts[1][0],
        weight_parts[2][0],
        grad_table,
        weight_parts[3][0],
        grad_norm2,
        grad_router,
        grad_hidden,
        grad_back,
    )


def solution(mesh):
    return jax.shard_map(
        local,
        mesh=mesh,
        in_specs=(
            P(("gx", "gy"), None),
            P(),
            P("gx", "gy"),
            P("gx", "gy"),
            P("gx", "gy"),
            P(),
            P("gy", "gx"),
            P("gx"),
            P("gx", None),
            P("gx", "gy"),
            P("gx", "gy"),
            P(),
            P("gx"),
            P(("gx", "gy"), None),
        ),
        out_specs=(
            P(("gx", "gy"), None),
            P(("gx", "gy"), None),
            P(),
            P("gx", "gy"),
            P("gx", "gy"),
            P("gx", "gy"),
            P(),
            P("gy", "gx"),
            P("gx"),
            P("gx", None),
            P("gx", "gy"),
            P("gx", "gy"),
        ),
        check_vma=False,
    )
```

profile of v0, /device:TPU:0, one launch (start us, length us, event | category | flops | bytes accessed | tf_op | source)
XLA Modules:
  0.0 2596.2 jit_solution(18252264465086320501)
XLA Ops:
  14.6 54.0 %all-gather.21.cloned.1.call-done = bf16[6144,96]{1,0:T(8,128)(2,1)} async-done(((bf16[192,96]{1,0:T(8,128)(2,1)}), bf16[6144,96]{1,0:T(8,128)(2,1)}) %all-gather.21.cloned.1.call-update) | async-done | bytes 1179664 | tf_op jit(solution)/shard_map/all_gather | solution.py:165
  72.3 53.0 %all-gather.23.cloned.1.call-done = bf16[6144,96]{1,0:T(8,128)(2,1)} async-done(((bf16[192,96]{1,0:T(8,128)(2,1)}), bf16[6144,96]{1,0:T(8,128)(2,1)}) %all-gather.23.cloned.1.call-update) | async-done | bytes 1179664 | tf_op jit(solution)/shard_map/all_gather | solution.py:166
  129.9 52.2 %all-gather.25.cloned.1.call-done = bf16[6144,96]{1,0:T(8,128)(2,1)} async-done(((bf16[192,96]{1,0:T(8,128)(2,1)}), bf16[6144,96]{1,0:T(8,128)(2,1)}) %all-gather.25.cloned.1.call-update) | async-done | bytes 1179664 | tf_op jit(solution)/shard_map/all_gather | solution.py:167
  190.9 3.9 collective-permute-start
  202.6 811.7 %gather_fusion = f32[245760,12]{1,0:T(8,128)} fusion(f32[12,32]{0,1:T(8,128)S(1)} %bitcast.216, s32[245760]{0:T(1024)S(1)} %copy-done.19), kind=kCustom, calls=%fused_computation.4 | custom fusion | bytes 24576000 | tf_op jit(solution)/shard_map/jit(_take)/gather | solution.py:196
  1014.2 67.6 %copy.129 = f32[128,1920,12]{1,0,2:T(8,128)} copy(f32[128,1920,12]{2,1,0:T(8,128)} %bitcast.11) | data formatting | bytes 23592960 | tf_op jit(solution)/shard_map/jit(_take)/gather | solution.py:196
  1106.2 10.6 collective-permute-done.8
  1119.3 23.1 collective-permute-done.10
  1144.6 9.4 fusion.161
  1154.1 12.4 copy.92
  1166.4 10.8 copy.94
  1177.3 7.9 fusion.162
  1202.0 10.5 all-to-all-done
  1212.8 9.9 psum.56
  1224.0 36.1 %all-reduce.4.cloned.1.call-done = f32[512,32]{0,1:T(8,128)} async-done(((f32[512,32]{0,1:T(8,128)}), f32[512,32]{0,1:T(8,128)}) %all-reduce.4.cloned.1.call-update) | async-done | bytes 65552 | tf_op jit(solution)/shard_map/psum | solution.py:34
  1264.9 7.9 copy.104
  1272.9 8.7 copy.105
  1282.7 15.5 scatter_custom_fusion
  1301.6 21.1 gather_fusion.5
  1325.8 21.1 gather_fusion.3
  1346.9 4.6 broadcast_select_fusion
  1353.1 7.3 fusion.163
  1360.4 8.2 copy.106
  1368.6 8.7 copy.107
  1377.3 7.1 fusion.165
  1384.5 112.0 %reduce-scatter.9.cloned.1.call-done = f32[8,160,384]{2,1,0:T(8,128)} async-done(((f32[32,160,384]{2,1,0:T(8,128)}), f32[8,160,384]{2,1,0:T(8,128)}) %reduce-scatter.9.cloned.1.call-update) | async-done | bytes 1966096 | tf_op jit(solution)/shard_map/reduce_scatter | solution.py:46
  1496.5 139.8 %reduce-scatter.13.cloned.1.call-done = f32[8,160,384]{2,1,0:T(8,128)} async-done(((f32[32,160,384]{2,1,0:T(8,128)}), f32[8,160,384]{2,1,0:T(8,128)}) %reduce-scatter.13.cloned.1.call-update) | async-done | bytes 1966096 | tf_op jit(solution)/shard_map/reduce_scatter | solution.py:46
  1636.3 4.8 fusion.15
  1642.2 23.0 gather_fusion.2
  1665.3 53.0 %all-gather.19.cloned.1.call-done = bf16[32,160,384]{2,1,0:T(8,128)(2,1)} async-done(((bf16[8,160,384]{2,1,0:T(8,128)(2,1)}), bf16[32,160,384]{2,1,0:T(8,128)(2,1)}) %all-gather.19.cloned.1.call-update) | async-done | bytes 3932176 | tf_op jit(solution)/shard_map/all_gather | solution.py:42
  1718.3 8.1 fusion.166
  1726.4 19.0 gather_fusion.6
  1745.4 5.3 copy.113
  1750.7 44.3 %all-gather.15.cloned.1.call-done = bf16[32,160,384]{2,1,0:T(8,128)(2,1)} async-done(((bf16[8,160,384]{2,1,0:T(8,128)(2,1)}), bf16[32,160,384]{2,1,0:T(8,128)(2,1)}) %all-gather.15.cloned.1.call-update) | async-done | bytes 3932176 | tf_op jit(solution)/shard_map/all_gather | solution.py:42
  1795.0 8.1 fusion.164
  1803.1 18.6 gather_fusion.4
  1821.7 5.3 copy.108
  1827.0 6.3 broadcast_select_fusion.2
  1834.1 44.2 %reduce-scatter.11.cloned.1.call-done = f32[512,192]{0,1:T(8,128)} async-done(((f32[4096,192]{0,1:T(8,128)}), f32[512,192]{0,1:T(8,128)}) %reduce-scatter.11.cloned.1.call-update) | async-done | bytes 393232 | tf_op jit(solution)/shard_map/reduce_scatter | solution.py:55
  1880.2 11.6 psum.58
  1891.9 36.7 %reduce-scatter.15.cloned.1.call-done = f32[512,192]{0,1:T(8,128)} async-done(((f32[4096,192]{0,1:T(8,128)}), f32[512,192]{0,1:T(8,128)}) %reduce-scatter.15.cloned.1.call-update) | async-done | bytes 393232 | tf_op jit(solution)/shard_map/reduce_scatter | solution.py:55
  1930.8 11.7 psum.59
  1943.4 4.1 all-to-all-start.2
  1950.3 7.2 all-to-all-done.2
  1963.3 11.9 multiply_reduce_fusion
  1977.4 8.2 multiply_convert_fusion
  2005.5 3.7 fusion.51
  2012.9 15.6 collective-permute-done.26
  2029.9 20.7 collective-permute-done.25
  2051.8 15.7 collective-permute-done.24
  2074.0 15.2 collective-permute-done.19
  2090.7 4.9 fusion.31
  2095.7 45.7 %collective-permute-done.17 = f32[128,2,768]{0,2,1:T(8,128)S(1)} collective-permute-done((f32[128,2,768]{0,2,1:T(8,128)S(1)}, f32[128,2,768]{0,2,1:T(8,128)S(1)}, u32[]{:S(2)}, u32[]{:S(2)}) %collective-permute-start.17) | collective-permute-done | bytes 786464 | tf_op jit(solution)/shard_map/ppermute | solution.py:23
  2168.9 8.8 convolution_bitcast_fusion.1
  2182.1 7.7 convolution_bitcast_fusion
  2189.8 12.9 copy.123
  2202.6 11.6 copy.126
  2214.2 12.8 copy.124
  2227.0 11.6 copy.127
  2245.4 4.5 convert_reduce_fusion.1
  2252.3 40.0 %all-reduce = (f32[768]{0:T(1024)}, f32[32,12]{0,1:T(8,128)}, f32[4,192]{1,0:T(4,128)S(1)}) all-reduce(f32[768]{0:T(1024)S(1)} %get-tuple-element.42, f32[32,12]{0,1:T(8,128)S(1)} %fusion.36, f32[4,192]{1,0:T(4,128)S(1)} %broadcast_multiply_fusion.1), channel_id=1, replica_groups=mesh['gx'=4,'gy'=8] {'gx','gy'}, use_global_device_ids=true, to_apply=%region_23.26 | all-reduce | flops 1920 | bytes 15360 | tf_op jit(solution)/shard_map/psum | solution.py:403
  2293.8 80.8 %reduce-scatter.17.cloned.1.call-done = f32[1,192,96]{2,1,0:T(8,128)} async-done(((f32[32,192,96]{2,1,0:T(8,128)}), f32[1,192,96]{2,1,0:T(8,128)}) %reduce-scatter.17.cloned.1.call-update) | async-done | bytes 73744 | tf_op jit(solution)/shard_map/reduce_scatter | solution.py:417
  2374.6 107.2 %reduce-scatter.19.cloned.1.call-done = f32[1,192,96]{2,1,0:T(8,128)} async-done(((f32[32,192,96]{2,1,0:T(8,128)}), f32[1,192,96]{2,1,0:T(8,128)}) %reduce-scatter.19.cloned.1.call-update) | async-done | bytes 73744 | tf_op jit(solution)/shard_map/reduce_scatter | solution.py:423
  2481.8 107.3 %reduce-scatter.21.cloned.1.call-done = f32[1,192,96]{2,1,0:T(8,128)} async-done(((f32[32,192,96]{2,1,0:T(8,128)}), f32[1,192,96]{2,1,0:T(8,128)}) %reduce-scatter.21.cloned.1.call-update) | async-done | bytes 73744 | tf_op jit(solution)/shard_map/reduce_scatter | solution.py:429
  (316 shorter events, 187.2 us)
Async XLA Ops:
  7.2 1215.5 %copy-start = (f32[192,32]{0,1:T(8,128)S(1)}, f32[192,32]{0,1:T(8,128)}, u32[]{:S(2)}) copy-start(f32[192,32]{0,1:T(8,128)} %param.26) | copy-start | bytes 73732
  7.2 61.4 %all-gather.21.cloned.1.call-start = ((), (), s32[]{:S(2)}) async-start(), calls=%async_computation.25 | async-start | bytes 1622016 | tf_op jit(solution)/shard_map/all_gather | solution.py:165
  7.9 117.3 %all-gather.23.cloned.1.call-start = ((), (), s32[]{:S(2)}) async-start(), calls=%async_computation.26 | async-start | bytes 1622016 | tf_op jit(solution)/shard_map/all_gather | solution.py:166
  8.7 173.3 %all-gather.25.cloned.1.call-start = ((), (), s32[]{:S(2)}) async-start(), calls=%async_computation.27 | async-start | bytes 1622016 | tf_op jit(solution)/shard_map/all_gather | solution.py:167
  9.4 1074.7 %all-gather.27.cloned.1.call-start = ((), (), s32[]{:S(2)}) async-start(), calls=%async_computation.28 | async-start | bytes 1622016 | tf_op jit(solution)/shard_map/all_gather | solution.py:168
  10.0 190.2 %copy-start.44 = (s32[128]{0:T(128)}, s32[128]{0:T(128)S(1)}, u32[]{:S(2)}) copy-start(s32[128]{0:T(128)S(1)} %iota_add_fusion.1) | copy-start | bytes 1540
  10.8 189.4 %copy-start.36 = (s32[1920]{0:T(1024)}, s32[1920]{0:T(1024)S(1)}, u32[]{:S(2)}) copy-start(s32[1920]{0:T(1024)S(1)} %get-tuple-element.95) | copy-start | bytes 23044
  14.6 173.7 %copy-start.42 = (f32[128]{0:T(128)}, f32[128]{0:T(128)S(1)}, u32[]{:S(2)}) copy-start(f32[128]{0:T(128)S(1)} %get-tuple-element.87) | copy-start | bytes 1540
  190.9 897.5 %collective-permute-start = (bf16[128,2,768]{2,1,0:T(2,128)(2,1)S(1)}, bf16[128,2,768]{2,1,0:T(2,128)(2,1)}, u32[]{:S(2)}, u32[]{:S(2)}) collective-permute-start(bf16[128,2,768]{2,1,0:T(2,128)(2,1)S(1)} %reshape.589), channel_id=1, source_target_pairs={{0,7},{8,15},{16,23},{24,31}} | collective-permute-start | bytes 1179656 | tf_op jit(solution)/shard_map/ppermute | solution.py:23
  194.8 896.6 %collective-permute-start.1 = (bf16[128,2,768]{2,1,0:T(2,128)(2,1)S(1)}, bf16[128,2,768]{2,1,0:T(2,128)(2,1)}, u32[]{:S(2)}, u32[]{:S(2)}) collective-permute-start(bf16[128,2,768]{2,1,0:T(2,128)(2,1)S(1)} %reshape.589), channel_id=1, source_target_pairs={{0,6},{1,7},{8,14},{9,15},{16,22},{17,23},{24,30},{25,31}} | collective-permute-start | bytes 1179656 | tf_op jit(solution)/shard_map/ppermute | solution.py:23
  196.9 897.2 %collective-permute-start.2 = (bf16[128,2,768]{2,1,0:T(2,128)(2,1)S(1)}, bf16[128,2,768]{2,1,0:T(2,128)(2,1)}, u32[]{:S(2)}, u32[]{:S(2)}) collective-permute-start(bf16[128,2,768]{2,1,0:T(2,128)(2,1)S(1)} %reshape.589), channel_id=1, source_target_pairs={{0,5},{1,6},{2,7},{8,13},{9,14},{10,15},{16,21},{17,22},{18,23},{2... | collective-permute-start | bytes 1179656 | tf_op jit(solution)/shard_map/ppermute | solution.py:23
  198.9 897.8 %collective-permute-start.3 = (bf16[128,2,768]{2,1,0:T(2,128)(2,1)S(1)}, bf16[128,2,768]{2,1,0:T(2,128)(2,1)S(1)}, u32[]{:S(2)}, u32[]{:S(2)}) collective-permute-start(bf16[128,2,768]{2,1,0:T(2,128)(2,1)S(1)} %reshape.589), channel_id=1, source_target_pairs={{0,4},{1,5},{2,6},{3,7},{8,12},{9,13},{10,14},{11,15},{16,20},{17,... | collective-permute-start | bytes 1179656 | tf_op jit(solution)/shard_map/ppermute | solution.py:23
  1081.8 16.5 collective-permute-start.4
  1084.1 93.2 %copy-start.20 = (bf16[128,768]{0,1:T(8,128)(2,1)}, bf16[128,768]{0,1:T(8,128)(2,1)S(1)}, u32[]{:S(2)}) copy-start(bf16[128,768]{0,1:T(8,128)(2,1)S(1)} %copy.93) | copy-start | bytes 589828
  1088.3 12.6 collective-permute-start.5
  1091.4 11.2 collective-permute-start.6
  1094.0 10.5 collective-permute-start.7
  1096.7 20.1 collective-permute-start.8
  1098.3 20.7 collective-permute-start.9
  1100.9 41.5 %collective-permute-start.10 = (bf16[128,2,768]{2,1,0:T(2,128)(2,1)S(1)}, bf16[128,2,768]{2,1,0:T(2,128)(2,1)S(1)}, u32[]{:S(2)}, u32[]{:S(2)}) collective-permute-start(bf16[128,2,768]{2,1,0:T(2,128)(2,1)S(1)} %reshape.589), channel_id=1, source_target_pairs={{4,0},{5,1},{6,2},{7,3},{12,8},{13,9},{14,10},{15,11},{20,16},{21,... | collective-permute-start | bytes 1179656 | tf_op jit(solution)/shard_map/ppermute | solution.py:23
  1102.6 41.1 %collective-permute-start.11 = (bf16[128,2,768]{2,1,0:T(2,128)(2,1)S(1)}, bf16[128,2,768]{2,1,0:T(2,128)(2,1)S(1)}, u32[]{:S(2)}, u32[]{:S(2)}) collective-permute-start(bf16[128,2,768]{2,1,0:T(2,128)(2,1)S(1)} %reshape.589), channel_id=1, source_target_pairs={{5,0},{6,1},{7,2},{13,8},{14,9},{15,10},{21,16},{22,17},{23,18},{2... | collective-permute-start | bytes 1179656 | tf_op jit(solution)/shard_map/ppermute | solution.py:23
  1104.5 39.4 %collective-permute-start.12 = (bf16[128,2,768]{2,1,0:T(2,128)(2,1)S(1)}, bf16[128,2,768]{2,1,0:T(2,128)(2,1)S(1)}, u32[]{:S(2)}, u32[]{:S(2)}) collective-permute-start(bf16[128,2,768]{2,1,0:T(2,128)(2,1)S(1)} %reshape.589), channel_id=1, source_target_pairs={{6,0},{7,1},{14,8},{15,9},{22,16},{23,17},{30,24},{31,25}} | collective-permute-start | bytes 1179656 | tf_op jit(solution)/shard_map/ppermute | solution.py:23
  1116.7 27.6 %collective-permute-start.13 = (bf16[128,2,768]{2,1,0:T(2,128)(2,1)S(1)}, bf16[128,2,768]{2,1,0:T(2,128)(2,1)S(1)}, u32[]{:S(2)}, u32[]{:S(2)}) collective-permute-start(bf16[128,2,768]{2,1,0:T(2,128)(2,1)S(1)} %reshape.589), channel_id=1, source_target_pairs={{7,0},{15,8},{23,16},{31,24}} | collective-permute-start | bytes 1179656 | tf_op jit(solution)/shard_map/ppermute | solution.py:23
  1195.2 17.3 all-to-all-start
  1198.7 61.3 %all-reduce.4.cloned.1.call-start = ((), (), s32[]{:S(2)}) async-start(), calls=%async_computation.11 | async-start | bytes 131072 | tf_op jit(solution)/shard_map/psum | solution.py:34
  1212.7 729.8 %copy-start.11 = (bf16[3,4,24,8,128]{4,3,1,2,0:T(8,128)(2,1)}, bf16[3,4,24,8,128]{4,3,1,2,0:T(8,128)(2,1)S(1)}, u32[]{:S(2)}) copy-start(bf16[3,4,24,8,128]{4,3,1,2,0:T(8,128)(2,1)S(1)} %copy.147) | copy-start | bytes 1769476
  1223.8 74.5 %all-gather.17.cloned.1.call-start = ((), (), s32[]{:S(2)}) async-start(), calls=%async_computation.16 | async-start | bytes 1769472 | tf_op jit(solution)/shard_map/all_gather | solution.py:38
  1224.0 704.6 %copy-start.40 = (s32[512]{0:T(512)}, s32[512]{0:T(512)S(1)}, u32[]{:S(2)}) copy-start(s32[512]{0:T(512)S(1)} %and_select_fusion.4) | copy-start | bytes 6148
  1261.8 666.8 %copy-start.39 = (f32[512]{0:T(512)}, f32[512]{0:T(512)S(1)}, u32[]{:S(2)}) copy-start(f32[512]{0:T(512)S(1)} %fusion.103) | copy-start | bytes 6148
  1263.5 59.1 %all-gather.13.cloned.1.call-start = ((), (), s32[]{:S(2)}) async-start(), calls=%async_computation.12 | async-start | bytes 1769472 | tf_op jit(solution)/shard_map/all_gather | solution.py:38
  1264.3 232.2 %reduce-scatter.9.cloned.1.call-start = ((), (), s32[]{:S(2)}) async-start(), calls=%async_computation.13 | async-start | bytes 9830400 | tf_op jit(solution)/shard_map/reduce_scatter | solution.py:46
  1360.4 275.9 %reduce-scatter.13.cloned.1.call-start = ((), (), s32[]{:S(2)}) async-start(), calls=%async_computation.17 | async-start | bytes 9830400 | tf_op jit(solution)/shard_map/reduce_scatter | solution.py:46
  1384.4 333.9 %all-gather.19.cloned.1.call-start = ((), (), s32[]{:S(2)}) async-start(), calls=%async_computation.18 | async-start | bytes 4915200 | tf_op jit(solution)/shard_map/all_gather | solution.py:42
  1641.2 153.8 %all-gather.15.cloned.1.call-start = ((), (), s32[]{:S(2)}) async-start(), calls=%async_computation.14 | async-start | bytes 4915200 | tf_op jit(solution)/shard_map/all_gather | solution.py:42
  1641.9 236.4 %reduce-scatter.11.cloned.1.call-start = ((), (), s32[]{:S(2)}) async-start(), calls=%async_computation.15 | async-start | bytes 3538944 | tf_op jit(solution)/shard_map/reduce_scatter | solution.py:55
  1833.3 95.2 %copy-start.32 = (f32[512,32]{0,1:T(8,128)S(1)}, f32[512,32]{0,1:T(8,128)}, u32[]{:S(2)}) copy-start(f32[512,32]{0,1:T(8,128)} %all-reduce.4.cloned.1.call-done) | copy-start | bytes 196612
  1833.3 95.2 %reduce-scatter.15.cloned.1.call-start = ((), (), s32[]{:S(2)}) async-start(), calls=%async_computation.19 | async-start | bytes 3538944 | tf_op jit(solution)/shard_map/reduce_scatter | solution.py:55
  1891.8 56.7 %copy-start.41 = (f32[512]{0:T(512)}, f32[512]{0:T(512)S(1)}, u32[]{:S(2)}) copy-start(f32[512]{0:T(512)S(1)} %psum.58) | copy-start | bytes 6148
  1891.8 56.2 %copy-start.48 = (f32[512]{0:T(512)}, f32[512]{0:T(512)S(1)}, u32[]{:S(2)}) copy-start(f32[512]{0:T(512)S(1)} %mul.388) | copy-start | bytes 6148
  1943.4 14.1 all-to-all-start.2
  1947.5 291.2 %all-reduce.6.cloned.1.call-start = ((), (), s32[]{:S(2)}) async-start(), calls=%async_computation.24 | async-start | bytes 262144 | tf_op jit(solution)/shard_map/psum | solution.py:403
  1991.9 19.7 collective-permute-start.27
  1994.1 34.4 %collective-permute-start.26 = (f32[128,2,768]{0,2,1:T(8,128)}, f32[128,2,768]{0,2,1:T(8,128)}, u32[]{:S(2)}, u32[]{:S(2)}) collective-permute-start(f32[128,2,768]{0,2,1:T(8,128)} %get-tuple-element.64), channel_id=1, source_target_pairs={{0,6},{1,7},{8,14},{9,15},{16,22},{17,23},{24,30},{25,31}} | collective-permute-start | bytes 2359304 | tf_op jit(solution)/shard_map/ppermute | solution.py:23
  1997.7 52.8 %collective-permute-start.25 = (f32[128,2,768]{0,2,1:T(8,128)}, f32[128,2,768]{0,2,1:T(8,128)}, u32[]{:S(2)}, u32[]{:S(2)}) collective-permute-start(f32[128,2,768]{0,2,1:T(8,128)} %get-tuple-element.62), channel_id=1, source_target_pairs={{0,5},{1,6},{2,7},{8,13},{9,14},{10,15},{16,21},{17,22},{18,23},{2... | collective-permute-start | bytes 2359304 | tf_op jit(solution)/shard_map/ppermute | solution.py:23
  1999.9 67.6 %collective-permute-start.24 = (f32[128,2,768]{0,2,1:T(8,128)}, f32[128,2,768]{0,2,1:T(8,128)}, u32[]{:S(2)}, u32[]{:S(2)}) collective-permute-start(f32[128,2,768]{0,2,1:T(8,128)} %get-tuple-element.61), channel_id=1, source_target_pairs={{0,4},{1,5},{2,6},{3,7},{8,12},{9,13},{10,14},{11,15},{16,20},{17,... | collective-permute-start | bytes 2359304 | tf_op jit(solution)/shard_map/ppermute | solution.py:23
  2002.8 291.0 %reduce-scatter.23.cloned.1.call-start = ((), (), s32[]{:S(2)}) async-start(), calls=%async_computation.23 | async-start | bytes 3244032 | tf_op jit(solution)/shard_map/reduce_scatter | solution.py:435
  2005.5 85.3 %copy-start.7 = (bf16[1920,1,768]{0,2,1:T(8,128)(2,1)S(1)}, bf16[1920,1,768]{0,2,1:T(8,128)(2,1)}, u32[]{:S(2)}) copy-start(bf16[1920,1,768]{0,2,1:T(8,128)(2,1)} %copy-done.6) | copy-start | bytes 8847364
  2005.5 369.1 %reduce-scatter.17.cloned.1.call-start = ((), (), s32[]{:S(2)}) async-start(), calls=%async_computation.20 | async-start | bytes 3244032 | tf_op jit(solution)/shard_map/reduce_scatter | solution.py:417
  2009.2 59.5 %collective-permute-start.23 = (f32[128,2,768]{0,2,1:T(8,128)S(1)}, f32[128,2,768]{0,2,1:T(8,128)S(1)}, u32[]{:S(2)}, u32[]{:S(2)}) collective-permute-start(f32[128,2,768]{0,2,1:T(8,128)S(1)} %copy-done.29), channel_id=1, source_target_pairs={{0,3},{1,4},{2,5},{3,6},{4,7},{8,11},{9,12},{10,13},{11,14},{12,15... | collective-permute-start | bytes 2359304 | tf_op jit(solution)/shard_map/ppermute | solution.py:23
  2011.6 58.5 %collective-permute-start.22 = (f32[128,2,768]{0,2,1:T(8,128)S(1)}, f32[128,2,768]{0,2,1:T(8,128)S(1)}, u32[]{:S(2)}, u32[]{:S(2)}) collective-permute-start(f32[128,2,768]{0,2,1:T(8,128)S(1)} %get-tuple-element.59), channel_id=1, source_target_pairs={{0,2},{1,3},{2,4},{3,5},{4,6},{5,7},{8,10},{9,11},{10,12},{11,13},... | collective-permute-start | bytes 2359304 | tf_op jit(solution)/shard_map/ppermute | solution.py:23
  2028.6 42.8 %collective-permute-start.21 = (f32[128,2,768]{0,2,1:T(8,128)S(1)}, f32[128,2,768]{0,2,1:T(8,128)S(1)}, u32[]{:S(2)}, u32[]{:S(2)}) collective-permute-start(f32[128,2,768]{0,2,1:T(8,128)S(1)} %get-tuple-element.58), channel_id=1, source_target_pairs={{0,1},{1,2},{2,3},{3,4},{4,5},{5,6},{6,7},{8,9},{9,10},{10,11},{11... | collective-permute-start | bytes 2359304 | tf_op jit(solution)/shard_map/ppermute | solution.py:23
  2050.5 22.2 collective-permute-start.20
  2067.5 21.8 collective-permute-start.19
  2068.8 26.9 %collective-permute-start.18 = (f32[128,2,768]{0,2,1:T(8,128)S(1)}, f32[128,2,768]{0,2,1:T(8,128)S(1)}, u32[]{:S(2)}, u32[]{:S(2)}) collective-permute-start(f32[128,2,768]{0,2,1:T(8,128)S(1)} %get-tuple-element.55), channel_id=1, source_target_pairs={{3,0},{4,1},{5,2},{6,3},{7,4},{11,8},{12,9},{13,10},{14,11},{15,12... | collective-permute-start | bytes 2359304 | tf_op jit(solution)/shard_map/ppermute | solution.py:23
  2070.1 71.3 %collective-permute-start.17 = (f32[128,2,768]{0,2,1:T(8,128)S(1)}, f32[128,2,768]{0,2,1:T(8,128)S(1)}, u32[]{:S(2)}, u32[]{:S(2)}) collective-permute-start(f32[128,2,768]{0,2,1:T(8,128)S(1)} %get-tuple-element.54), channel_id=1, source_target_pairs={{4,0},{5,1},{6,2},{7,3},{12,8},{13,9},{14,10},{15,11},{20,16},{21,... | collective-permute-start | bytes 2359304 | tf_op jit(solution)/shard_map/ppermute | solution.py:23
  2071.4 71.8 %collective-permute-start.16 = (f32[128,2,768]{0,2,1:T(8,128)S(1)}, f32[128,2,768]{0,2,1:T(8,128)S(1)}, u32[]{:S(2)}, u32[]{:S(2)}) collective-permute-start(f32[128,2,768]{0,2,1:T(8,128)S(1)} %get-tuple-element.53), channel_id=1, source_target_pairs={{5,0},{6,1},{7,2},{13,8},{14,9},{15,10},{21,16},{22,17},{23,18},{2... | collective-permute-start | bytes 2359304 | tf_op jit(solution)/shard_map/ppermute | solution.py:23
  2072.7 70.5 %collective-permute-start.15 = (f32[128,2,768]{0,2,1:T(8,128)S(1)}, f32[128,2,768]{0,2,1:T(8,128)S(1)}, u32[]{:S(2)}, u32[]{:S(2)}) collective-permute-start(f32[128,2,768]{0,2,1:T(8,128)S(1)} %get-tuple-element.52), channel_id=1, source_target_pairs={{6,0},{7,1},{14,8},{15,9},{22,16},{23,17},{30,24},{31,25}} | collective-permute-start | bytes 2359304 | tf_op jit(solution)/shard_map/ppermute | solution.py:23
  2089.3 54.0 %collective-permute-start.14 = (f32[128,2,768]{0,2,1:T(8,128)S(1)}, f32[128,2,768]{0,2,1:T(8,128)S(1)}, u32[]{:S(2)}, u32[]{:S(2)}) collective-permute-start(f32[128,2,768]{0,2,1:T(8,128)S(1)} %get-tuple-element.51), channel_id=1, source_target_pairs={{7,0},{15,8},{23,16},{31,24}} | collective-permute-start | bytes 2359304 | tf_op jit(solution)/shard_map/ppermute | solution.py:23
  2095.6 51.3 %copy-start.15 = (bf16[128,768]{1,0:T(8,128)(2,1)S(1)}, bf16[128,768]{1,0:T(8,128)(2,1)}, u32[]{:S(2)}) copy-start(bf16[128,768]{1,0:T(8,128)(2,1)} %param.18) | copy-start | bytes 589828
  2095.6 51.3 %copy-start.35 = (f32[768]{0:T(1024)S(1)}, f32[768]{0:T(1024)}, u32[]{:S(2)}) copy-start(f32[768]{0:T(1024)} %param.19) | copy-start | bytes 9220
  2095.6 51.3 %copy-start.43 = (f32[128]{0:T(128)S(1)}, f32[128]{0:T(128)}, u32[]{:S(2)}) copy-start(f32[128]{0:T(128)} %copy-done.42) | copy-start | bytes 1540
  2156.7 325.1 %reduce-scatter.19.cloned.1.call-start = ((), (), s32[]{:S(2)}) async-start(), calls=%async_computation.21 | async-start | bytes 3244032 | tf_op jit(solution)/shard_map/reduce_scatter | solution.py:423
  2162.1 427.0 %reduce-scatter.21.cloned.1.call-start = ((), (), s32[]{:S(2)}) async-start(), calls=%async_computation.22 | async-start | bytes 3244032 | tf_op jit(solution)/shard_map/reduce_scatter | solution.py:429
  2178.4 63.7 %all-to-all-start.1 = ((f32[4,128,192]{1,2,0:T(8,128)}), f32[4,128,192]{1,2,0:T(8,128)S(1)}, u32[]{:S(2)}, u32[]{:S(2)}) async-start(f32[4,128,192]{1,2,0:T(8,128)} %bitcast.272), calls=%async_computation.3 | async-start | bytes 786432 | tf_op jit(solution)/shard_map/all_to_all | solution.py:327
  (39 other events, 415.0 us)
Sparse Core Ops, SparseCore 0:
  10.9 57.6 all-gather.20
  71.4 53.8 all-gather.22
  128.2 53.8 all-gather.24
  184.7 55.9 all-gather.26
  1223.9 36.0 all-reduce.3
  1263.7 25.5 all-gather.16
  1291.9 25.8 all-gather.12
  1360.5 135.9 reduce-scatter.8
  1499.5 136.7 reduce-scatter.12
  1641.3 76.9 all-gather.18
  1719.9 75.0 all-gather.14
  1833.5 44.8 reduce-scatter.10
  1882.3 46.2 reduce-scatter.14
  2002.9 156.3 all-reduce.5
  2166.1 101.2 reduce-scatter.22
  2274.1 100.4 reduce-scatter.16
  2381.3 100.4 reduce-scatter.18
  2488.6 100.5 reduce-scatter.20
where the time goes:
time: 2610 us; the launch traced here: 2600 us
  local copies, waits for them, and re-layouts  1200 us (46%)
  waiting for transfers between devices  1090 us (42%)
  matrix products  90.9 us (3%)
  blocking collectives  73.2 us (3%)
  starting transfers between devices  59.6 us (2%)
  other arithmetic  57.6 us (2%)
    gather x2, local copies, waits for them, and re-layouts, local(): bias_terms = jnp.take(jnp.transpose(relative_bias_table), buckets, axis=1)  879 us
    reduce_scatter x2, waiting for transfers between devices, width_sums(): lax.psum_scatter(term_fn(jnp.int32(0), lax.axis_size('gx') * row_number),...  252 us
    ppermute x28, waiting for transfers between devices, passed_along(): lax.ppermute(value, axis, [(source, source + steps) for source in range(f...  151 us
    reduce_scatter x1, waiting for transfers between devices, local(): lax.psum_scatter(grid_rows_cols(qkv_grads[:, 2 * head_width:], width_devs...  107 us
    reduce_scatter x1, waiting for transfers between devices, local(): lax.psum_scatter(grid_rows_cols(qkv_grads[:, head_width:2 * head_width],...  107 us
    all_gather x2, waiting for transfers between devices, width_rows(): return lax.all_gather(block_part, 'gx', axis=0, tiled=True)  97.3 us
    gather x6, local copies, waits for them, and re-layouts, take_rows(): return jnp.take(table, index, axis=0, mode='fill', fill_value=0)  90.4 us
    reduce_scatter x2, waiting for transfers between devices, token_sums(): lax.psum_scatter(term_fn(jnp.int32(0), lax.axis_size('gy') * row_number),...  81 us
  transfers between devices with their start and end apart: 49, of which 26 were waited for; matrix products, arithmetic and copies ran while one was open for 45% of the time, Pallas kernels for 0%

commit v1 on v0

--- a/solution.py
+++ b/solution.py
@@ -1,8 +1,11 @@
+import functools
 import math
 
 import jax
 import jax.numpy as jnp
 from jax import lax
+from jax.experimental import pallas as pl
+from jax.experimental.pallas import tpu as pltpu
 from jax.sharding import PartitionSpec as P
 
 D = 768
@@ -455,9 +458,534 @@
     )
 
 
+MESH = pl.DeviceIdType.MESH
+GELU_C = math.sqrt(2.0 / math.pi)
+f32, bf16 = jnp.float32, jnp.bfloat16
+
+
+def nt(a, b):
+    return lax.dot_general(a, b, (((1,), (1,)), ((), ())), preferred_element_type=f32)
+
+
+def tn(a, b):
+    return lax.dot_general(a, b, (((0,), (0,)), ((), ())), preferred_element_type=f32)
+
+
+def remote(src, dst, send_sem, recv_sem, device):
+    return pltpu.make_async_remote_copy(
+        src_ref=src, dst_ref=dst, send_sem=send_sem, recv_sem=recv_sem,
+        device_id=device, device_id_type=MESH)
+
+
+def greet(devices):
+    barrier = pltpu.get_barrier_semaphore()
+    for device in devices:
+        pl.semaphore_signal(barrier, inc=1, device_id=device, device_id_type=MESH)
+    pl.semaphore_wait(barrier, len(devices))
+
+
+RING = 8
+GROUP = 8
+LAG_B, LAG_C, LAG_D = 2, 4, 6
+
+
+def moe_kernel(experts, capacity, width, units, tokens,
+               r_ref, slot_row, slot_col, w1_ref, w2_ref,
+               out_ref, gh_ref, gb_ref,
+               x_sl, g_sl, p_ref, re_ref, rm_ref, c_ref, y_ref, gh_st, gb_st,
+               pair_out, pair_in, chip_out, chip_in, line_out, line_in,
+               p_sem, re_sem, rm_sem, t_sem, gh_sem, gb_sem,
+               po_sem, pi_sem, co_sem, ci_sem, lo_sem, li_sem):
+    gx, gy = lax.axis_index("gx"), lax.axis_index("gy")
+    core, chip = lax.rem(gy, 2), gy // 2
+    peer = gy + 1 - 2 * core
+    is_mid = jnp.logical_and(gx > 0, gx < 3)
+    is_end = jnp.logical_not(is_mid)
+    mid_of = jnp.where(gx < 2, 1, 2)
+    other_mid = 3 - mid_of
+    end_of = jnp.where(gx < 2, 0, 3)
+    line = [lax.rem(gx + k, 4) for k in (1, 2, 3)]
+    chips = [lax.rem(chip + k, 4) for k in (1, 2, 3)]
+    greet([(z, gy) for z in line] + [(gx, 2 * c + core) for c in chips] + [(gx, peer)])
+
+    def send_p(e):
+        return remote(p_ref.at[lax.rem(e, RING)], re_ref.at[e], p_sem.at[lax.rem(e, RING)], re_sem.at[e], (mid_of, gy))
+
+    def send_s(e):
+        return remote(p_ref.at[lax.rem(e, RING)], rm_ref.at[e], p_sem.at[lax.rem(e, RING)], rm_sem.at[e], (other_mid, gy))
+
+    def send_t(e):
+        return remote(re_ref.at[e], re_ref.at[e], t_sem.at[e], re_sem.at[e], (end_of, gy))
+
+    def grad_copy(stage, target, sems, e):
+        return pltpu.make_async_copy(stage.at[lax.rem(e, 2)], target.at[e], sems.at[lax.rem(e, 2)])
+
+    kblock = 1024
+
+    def step(i, carry):
+        @pl.when(i < experts)
+        def _():
+            e = i
+            sl = lax.rem(e, RING)
+
+            @pl.when(e >= RING)
+            def _():
+                send_p(e - RING).wait_send()
+            ids = lax.broadcasted_iota(jnp.int32, (capacity, kblock), 0) + e * capacity
+            acc = jnp.zeros((capacity, 2 * width), f32)
+            for kb in range(tokens // kblock):
+                hot = (slot_row[:, kb * kblock:(kb + 1) * kblock] == ids).astype(f32).astype(bf16)
+                acc = acc + jnp.dot(hot, r_ref[kb * kblock:(kb + 1) * kblock, :], preferred_element_type=f32)
+            xs = acc[:, :width].astype(bf16)
+            gs = acc[:, width:].astype(bf16)
+            x_sl[sl] = xs
+            g_sl[sl] = gs
+            p_ref[sl, 0:capacity, :] = jnp.dot(xs, w1_ref[e], preferred_element_type=f32).astype(bf16)
+            p_ref[sl, capacity:2 * capacity, :] = jnp.dot(gs, w2_ref[e], preferred_element_type=f32).astype(bf16)
+
+            @pl.when(is_end)
+            def _():
+                send_p(e).start()
+
+        eb = i - LAG_B
+
+        @pl.when(jnp.logical_and(is_mid, jnp.logical_and(eb >= 0, eb < experts)))
+        def _():
+            sl = lax.rem(eb, RING)
+            send_p(eb).wait_recv()
+            p_ref[sl] = (p_ref[sl].astype(f32) + re_ref[eb].astype(f32)).astype(bf16)
+            send_s(eb).start()
+
+        ec = i - LAG_C
+
+        @pl.when(jnp.logical_and(is_mid, jnp.logical_and(ec >= 0, ec < experts)))
+        def _():
+            sl = lax.rem(ec, RING)
+            send_s(ec).wait_recv()
+            re_ref[ec] = (p_ref[sl].astype(f32) + rm_ref[ec].astype(f32)).astype(bf16)
+            send_t(ec).start()
+
+        ed = i - LAG_D
+
+        @pl.when(ed >= 0)
+        def _():
+            e = ed
+            sl = lax.rem(e, RING)
+
+            @pl.when(is_end)
+            def _():
+                send_t(e).wait_recv()
+            u = re_ref[e, 0:capacity, :].astype(f32)
+            ag = re_ref[e, capacity:2 * capacity, :].astype(f32)
+            u2 = u * u
+            th = jnp.tanh(GELU_C * (u + 0.044715 * (u2 * u)))
+            half = 0.5 * (1.0 + th)
+            act = (u * half).astype(bf16)
+            dg = half + 0.5 * u * (1.0 - th * th) * (GELU_C * (1.0 + 3 * 0.044715 * u2))
+            pg = (ag * dg).astype(bf16)
+            y1 = nt(act, w2_ref[e])
+            y2 = nt(pg, w1_ref[e])
+            row = pl.multiple_of(lax.rem(e, GROUP) * capacity, 32)
+            y_ref[pl.ds(row, capacity), :] = jnp.concatenate([y1, y2], axis=1).astype(bf16)
+
+            @pl.when(e >= 2)
+            def _():
+                grad_copy(gh_st, gh_ref, gh_sem, e - 2).wait()
+                grad_copy(gb_st, gb_ref, gb_sem, e - 2).wait()
+            gh_st[lax.rem(e, 2)] = tn(x_sl[sl], pg)
+            gb_st[lax.rem(e, 2)] = tn(g_sl[sl], act)
+            grad_copy(gh_st, gh_ref, gh_sem, e).start()
+            grad_copy(gb_st, gb_ref, gb_sem, e).start()
+
+            @pl.when(lax.rem(e, GROUP) == GROUP - 1)
+            def _():
+                rows = 512
+                base = (e - (GROUP - 1)) * capacity
+
+                def block(b, c):
+                    at = pl.ds(pl.multiple_of(b * rows, rows), rows)
+                    cols = lax.broadcasted_iota(jnp.int32, (rows, GROUP * capacity), 1) + base
+                    hot = (slot_col[at, :] == cols).astype(f32).astype(bf16)
+                    add = jnp.dot(hot, y_ref[...], preferred_element_type=f32)
+
+                    @pl.when(e == GROUP - 1)
+                    def _():
+                        c_ref[at, :] = add
+
+                    @pl.when(e > GROUP - 1)
+                    def _():
+                        c_ref[at, :] = c_ref[at, :] + add
+                    return c
+                lax.fori_loop(0, tokens // rows, block, 0)
+        return carry
+
+    lax.fori_loop(0, experts + LAG_D, step, 0)
+
+    def drain(e, carry):
+        send_p(e).wait_send()
+        return carry
+    lax.fori_loop(experts - RING, experts, drain, 0)
+
+    @pl.when(is_mid)
+    def _():
+        lax.fori_loop(0, experts, lambda e, c: (send_t(e).wait_send(), c)[1], 0)
+    for e in (experts - 2, experts - 1):
+        grad_copy(gh_st, gh_ref, gh_sem, e).wait()
+        grad_copy(gb_st, gb_ref, gb_sem, e).wait()
+
+    local = tokens // 32
+
+    def c_block(z, c, k):
+        return pl.ds(pl.multiple_of((z * 8 + 2 * c + k) * local, local), local)
+
+    def pair_copy(z):
+        return remote(pair_out.at[z], pair_in.at[z], po_sem.at[z], pi_sem.at[z], (gx, peer))
+
+    def chip_copy(z, k):
+        return remote(chip_out.at[z, k], chip_in.at[z, k], co_sem.at[z, k], ci_sem.at[z, k],
+                      (gx, 2 * chips[k] + core))
+
+    def line_copy(k):
+        return remote(line_out.at[k], line_in.at[k], lo_sem.at[k], li_sem.at[k], (line[k], gy))
+
+    order = [lax.rem(gx + 1 + k, 4) for k in range(4)]
+    for k in range(4):
+        z = order[k]
+        for c in range(4):
+            pair_out[k, c] = c_ref[c_block(z, c, 1 - core), :].astype(bf16)
+        pair_copy(k).start()
+    for k in range(4):
+        z = order[k]
+        pair_copy(k).wait_recv()
+        for j in range(3):
+            chip_out[k, j] = (c_ref[c_block(z, chips[j], core), :] + pair_in[k, chips[j]].astype(f32)).astype(bf16)
+            chip_copy(k, j).start()
+    for k in range(4):
+        z = order[k]
+        total = c_ref[c_block(z, chip, core), :] + pair_in[k, chip].astype(f32)
+        for j in range(3):
+            chip_copy(k, j).wait_recv()
+            total = total + chip_in[k, j].astype(f32)
+        if k < 3:
+            line_out[k] = total.astype(bf16)
+            line_copy(k).start()
+        else:
+            out_ref[gx] = total
+    for k in range(3):
+        line_copy(k).wait_recv()
+        src = lax.rem(gx + 3 - k, 4)
+        out_ref[src] = line_in[k].astype(f32)
+    for k in range(4):
+        pair_copy(k).wait_send()
+        for j in range(3):
+            chip_copy(k, j).wait_send()
+    for k in range(3):
+        line_copy(k).wait_send()
+
+
+def moe(rows, slot_row, slot_col, w1, w2, collective_id):
+    experts, width, units = w1.shape
+    tokens = rows.shape[0]
+    capacity = tokens * 5 // (4 * experts)
+    local = tokens // 32
+    vm = pl.BlockSpec(memory_space=pltpu.VMEM)
+    hbm = pl.BlockSpec(memory_space=pl.ANY)
+    dma = pltpu.SemaphoreType.DMA
+    return pl.pallas_call(
+        functools.partial(moe_kernel, experts, capacity, width, units, tokens),
+        out_shape=(jax.ShapeDtypeStruct((4, local, 2 * width), f32),
+                   jax.ShapeDtypeStruct((experts, width, units), f32),
+                   jax.ShapeDtypeStruct((experts, width, units), f32)),
+        in_specs=[vm] * 5,
+        out_specs=(vm, hbm, hbm),
+        scratch_shapes=[
+            pltpu.VMEM((RING, capacity, width), bf16),
+            pltpu.VMEM((RING, capacity, width), bf16),
+            pltpu.VMEM((RING, 2 * capacity, units), bf16),
+            pltpu.VMEM((experts, 2 * capacity, units), bf16),
+            pltpu.VMEM((experts, 2 * capacity, units), bf16),
+            pltpu.VMEM((tokens, 2 * width), f32),
+            pltpu.VMEM((GROUP * capacity, 2 * width), bf16),
+            pltpu.VMEM((2, width, units), f32),
+            pltpu.VMEM((2, width, units), f32),
+            pltpu.VMEM((4, 4, local, 2 * width), bf16),
+            pltpu.VMEM((4, 4, local, 2 * width), bf16),
+            pltpu.VMEM((4, 3, local, 2 * width), bf16),
+            pltpu.VMEM((4, 3, local, 2 * width), bf16),
+            pltpu.VMEM((3, local, 2 * width), bf16),
+            pltpu.VMEM((3, local, 2 * width), bf16),
+            dma((RING,)), dma((experts,)), dma((experts,)), dma((experts,)), dma((2,)), dma((2,)),
+            dma((4,)), dma((4,)), dma((4, 3)), dma((4, 3)), dma((3,)), dma((3,)),
+        ],
+        compiler_params=pltpu.CompilerParams(
+            collective_id=collective_id, has_side_effects=True, vmem_limit_bytes=62 * 2**20),
+        cost_estimate=pl.CostEstimate(flops=20 * 10**9, bytes_accessed=50 * 10**6, transcendentals=2 * 10**6),
+    )(rows, slot_row, slot_col, w1, w2)
+
+
+def fits(mesh):
+    return mesh.shape["gx"] == 4 and mesh.shape["gy"] == 8
+
+
+def expert_slots(expert_choice, experts, capacity):
+    all_tokens = expert_choice.shape[0]
+    tok_block = 128
+    chosen_rows = jnp.arange(experts, dtype=jnp.int32)[:, None] == expert_choice[None, :]
+    chosen_low = chosen_rows.astype(jnp.bfloat16).reshape(experts, all_tokens // tok_block, tok_block)
+    block_iota = jnp.arange(tok_block, dtype=jnp.int32)
+    upper = (block_iota[:, None] <= block_iota[None, :]).astype(jnp.bfloat16)
+    inside_count = jnp.einsum("ebi,ij->ebj", chosen_low, upper, preferred_element_type=jnp.float32)
+    block_totals = inside_count[:, :, tok_block - 1]
+    earlier_blocks = jnp.cumsum(block_totals, axis=1) - block_totals
+    counted = (inside_count + earlier_blocks[:, :, None]).reshape(experts, all_tokens)
+    position = (jnp.sum(jnp.where(chosen_rows, counted, 0.0), axis=0) - 1.0).astype(jnp.int32)
+    return jnp.where(position < capacity, expert_choice * capacity + position, -1)
+
+
+def fast(
+    x_in,
+    norm1_gain,
+    w_query,
+    w_key,
+    w_value,
+    relative_bias_table,
+    w_out,
+    norm2_gain,
+    w_router,
+    w_hidden,
+    w_back,
+    expert_choice,
+    doc_ids,
+    grad_out,
+):
+    token_devs = lax.axis_size("gy")
+    width_devs = lax.axis_size("gx")
+    member = lax.axis_index("gy")
+    column = lax.axis_index("gx")
+    local_count = x_in.shape[0]
+    width_cols = w_router.shape[0]
+    own_rows = local_count * width_devs
+    all_tokens = own_rows * token_devs
+    seq_len = local_count * token_devs
+    experts = EXPERTS
+    capacity = all_tokens * 5 // (4 * experts)
+    score_scale = HSIZE ** (-0.5)
+    reach = min((WINDOW + local_count - 2) // local_count, token_devs - 1)
+    key_count = (2 * reach + 1) * local_count
+    all_weights = lax.all_gather(
+        jnp.concatenate([w_query, w_key, w_value, w_out.reshape(w_query.shape)], axis=1)[None],
+        ("gx", "gy"),
+        axis=0,
+        tiled=True,
+    )
+    head_cols = w_query.shape[1]
+    qkv_full = jnp.concatenate(
+        [
+            rows_cols(all_weights[:, :, k * head_cols : (k + 1) * head_cols], width_devs, token_devs)
+            for k in range(3)
+        ],
+        axis=1,
+    )
+    out_full = cols_rows(
+        all_weights[:, :, 3 * head_cols :].reshape(-1, *w_out.shape), width_devs, token_devs
+    )
+    head_width = out_full.shape[0]
+    inputs_row = x_in.astype(jnp.float32)
+    scale_first = lax.rsqrt(jnp.mean(inputs_row * inputs_row, axis=-1, keepdims=True) + epsilon)
+    normed_first = (inputs_row * scale_first * norm1_gain).astype(jnp.bfloat16)
+    qkv_rows = jnp.dot(normed_first, qkv_full, preferred_element_type=jnp.float32).astype(
+        jnp.bfloat16
+    )
+    query_heads = qkv_rows[:, :head_width].reshape(local_count, HEADS, HSIZE)
+    pair_window = collect_window(
+        qkv_rows[:, head_width:].reshape(local_count, 2, head_width), reach
+    )
+    key_heads = pair_window[:, 0].reshape(key_count, HEADS, HSIZE)
+    value_heads = pair_window[:, 1].reshape(key_count, HEADS, HSIZE)
+    query_pos = member * local_count + jnp.arange(local_count, dtype=jnp.int32)
+    key_pos = (member - reach) * local_count + jnp.arange(key_count, dtype=jnp.int32)
+    offset = key_pos[None, :] - query_pos[:, None]
+    buckets = bucket_ids(offset)
+    bias_terms = sum(
+        jnp.where(buckets[None] == b, relative_bias_table[b][:, None, None], 0.0)
+        for b in range(relative_bias_table.shape[0])
+    )
+    no_doc = jnp.full((reach * local_count,), -1, jnp.int32)
+    doc_padded = jnp.concatenate([no_doc, doc_ids, no_doc], axis=0)
+    key_docs = lax.dynamic_slice_in_dim(doc_padded, member * local_count, key_count, 0)
+    query_docs = lax.dynamic_slice_in_dim(doc_ids, member * local_count, local_count, 0)
+    allowed = (jnp.abs(offset) < WINDOW) & (query_docs[:, None] == key_docs[None, :])
+    attention_scores = head_scores(query_heads, key_heads, bias_terms, allowed, score_scale)
+    row_peak = jnp.max(attention_scores, axis=-1, keepdims=True)
+    shifted = jnp.exp(attention_scores - row_peak)
+    row_sum = jnp.sum(shifted, axis=-1, keepdims=True)
+    log_total = row_peak + jnp.log(row_sum)
+    weights_reduced_precision = (shifted / row_sum).astype(jnp.bfloat16)
+    attended = jnp.einsum(
+        "hqk,khd->qhd", weights_reduced_precision, value_heads, preferred_element_type=jnp.float32
+    )
+    attended_low = attended.reshape(local_count, head_width).astype(jnp.bfloat16)
+    attn_low = jnp.dot(attended_low, out_full, preferred_element_type=jnp.float32).astype(
+        jnp.bfloat16
+    )
+
+    hidden_first = inputs_row + attn_low.astype(jnp.float32)
+    grad_rows = grad_out.astype(jnp.float32)
+    scale_second = lax.rsqrt(
+        jnp.mean(hidden_first * hidden_first, axis=-1, keepdims=True) + epsilon
+    )
+    gain_second = lax.all_gather(norm2_gain, "gx", axis=0, tiled=True)
+    router_full = lax.all_gather(w_router, "gx", axis=0, tiled=True)
+    normed_second = hidden_first * scale_second * gain_second
+    logits = jnp.dot(normed_second, router_full, precision=highest)
+    router = jax.nn.softmax(logits, axis=-1)
+    own_choice = lax.dynamic_slice_in_dim(
+        expert_choice, (column * token_devs + member) * local_count, local_count, 0
+    )
+    picked = (own_choice[:, None] == jnp.arange(experts, dtype=jnp.int32)[None, :]).astype(
+        jnp.float32
+    )
+    gate_value = jnp.sum(picked * router, axis=-1, keepdims=True)
+    slot_all = expert_slots(expert_choice, experts, capacity)
+    pair_rows = jnp.stack(
+        [normed_second.astype(jnp.bfloat16), (grad_rows * gate_value).astype(jnp.bfloat16)], axis=1
+    ).reshape(local_count, 2, width_devs, width_cols)
+    pair_rows = jnp.transpose(pair_rows, (2, 0, 1, 3)).reshape(
+        width_devs, local_count, 2 * width_cols
+    )
+    moved = lax.all_to_all(pair_rows, "gx", split_axis=0, concat_axis=0, tiled=True)
+    everyone = lax.all_gather(moved[:, None], "gy", axis=1, tiled=True)
+    dispatch_rows = everyone.reshape(all_tokens, 2 * width_cols)
+    hidden_weight = jnp.transpose(w_hidden.reshape(width_cols, -1, experts), (2, 0, 1))
+    back_weight = jnp.transpose(w_back.reshape(width_cols, -1, experts), (2, 0, 1))
+    returned, hidden_grads, back_grads = moe(
+        dispatch_rows, slot_all[None, :], slot_all[:, None], hidden_weight, back_weight, 1
+    )
+    grad_hidden = jnp.transpose(hidden_grads, (1, 2, 0)).reshape(width_cols, -1)
+    grad_back = jnp.transpose(back_grads, (1, 2, 0)).reshape(width_cols, -1)
+    returned = jnp.transpose(
+        returned.reshape(width_devs, local_count, 2, width_cols), (2, 1, 0, 3)
+    ).reshape(2, local_count, width_devs * width_cols)
+    routed, back_routed = returned[0], returned[1]
+    out_rows = hidden_first + gate_value * routed
+    gate_grad = jnp.sum(grad_rows * routed, axis=-1, keepdims=True)
+    logit_grad = router * (gate_grad * picked - gate_value * gate_grad)
+    second_grad = back_routed + jnp.einsum("re,de->rd", logit_grad, router_full, precision=highest)
+    router_part = jnp.einsum("rd,re->de", normed_second, logit_grad, precision=highest)
+    norm2_part = jnp.sum(second_grad * hidden_first * scale_second, axis=0)
+    gained_second = second_grad * gain_second
+    row_dot_second = jnp.sum(gained_second * hidden_first, axis=-1, keepdims=True)
+    hidden_rows = (
+        grad_rows
+        + scale_second * gained_second
+        - hidden_first * scale_second**3 * row_dot_second / D
+    )
+    attn_grad = hidden_rows.astype(jnp.bfloat16)
+    grad_out_full = jnp.einsum(
+        "rf,rd->fd", attended_low, attn_grad, preferred_element_type=jnp.float32
+    )
+    attended_grad = (
+        jnp.einsum("rd,fd->rf", attn_grad, out_full, preferred_element_type=jnp.float32)
+        .astype(jnp.bfloat16)
+        .reshape(local_count, HEADS, HSIZE)
+    )
+    scores_again = head_scores(query_heads, key_heads, bias_terms, allowed, score_scale)
+    probs_again = jnp.exp(scores_again - log_total)
+    value_grad = jnp.einsum(
+        "hqk,qhd->khd",
+        probs_again.astype(jnp.bfloat16),
+        attended_grad,
+        preferred_element_type=jnp.float32,
+    )
+    prob_grad = jnp.einsum(
+        "qhd,khd->hqk", attended_grad, value_heads, preferred_element_type=jnp.float32
+    )
+    score_gradient = (
+        probs_again * (prob_grad - jnp.sum(probs_again * prob_grad, axis=-1, keepdims=True))
+    ).astype(jnp.bfloat16)
+    query_grad = (
+        jnp.einsum("hqk,khd->qhd", score_gradient, key_heads, preferred_element_type=jnp.float32)
+        * score_scale
+    ).astype(jnp.bfloat16)
+    key_grad = (
+        jnp.einsum("hqk,qhd->khd", score_gradient, query_heads, preferred_element_type=jnp.float32)
+        * score_scale
+    )
+    band_low = max(0, reach * local_count - 90)
+    band_high = min(key_count, reach * local_count + local_count + 90)
+    bucket_iota = jnp.arange(relative_bias_table.shape[0], dtype=jnp.int32)
+    band_onehot = (buckets[None, :, band_low:band_high] == bucket_iota[:, None, None]).astype(
+        jnp.bfloat16
+    )
+    table_near = jnp.einsum(
+        "ivt,zvt->zi",
+        score_gradient[:, :, band_low:band_high],
+        band_onehot,
+        preferred_element_type=jnp.float32,
+    )
+    left_far = jnp.sum(score_gradient[:, :, :band_low].astype(jnp.float32), axis=(1, 2))
+    right_far = jnp.sum(score_gradient[:, :, band_high:].astype(jnp.float32), axis=(1, 2))
+    table_part = (
+        table_near
+        + (bucket_iota == 15).astype(jnp.float32)[:, None] * left_far[None, :]
+        + (bucket_iota == 31).astype(jnp.float32)[:, None] * right_far[None, :]
+    )
+    pair_grads = return_window(
+        jnp.stack(
+            [key_grad.reshape(key_count, head_width), value_grad.reshape(key_count, head_width)],
+            axis=1,
+        ),
+        reach,
+        local_count,
+    )
+    qkv_grad = jnp.concatenate(
+        [
+            query_grad.reshape(local_count, head_width),
+            pair_grads.astype(jnp.bfloat16).reshape(local_count, 2 * head_width),
+        ],
+        axis=1,
+    )
+    qkv_grads = jnp.einsum("rd,rc->dc", normed_first, qkv_grad, preferred_element_type=jnp.float32)
+    first_grad = jnp.einsum("rc,dc->rd", qkv_grad, qkv_full, preferred_element_type=jnp.float32)
+    norm1_part = jnp.sum(first_grad * inputs_row * scale_first, axis=0)
+    gained_first = first_grad * norm1_gain
+    row_dot_first = jnp.sum(gained_first * inputs_row, axis=-1, keepdims=True)
+    input_rows = (
+        hidden_rows + scale_first * gained_first - inputs_row * scale_first**3 * row_dot_first / D
+    )
+    summed = lax.psum((norm1_part, table_part, norm2_part, router_part), ("gx", "gy"))
+    grad_norm2 = lax.dynamic_slice_in_dim(summed[2], column * width_cols, width_cols, 0)
+    grad_router = lax.dynamic_slice_in_dim(summed[3], column * width_cols, width_cols, 0)
+    weight_blocks = jnp.concatenate(
+        [
+            grid_rows_cols(qkv_grads[:, k * head_width : (k + 1) * head_width], width_devs, token_devs)
+            for k in range(3)
+        ]
+        + [grid_cols_rows(grad_out_full, width_devs, token_devs).reshape(-1, *w_query.shape)],
+        axis=2,
+    )
+    weight_part = lax.psum_scatter(
+        weight_blocks, ("gx", "gy"), scatter_dimension=0, tiled=True
+    )[0]
+    return (
+        out_rows,
+        input_rows,
+        summed[0],
+        weight_part[:, :head_cols],
+        weight_part[:, head_cols : 2 * head_cols],
+        weight_part[:, 2 * head_cols : 3 * head_cols],
+        summed[1],
+        weight_part[:, 3 * head_cols :].reshape(w_out.shape),
+        grad_norm2,
+        grad_router,
+        grad_hidden,
+        grad_back,
+    )
+
+
 def solution(mesh):
     return jax.shard_map(
-        local,
+        fast if fits(mesh) else local,
         mesh=mesh,
         in_specs=(
             P(("gx", "gy"), None),

time: 2610 us -> 1010 us (0.39)
  local copies, waits for them, and re-layouts: 1200 us -> 219 us
  waiting for transfers between devices: 1090 us -> 212 us
  Pallas kernels: 0 us -> 231 us
  blocking collectives: 73.2 us -> 102 us
    gather x10 -> x0, local copies, waits for them, and re-layouts: 996 us -> none  [the longest x2 879 us: local(): bias_terms = jnp.take(jnp.transpose(relative_bias_table), buckets, axis=1)]
    reduce_scatter x8 -> x1, waiting for transfers between devices: 628 us -> 48.2 us  [fast(): lax.psum_scatter(weight_blocks, ('gx', 'gy'), scatter_dimension=0, tiled=...]
    pallas_call x0 -> x1, Pallas kernels: none -> 231 us  [moe(): pl.pallas_call(functools.partial(moe_kernel, experts, capacity, width, un...]
    all_gather x8 -> x2, waiting for transfers between devices: 256 us -> 63.3 us  [the longest x1 63.3 us: fast(): lax.all_gather(jnp.concatenate([w_query, w_key, w_value, w_out.reshape(w_...]
    ppermute x28, waiting for transfers between devices: 151 us -> 100 us  [passed_along(): lax.ppermute(value, axis, [(source, source + steps) for source in range(f...]
    dot_general x1, matrix products: 7.85 us -> 57.8 us  [head_scores(): jnp.einsum('qhd,khd->hqk', query_heads, key_heads, preferred_element_type...]
    dot_general x22 -> x16, matrix products: 83 us -> 40.1 us  [the longest x1 12 us: fast(): jnp.einsum('qhd,khd->hqk', attended_grad, value_heads, preferred_element_...]
    psum x2 -> x1, waiting for transfers between devices: 36.1 us -> 0.02 us  [fast(): lax.psum((norm1_part, table_part, norm2_part, router_part), ('gx', 'gy'))]
  transfers between devices with their start and end apart: 49 -> 32, of which waited for: 26 -> 11; matrix products, arithmetic and copies ran while one was open for 45% -> 18% of each run, Pallas kernels for 0% -> 0%
where the time goes in v1:
time: 1010 us; the launch traced here: 1000 us
  Pallas kernels  231 us (23%)
  local copies, waits for them, and re-layouts  219 us (22%)
  waiting for transfers between devices  212 us (21%)
  blocking collectives  102 us (10%)
  matrix products  98 us (10%)
  starting transfers between devices  64.8 us (6%)
  other arithmetic  58.5 us (6%)
  between operations  16.1 us (2%)
    pallas_call x1, Pallas kernels, moe(): pl.pallas_call(functools.partial(moe_kernel, experts, capacity, width, un...  231 us
    ppermute x28, waiting for transfers between devices, passed_along(): lax.ppermute(value, axis, [(source, source + steps) for source in range(f...  100 us
    psum x1, blocking collectives, fast(): lax.psum((norm1_part, table_part, norm2_part, router_part), ('gx', 'gy'))  65.8 us
    ppermute x28, starting transfers between devices, passed_along(): lax.ppermute(value, axis, [(source, source + steps) for source in range(f...  64.6 us
    all_gather x1, waiting for transfers between devices, fast(): lax.all_gather(jnp.concatenate([w_query, w_key, w_value, w_out.reshape(w_...  63.3 us
    unnamed x128, local copies, waits for them, and re-layouts  61.5 us
    dot_general x1, matrix products, head_scores(): jnp.einsum('qhd,khd->hqk', query_heads, key_heads, preferred_element_type...  57.8 us
    reduce_scatter x1, waiting for transfers between devices, fast(): lax.psum_scatter(weight_blocks, ('gx', 'gy'), scatter_dimension=0, tiled=...  48.2 us
  transfers between devices with their start and end apart: 32, of which 11 were waited for; matrix products, arithmetic and copies ran while one was open for 18% of the time, Pallas kernels for 0%

profile of v1, /device:TPU:0, one launch (start us, length us, event | category | flops | bytes accessed | tf_op | source)
XLA Modules:
  0.0 1000.8 jit_solution(271864328873811471)
XLA Ops:
  14.6 63.3 %all-gather.6.cloned.1.call-done = bf16[6144,384]{1,0:T(8,128)(2,1)} async-done(((bf16[192,384]{1,0:T(8,128)(2,1)}), bf16[6144,384]{1,0:T(8,128)(2,1)}) %all-gather.6.cloned.1.call-update) | async-done | bytes 4718608 | tf_op jit(solution)/shard_map/all_gather | solution.py:775
  77.9 6.5 fusion.101
  86.5 3.8 reshape.1234
  90.3 2.4 constant_dynamic-update-slice_fusion.2
  94.9 2.9 reshape.1236
  97.8 3.6 copy.111
  101.4 3.8 reshape.1238
  106.4 2.4 constant_dynamic-update-slice_fusion
  108.9 2.7 convolution_convert_fusion
  111.7 4.0 collective-permute-start
  115.7 2.3 collective-permute-start.1
  118.1 7.8 fusion.24
  131.4 13.3 %all-gather.2 = f32[4,192,32]{1,2,0:T(8,128)S(1)} all-gather(f32[1,192,32]{1,2,0:T(8,128)S(1)} %bitcast.180), channel_id=1, replica_groups=mesh['gx'=4,'gy'=8] {'gx'}, dimensions={0}, use_global_device_ids=true | all-gather | bytes 122880 | tf_op jit(solution)/shard_map/all_gather | solution.py:838
  146.5 10.8 %all-reduce = f32[768]{0:T(1024)S(1)} all-reduce(f32[768]{0:T(1024)S(1)} %dynamic-update-slice), channel_id=1, replica_groups=mesh['gx'=4,'gy'=8] {'gx'}, use_global_device_ids=true, to_apply=%add | all-reduce | flops 768 | bytes 6144
  159.6 2.3 reshape_reshape.6
  184.4 9.5 collective-permute-done.8
  195.9 20.4 %collective-permute-done.10 = bf16[128,2,768]{2,1,0:T(2,128)(2,1)S(1)} collective-permute-done((bf16[128,2,768]{2,1,0:T(2,128)(2,1)S(1)}, bf16[128,2,768]{2,1,0:T(2,128)(2,1)S(1)}, u32[]{:S(2)}, u32[]{:S(2)}) %collective-permute-start.10) | collective-permute-done | bytes 393248 | tf_op jit(solution)/shard_map/ppermute | solution.py:26
  219.4 9.4 fusion.100
  228.9 10.8 %copy.114 = bf16[1920,1,768]{0,2,1:T(8,128)(2,1)S(1)} copy(bf16[1920,1,768]{2,1,0:T(2,128)(2,1)} %get-tuple-element.114) | data formatting | bytes 5898240 | tf_op jit(solution)/shard_map/slice | solution.py:803
  239.7 12.6 %copy.112 = bf16[1920,1,768]{0,2,1:T(8,128)(2,1)} copy(bf16[1920,1,768]{2,1,0:T(2,128)(2,1)} %get-tuple-element.115) | data formatting | bytes 5898240 | tf_op jit(solution)/shard_map/slice | solution.py:804
  252.3 57.8 %fusion.104 = (f32[12,128]{1,0:T(8,128)S(1)}, f32[12,128,1920]{2,1,0:T(8,128)}) fusion(f32[12]{0:T(128)} %get-tuple-element.90, pred[128,1920]{1,0:T(8,128)(4,1)} %get-tuple-element.159, f32[12]{0:T(128)} %get-tuple-element.91, pred[128,1920]{1,0:T(8,128)(4,1)} %get-tuple-element.158, f32[12]{0:T(128)S(1)} %get-tuple-element.61, ...), kind=kOutput, calls=%fused_computation.269 | convolution fusion | flops 575076864 | bytes 23059968 | tf_op jit(solution)/shard_map/qhd,khd->hqk/dot_general | solution.py:88
  310.2 6.2 fusion
  317.9 4.6 fusion.19
  325.0 12.0 %all_to_all.5 = bf16[4,128,384]{1,2,0:T(8,128)(2,1)} all-to-all(bf16[4,128,384]{1,2,0:T(8,128)(2,1)S(1)} %bitcast.163), channel_id=1, replica_groups=mesh['gx'=4,'gy'=8] {'gx'}, dimensions={0} | all-to-all | bytes 786432 | tf_op jit(solution)/shard_map/all_to_all | solution.py:856
  340.5 8.0 copy.123
  348.5 8.8 copy.124
  357.3 7.9 copy.125
  365.2 8.7 copy.126
  373.9 4.6 copy.120
  378.5 230.6 %shard_map.229 = (f32[4,128,384]{2,1,0:T(8,128)}, f32[32,192,384]{2,1,0:T(8,128)}, f32[32,192,384]{2,1,0:T(8,128)}) custom-call(bf16[4096,384]{1,0:T(8,128)(2,1)} %bitcast.157, s32[1,4096]{1,0:T(1,128)} %bitcast.179, s32[4096,1]{1,0:T(8,128)} %copy.127.slot_col, bf16[32,192,384]{2,1,0:T(8,128)(2,1)} %bitcast.155, bf16[32,192,384]{2,1,0:T(8,128)(2,1)} %bitcast.156), custom_call_target="tpu_custom_call" | custom-call | flops 20000000000 | bytes 50000000 | tf_op jit(solution)/shard_map/pallas_call | solution.py:694
  611.8 2.4 convert_bitcast_fusion
  614.9 2.3 convolution_convert_fusion.1
  619.0 12.0 %multiply_reduce_fusion = (f32[12,128]{1,0:T(8,128)S(1)}, f32[12,128,1920]{2,1,0:T(8,128)}) fusion(f32[12,128,1920]{2,1,0:T(8,128)} %get-tuple-element.165, f32[12,128]{1,0:T(8,128)S(1)} %log_add_fusion, bf16[128,12,64]{0,2,1:T(8,128)(2,1)} %bitcast.159, bf16[1920,12,64]{0,2,1:T(8,128)(2,1)} %bitcast.147), kind=kOutput, calls=%fused_computation.29 | convolution fusion | flops 386333184 | bytes 26750976 | tf_op jit(solution)/shard_map/qhd,khd->hqk/dot_general | solution.py:900
  631.0 2.2 fusion.2
  633.2 8.2 multiply_convert_fusion
  654.2 14.3 %collective-permute-done.14 = f32[128,2,768]{0,2,1:T(8,128)S(1)} collective-permute-done((f32[128,2,768]{0,2,1:T(8,128)S(1)}, f32[128,2,768]{0,2,1:T(8,128)S(1)}, u32[]{:S(2)}, u32[]{:S(2)}) %collective-permute-start.14) | collective-permute-done | bytes 786464 | tf_op jit(solution)/shard_map/ppermute | solution.py:26
  669.8 2.7 collective-permute-done.15
  673.8 30.3 %collective-permute-done.16 = f32[128,2,768]{0,2,1:T(8,128)} collective-permute-done((f32[128,2,768]{0,2,1:T(8,128)S(1)}, f32[128,2,768]{0,2,1:T(8,128)}, u32[]{:S(2)}, u32[]{:S(2)}) %collective-permute-start.16) | collective-permute-done | bytes 786464 | tf_op jit(solution)/shard_map/ppermute | solution.py:26
  704.1 2.2 collective-permute-start.21
  706.3 7.6 collective-permute-start.22
  715.2 4.2 fusion.45
  719.4 12.9 %collective-permute-start.23 = (f32[128,2,768]{0,2,1:T(8,128)}, f32[128,2,768]{0,2,1:T(8,128)}, u32[]{:S(2)}, u32[]{:S(2)}) collective-permute-start(f32[128,2,768]{0,2,1:T(8,128)} %get-tuple-element.106), channel_id=1, source_target_pairs={{0,3},{1,4},{2,5},{3,6},{4,7},{8,11},{9,12},{10,13},{11,14},{12,15... | collective-permute-start | bytes 2359304 | tf_op jit(solution)/shard_map/ppermute | solution.py:26
  736.6 2.2 collective-permute-start.26
  738.8 2.4 collective-permute-start.27
  743.8 4.8 reshape_reshape.7
  748.7 5.9 fusion.16
  754.7 3.8 collective-permute-done.24
  758.5 16.9 %collective-permute-done.25 = f32[128,2,768]{0,2,1:T(8,128)} collective-permute-done((f32[128,2,768]{0,2,1:T(8,128)}, f32[128,2,768]{0,2,1:T(8,128)}, u32[]{:S(2)}, u32[]{:S(2)}) %collective-permute-start.25) | collective-permute-done | bytes 786464 | tf_op jit(solution)/shard_map/ppermute | solution.py:26
  776.0 4.2 add_convert_fusion
  781.4 3.1 fusion.99
  784.5 3.1 reshape.1250
  787.7 2.2 copy.133
  789.9 3.1 reshape.1252
  793.1 2.2 copy.134
  795.3 3.1 reshape.1254
  801.3 9.6 pad_maximum_fusion
  816.0 12.8 %copy.140 = f32[192,384,32]{0,2,1:T(8,128)} copy(f32[192,384,32]{1,0,2:T(8,128)} %bitcast.149) | data formatting | bytes 18874368 | tf_op jit(solution)/shard_map/transpose | solution.py:864
  828.8 11.6 %copy.142 = f32[192,12288]{1,0:T(8,128)} copy(f32[192,12288]{0,1:T(8,128)} %bitcast.134) | data formatting | bytes 18874368
  840.4 12.8 %copy.141 = f32[192,384,32]{0,2,1:T(8,128)} copy(f32[192,384,32]{1,0,2:T(8,128)} %bitcast.148) | data formatting | bytes 18874368 | tf_op jit(solution)/shard_map/transpose | solution.py:865
  853.1 11.7 %copy.143 = f32[192,12288]{1,0:T(8,128)} copy(f32[192,12288]{0,1:T(8,128)} %bitcast.135) | data formatting | bytes 18874368
  864.9 4.7 convert_reduce_fusion.1
  872.0 3.6 fusion.63
  875.6 65.8 %all-reduce.1 = (f32[768]{0:T(1024)}, f32[32,12]{0,1:T(8,128)}, f32[768]{0:T(1024)S(1)}) all-reduce(f32[768]{0:T(1024)S(1)} %get-tuple-element.58, f32[32,12]{0,1:T(8,128)S(1)} %fusion.22, f32[768]{0:T(1024)S(1)} %get-tuple-element.56), channel_id=1, replica_groups=mesh['gx'=4,'gy'=8] {'gx','gy'}, use_global_device_ids=true, to_apply=%region_14.15 | all-reduce | flops 1920 | bytes 15360 | tf_op jit(solution)/shard_map/psum | solution.py:956
  942.9 48.2 %reduce-scatter.2.cloned.1.call-done = f32[1,192,384]{2,1,0:T(8,128)} async-done(((f32[32,192,384]{2,1,0:T(8,128)}), f32[1,192,384]{2,1,0:T(8,128)}) %reduce-scatter.2.cloned.1.call-update) | async-done | bytes 294928 | tf_op jit(solution)/shard_map/reduce_scatter | solution.py:967
  (245 shorter events, 101.7 us)
Async XLA Ops:
  7.2 70.7 %all-gather.6.cloned.1.call-start = ((), (), s32[]{:S(2)}) async-start(), calls=%async_computation.4 | async-start | bytes 4866048 | tf_op jit(solution)/shard_map/all_gather | solution.py:775
  9.8 364.1 %all-gather.8.cloned.1.call-start = ((), (), s32[]{:S(2)}) async-start(), calls=%async_computation.5 | async-start | bytes 3538944 | tf_op jit(solution)/shard_map/all_gather | solution.py:857
  14.6 94.3 %copy-start.37 = (f32[128]{0:T(128)}, f32[128]{0:T(128)S(1)}, u32[]{:S(2)}) copy-start(f32[128]{0:T(128)S(1)} %get-tuple-element.161) | copy-start | bytes 1540
  105.2 12.8 %copy-start.32 = (s32[1920]{0:T(1024)S(1)}, s32[1920]{0:T(1024)}, u32[]{:S(2)}) copy-start(s32[1920]{0:T(1024)} %get-tuple-element.175) | copy-start | bytes 23044
  105.2 12.8 %copy-start.36 = (s32[1920]{0:T(1024)S(1)}, s32[1920]{0:T(1024)}, u32[]{:S(2)}) copy-start(s32[1920]{0:T(1024)} %get-tuple-element.174) | copy-start | bytes 23044
  105.2 12.8 %copy-start.40 = (s32[128]{0:T(128)S(1)}, s32[128]{0:T(128)}, u32[]{:S(2)}) copy-start(s32[128]{0:T(128)} %iota_add_fusion.1) | copy-start | bytes 1540
  105.2 12.8 %copy-start.44 = (s32[128]{0:T(128)S(1)}, s32[128]{0:T(128)}, u32[]{:S(2)}) copy-start(s32[128]{0:T(128)} %dynamic_slice.15) | copy-start | bytes 1540
  111.6 14.3 %copy-start.10 = (f32[32,12]{0,1:T(8,128)S(1)}, f32[32,12]{0,1:T(8,128)}, u32[]{:S(2)}) copy-start(f32[32,12]{0,1:T(8,128)} %param.19) | copy-start | bytes 4612
  111.6 19.8 %copy-start.35 = (f32[192,32]{0,1:T(8,128)S(1)}, f32[192,32]{0,1:T(8,128)}, u32[]{:S(2)}) copy-start(f32[192,32]{0,1:T(8,128)} %param.22) | copy-start | bytes 73732
  111.6 33.4 %copy-start.46 = (u32[32]{0:T(128)S(1)}, u32[32]{0:T(128)}, u32[]{:S(2)}) copy-start(u32[32]{0:T(128)} %constant.53) | copy-start | bytes 388
  111.6 34.6 %copy-start.29 = (s32[4096]{0:T(1024)S(1)}, s32[4096]{0:T(1024)}, u32[]{:S(2)}) copy-start(s32[4096]{0:T(1024)} %param.25) | copy-start | bytes 49156
  111.6 34.7 %copy-start.42 = (f32[192]{0:T(256)S(1)}, f32[192]{0:T(256)}, u32[]{:S(2)}) copy-start(f32[192]{0:T(256)} %param.21) | copy-start | bytes 2308
  111.7 54.3 %collective-permute-start = (bf16[128,2,768]{2,1,0:T(2,128)(2,1)S(1)}, bf16[128,2,768]{2,1,0:T(2,128)(2,1)}, u32[]{:S(2)}, u32[]{:S(2)}) collective-permute-start(bf16[128,2,768]{2,1,0:T(2,128)(2,1)S(1)} %reshape.1239), channel_id=1, source_target_pairs={{0,7},{8,15},{16,23},{24,31}} | collective-permute-start | bytes 1179656 | tf_op jit(solution)/shard_map/ppermute | solution.py:26
  115.7 52.9 %collective-permute-start.1 = (bf16[128,2,768]{2,1,0:T(2,128)(2,1)S(1)}, bf16[128,2,768]{2,1,0:T(2,128)(2,1)}, u32[]{:S(2)}, u32[]{:S(2)}) collective-permute-start(bf16[128,2,768]{2,1,0:T(2,128)(2,1)S(1)} %reshape.1239), channel_id=1, source_target_pairs={{0,6},{1,7},{8,14},{9,15},{16,22},{17,23},{24,30},{25,31}} | collective-permute-start | bytes 1179656 | tf_op jit(solution)/shard_map/ppermute | solution.py:26
  126.4 44.9 %collective-permute-start.2 = (bf16[128,2,768]{2,1,0:T(2,128)(2,1)S(1)}, bf16[128,2,768]{2,1,0:T(2,128)(2,1)}, u32[]{:S(2)}, u32[]{:S(2)}) collective-permute-start(bf16[128,2,768]{2,1,0:T(2,128)(2,1)S(1)} %reshape.1239), channel_id=1, source_target_pairs={{0,5},{1,6},{2,7},{8,13},{9,14},{10,15},{16,21},{17,22},{18,23},{2... | collective-permute-start | bytes 1179656 | tf_op jit(solution)/shard_map/ppermute | solution.py:26
  129.4 44.5 %collective-permute-start.3 = (bf16[128,2,768]{2,1,0:T(2,128)(2,1)S(1)}, bf16[128,2,768]{2,1,0:T(2,128)(2,1)}, u32[]{:S(2)}, u32[]{:S(2)}) collective-permute-start(bf16[128,2,768]{2,1,0:T(2,128)(2,1)S(1)} %reshape.1239), channel_id=1, source_target_pairs={{0,4},{1,5},{2,6},{3,7},{8,12},{9,13},{10,14},{11,15},{16,20},{17,... | collective-permute-start | bytes 1179656 | tf_op jit(solution)/shard_map/ppermute | solution.py:26
  157.3 19.2 %collective-permute-start.4 = (bf16[128,2,768]{2,1,0:T(2,128)(2,1)S(1)}, bf16[128,2,768]{2,1,0:T(2,128)(2,1)}, u32[]{:S(2)}, u32[]{:S(2)}) collective-permute-start(bf16[128,2,768]{2,1,0:T(2,128)(2,1)S(1)} %reshape.1239), channel_id=1, source_target_pairs={{0,3},{1,4},{2,5},{3,6},{4,7},{8,11},{9,12},{10,13},{11,14},{12,15... | collective-permute-start | bytes 1179656 | tf_op jit(solution)/shard_map/ppermute | solution.py:26
  159.6 92.7 %copy-start.20 = (bf16[128,768]{0,1:T(8,128)(2,1)}, bf16[128,768]{0,1:T(8,128)(2,1)S(1)}, u32[]{:S(2)}) copy-start(bf16[128,768]{0,1:T(8,128)(2,1)S(1)} %copy.113) | copy-start | bytes 589828
  166.0 13.1 %collective-permute-start.5 = (bf16[128,2,768]{2,1,0:T(2,128)(2,1)S(1)}, bf16[128,2,768]{2,1,0:T(2,128)(2,1)S(1)}, u32[]{:S(2)}, u32[]{:S(2)}) collective-permute-start(bf16[128,2,768]{2,1,0:T(2,128)(2,1)S(1)} %reshape.1239), channel_id=1, source_target_pairs={{0,2},{1,3},{2,4},{3,5},{4,6},{5,7},{8,10},{9,11},{10,12},{11,13},... | collective-permute-start | bytes 1179656 | tf_op jit(solution)/shard_map/ppermute | solution.py:26
  168.6 12.2 %collective-permute-start.6 = (bf16[128,2,768]{2,1,0:T(2,128)(2,1)S(1)}, bf16[128,2,768]{2,1,0:T(2,128)(2,1)S(1)}, u32[]{:S(2)}, u32[]{:S(2)}) collective-permute-start(bf16[128,2,768]{2,1,0:T(2,128)(2,1)S(1)} %reshape.1239), channel_id=1, source_target_pairs={{0,1},{1,2},{2,3},{3,4},{4,5},{5,6},{6,7},{8,9},{9,10},{10,11},{11... | collective-permute-start | bytes 1179656 | tf_op jit(solution)/shard_map/ppermute | solution.py:26
  171.3 11.5 %collective-permute-start.7 = (bf16[128,2,768]{2,1,0:T(2,128)(2,1)S(1)}, bf16[128,2,768]{2,1,0:T(2,128)(2,1)S(1)}, u32[]{:S(2)}, u32[]{:S(2)}) collective-permute-start(bf16[128,2,768]{2,1,0:T(2,128)(2,1)S(1)} %reshape.1239), channel_id=1, source_target_pairs={{1,0},{2,1},{3,2},{4,3},{5,4},{6,5},{7,6},{9,8},{10,9},{11,10},{12... | collective-permute-start | bytes 1179656 | tf_op jit(solution)/shard_map/ppermute | solution.py:26
  173.9 20.0 %collective-permute-start.8 = (bf16[128,2,768]{2,1,0:T(2,128)(2,1)S(1)}, bf16[128,2,768]{2,1,0:T(2,128)(2,1)S(1)}, u32[]{:S(2)}, u32[]{:S(2)}) collective-permute-start(bf16[128,2,768]{2,1,0:T(2,128)(2,1)S(1)} %reshape.1239), channel_id=1, source_target_pairs={{2,0},{3,1},{4,2},{5,3},{6,4},{7,5},{10,8},{11,9},{12,10},{13,11},... | collective-permute-start | bytes 1179656 | tf_op jit(solution)/shard_map/ppermute | solution.py:26
  176.5 19.0 %collective-permute-start.9 = (bf16[128,2,768]{2,1,0:T(2,128)(2,1)S(1)}, bf16[128,2,768]{2,1,0:T(2,128)(2,1)S(1)}, u32[]{:S(2)}, u32[]{:S(2)}) collective-permute-start(bf16[128,2,768]{2,1,0:T(2,128)(2,1)S(1)} %reshape.1239), channel_id=1, source_target_pairs={{3,0},{4,1},{5,2},{6,3},{7,4},{11,8},{12,9},{13,10},{14,11},{15,12... | collective-permute-start | bytes 1179656 | tf_op jit(solution)/shard_map/ppermute | solution.py:26
  179.2 37.1 %collective-permute-start.10 = (bf16[128,2,768]{2,1,0:T(2,128)(2,1)S(1)}, bf16[128,2,768]{2,1,0:T(2,128)(2,1)S(1)}, u32[]{:S(2)}, u32[]{:S(2)}) collective-permute-start(bf16[128,2,768]{2,1,0:T(2,128)(2,1)S(1)} %reshape.1239), channel_id=1, source_target_pairs={{4,0},{5,1},{6,2},{7,3},{12,8},{13,9},{14,10},{15,11},{20,16},{21,... | collective-permute-start | bytes 1179656 | tf_op jit(solution)/shard_map/ppermute | solution.py:26
  180.8 37.6 %collective-permute-start.11 = (bf16[128,2,768]{2,1,0:T(2,128)(2,1)S(1)}, bf16[128,2,768]{2,1,0:T(2,128)(2,1)S(1)}, u32[]{:S(2)}, u32[]{:S(2)}) collective-permute-start(bf16[128,2,768]{2,1,0:T(2,128)(2,1)S(1)} %reshape.1239), channel_id=1, source_target_pairs={{5,0},{6,1},{7,2},{13,8},{14,9},{15,10},{21,16},{22,17},{23,18},{2... | collective-permute-start | bytes 1179656 | tf_op jit(solution)/shard_map/ppermute | solution.py:26
  182.7 36.0 %collective-permute-start.12 = (bf16[128,2,768]{2,1,0:T(2,128)(2,1)S(1)}, bf16[128,2,768]{2,1,0:T(2,128)(2,1)S(1)}, u32[]{:S(2)}, u32[]{:S(2)}) collective-permute-start(bf16[128,2,768]{2,1,0:T(2,128)(2,1)S(1)} %reshape.1239), channel_id=1, source_target_pairs={{6,0},{7,1},{14,8},{15,9},{22,16},{23,17},{30,24},{31,25}} | collective-permute-start | bytes 1179656 | tf_op jit(solution)/shard_map/ppermute | solution.py:26
  193.9 25.2 %collective-permute-start.13 = (bf16[128,2,768]{2,1,0:T(2,128)(2,1)S(1)}, bf16[128,2,768]{2,1,0:T(2,128)(2,1)S(1)}, u32[]{:S(2)}, u32[]{:S(2)}) collective-permute-start(bf16[128,2,768]{2,1,0:T(2,128)(2,1)S(1)} %reshape.1239), channel_id=1, source_target_pairs={{7,0},{15,8},{23,16},{31,24}} | collective-permute-start | bytes 1179656 | tf_op jit(solution)/shard_map/ppermute | solution.py:26
  239.6 70.5 %copy-start.8 = (bf16[1920,1,768]{0,2,1:T(8,128)(2,1)}, bf16[1920,1,768]{0,2,1:T(8,128)(2,1)S(1)}, u32[]{:S(2)}) copy-start(bf16[1920,1,768]{0,2,1:T(8,128)(2,1)S(1)} %copy.114) | copy-start | bytes 8847364
  322.5 18.0 %copy-start.26 = (bf16[12,64,128]{2,1,0:T(8,128)(2,1)}, bf16[12,64,128]{2,1,0:T(8,128)(2,1)S(1)}, u32[]{:S(2)}) copy-start(bf16[12,64,128]{2,1,0:T(8,128)(2,1)S(1)} %fusion.19) | copy-start | bytes 589828
  323.1 288.0 %copy-start.4 = (f32[128,768]{1,0:T(8,128)}, f32[128,768]{1,0:T(8,128)S(1)}, u32[]{:S(2)}) copy-start(f32[128,768]{1,0:T(8,128)S(1)} %get-tuple-element.167) | copy-start | bytes 1179652
  324.6 286.3 %copy-start.39 = (f32[128]{0:T(128)}, f32[128]{0:T(128)S(1)}, u32[]{:S(2)}) copy-start(f32[128]{0:T(128)S(1)} %select_reduce_fusion.1) | copy-start | bytes 1540
  337.0 533.5 %all-reduce.4.cloned.1.call-start = ((), (), s32[]{:S(2)}) async-start(), calls=%async_computation.3 | async-start | bytes 196608 | tf_op jit(solution)/shard_map/psum | solution.py:956
  611.8 19.1 %slice-start = ((s8[11796480]{0:T(1024)(128)(4,1)}), s8[3407872]{0:T(1024)(128)(4,1)S(1)}, s32[]{:S(2)}) async-start(s8[11796480]{0:T(1024)(128)(4,1)} %bitcast.124), calls=%async_computation.6 | async-start | bytes 6815744
  618.9 12.0 %slice-start.1 = ((s8[11796480]{0:T(1024)(128)(4,1)}), s8[4194304]{0:T(1024)(128)(4,1)S(1)}, s32[]{:S(2)}) async-start(s8[11796480]{0:T(1024)(128)(4,1)} %bitcast.124), calls=%async_computation.7 | async-start | bytes 8388608
  618.9 12.0 %slice-start.2 = ((s8[11796480]{0:T(1024)(128)(4,1)}), s8[4194304]{0:T(1024)(128)(4,1)S(1)}, s32[]{:S(2)}) async-start(s8[11796480]{0:T(1024)(128)(4,1)} %bitcast.124), calls=%async_computation.8 | async-start | bytes 8388608
  619.0 12.0 %copy-start.16 = (bf16[128,768]{0,1:T(8,128)(2,1)S(1)}, bf16[128,768]{0,1:T(8,128)(2,1)}, u32[]{:S(2)}) copy-start(bf16[128,768]{0,1:T(8,128)(2,1)} %copy.132) | copy-start | bytes 589828
  644.0 69.9 %copy-start.5 = (f32[128,768]{1,0:T(8,128)S(1)}, f32[128,768]{1,0:T(8,128)}, u32[]{:S(2)}) copy-start(f32[128,768]{1,0:T(8,128)} %copy-done.4) | copy-start | bytes 1179652
  644.0 71.0 %copy-start.28 = (bf16[768,128]{0,1:T(8,128)(2,1)S(1)}, bf16[768,128]{0,1:T(8,128)(2,1)}, u32[]{:S(2)}) copy-start(bf16[768,128]{0,1:T(8,128)(2,1)} %get-tuple-element.95) | copy-start | bytes 589828
  647.7 20.8 %collective-permute-start.14 = (f32[128,2,768]{0,2,1:T(8,128)S(1)}, f32[128,2,768]{0,2,1:T(8,128)S(1)}, u32[]{:S(2)}, u32[]{:S(2)}) collective-permute-start(f32[128,2,768]{0,2,1:T(8,128)S(1)} %get-tuple-element.97), channel_id=1, source_target_pairs={{7,0},{15,8},{23,16},{31,24}} | collective-permute-start | bytes 2359304 | tf_op jit(solution)/shard_map/ppermute | solution.py:26
  649.0 23.5 %collective-permute-start.15 = (f32[128,2,768]{0,2,1:T(8,128)S(1)}, f32[128,2,768]{0,2,1:T(8,128)}, u32[]{:S(2)}, u32[]{:S(2)}) collective-permute-start(f32[128,2,768]{0,2,1:T(8,128)S(1)} %get-tuple-element.98), channel_id=1, source_target_pairs={{6,0},{7,1},{14,8},{15,9},{22,16},{23,17},{30,24},{31,25}} | collective-permute-start | bytes 2359304 | tf_op jit(solution)/shard_map/ppermute | solution.py:26
  650.3 53.7 %collective-permute-start.16 = (f32[128,2,768]{0,2,1:T(8,128)S(1)}, f32[128,2,768]{0,2,1:T(8,128)}, u32[]{:S(2)}, u32[]{:S(2)}) collective-permute-start(f32[128,2,768]{0,2,1:T(8,128)S(1)} %get-tuple-element.99), channel_id=1, source_target_pairs={{5,0},{6,1},{7,2},{13,8},{14,9},{15,10},{21,16},{22,17},{23,18},{2... | collective-permute-start | bytes 2359304 | tf_op jit(solution)/shard_map/ppermute | solution.py:26
  651.6 54.6 %collective-permute-start.17 = (f32[128,2,768]{0,2,1:T(8,128)S(1)}, f32[128,2,768]{0,2,1:T(8,128)}, u32[]{:S(2)}, u32[]{:S(2)}) collective-permute-start(f32[128,2,768]{0,2,1:T(8,128)S(1)} %get-tuple-element.100), channel_id=1, source_target_pairs={{4,0},{5,1},{6,2},{7,3},{12,8},{13,9},{14,10},{15,11},{20,16},{21,... | collective-permute-start | bytes 2359304 | tf_op jit(solution)/shard_map/ppermute | solution.py:26
  652.9 66.5 %collective-permute-start.18 = (f32[128,2,768]{0,2,1:T(8,128)}, f32[128,2,768]{0,2,1:T(8,128)S(1)}, u32[]{:S(2)}, u32[]{:S(2)}) collective-permute-start(f32[128,2,768]{0,2,1:T(8,128)} %get-tuple-element.101), channel_id=1, source_target_pairs={{3,0},{4,1},{5,2},{6,3},{7,4},{11,8},{12,9},{13,10},{14,11},{15,12... | collective-permute-start | bytes 2359304 | tf_op jit(solution)/shard_map/ppermute | solution.py:26
  668.5 63.8 %collective-permute-start.19 = (f32[128,2,768]{0,2,1:T(8,128)}, f32[128,2,768]{0,2,1:T(8,128)S(1)}, u32[]{:S(2)}, u32[]{:S(2)}) collective-permute-start(f32[128,2,768]{0,2,1:T(8,128)} %get-tuple-element.102), channel_id=1, source_target_pairs={{2,0},{3,1},{4,2},{5,3},{6,4},{7,5},{10,8},{11,9},{12,10},{13,11},... | collective-permute-start | bytes 2359304 | tf_op jit(solution)/shard_map/ppermute | solution.py:26
  672.5 62.0 %collective-permute-start.20 = (f32[128,2,768]{0,2,1:T(8,128)}, f32[128,2,768]{0,2,1:T(8,128)}, u32[]{:S(2)}, u32[]{:S(2)}) collective-permute-start(f32[128,2,768]{0,2,1:T(8,128)} %get-tuple-element.103), channel_id=1, source_target_pairs={{1,0},{2,1},{3,2},{4,3},{5,4},{6,5},{7,6},{9,8},{10,9},{11,10},{12... | collective-permute-start | bytes 2359304 | tf_op jit(solution)/shard_map/ppermute | solution.py:26
  704.1 32.6 %collective-permute-start.21 = (f32[128,2,768]{0,2,1:T(8,128)}, f32[128,2,768]{0,2,1:T(8,128)}, u32[]{:S(2)}, u32[]{:S(2)}) collective-permute-start(f32[128,2,768]{0,2,1:T(8,128)} %get-tuple-element.104), channel_id=1, source_target_pairs={{0,1},{1,2},{2,3},{3,4},{4,5},{5,6},{6,7},{8,9},{9,10},{10,11},{11... | collective-permute-start | bytes 2359304 | tf_op jit(solution)/shard_map/ppermute | solution.py:26
  706.3 32.6 %collective-permute-start.22 = (f32[128,2,768]{0,2,1:T(8,128)}, f32[128,2,768]{0,2,1:T(8,128)}, u32[]{:S(2)}, u32[]{:S(2)}) collective-permute-start(f32[128,2,768]{0,2,1:T(8,128)} %get-tuple-element.105), channel_id=1, source_target_pairs={{0,2},{1,3},{2,4},{3,5},{4,6},{5,7},{8,10},{9,11},{10,12},{11,13},... | collective-permute-start | bytes 2359304 | tf_op jit(solution)/shard_map/ppermute | solution.py:26
  714.9 276.2 %reduce-scatter.2.cloned.1.call-start = ((), (), s32[]{:S(2)}) async-start(), calls=%async_computation.2 | async-start | bytes 9732096 | tf_op jit(solution)/shard_map/reduce_scatter | solution.py:967
  715.2 26.1 %copy-start.27 = (bf16[12,64,128]{2,1,0:T(8,128)(2,1)S(1)}, bf16[12,64,128]{2,1,0:T(8,128)(2,1)}, u32[]{:S(2)}) copy-start(bf16[12,64,128]{2,1,0:T(8,128)(2,1)} %copy-done.26) | copy-start | bytes 589828
  719.4 22.4 %copy-start.22 = (f32[128,2,768]{0,2,1:T(8,128)}, f32[128,2,768]{0,2,1:T(8,128)S(1)}, u32[]{:S(2)}) copy-start(f32[128,2,768]{0,2,1:T(8,128)S(1)} %collective-permute-done.18) | copy-start | bytes 2359300
  719.4 35.3 %collective-permute-start.23 = (f32[128,2,768]{0,2,1:T(8,128)}, f32[128,2,768]{0,2,1:T(8,128)}, u32[]{:S(2)}, u32[]{:S(2)}) collective-permute-start(f32[128,2,768]{0,2,1:T(8,128)} %get-tuple-element.106), channel_id=1, source_target_pairs={{0,3},{1,4},{2,5},{3,6},{4,7},{8,11},{9,12},{10,13},{11,14},{12,15... | collective-permute-start | bytes 2359304 | tf_op jit(solution)/shard_map/ppermute | solution.py:26
  732.3 26.2 %collective-permute-start.24 = (f32[128,2,768]{0,2,1:T(8,128)}, f32[128,2,768]{0,2,1:T(8,128)}, u32[]{:S(2)}, u32[]{:S(2)}) collective-permute-start(f32[128,2,768]{0,2,1:T(8,128)} %get-tuple-element.107), channel_id=1, source_target_pairs={{0,4},{1,5},{2,6},{3,7},{8,12},{9,13},{10,14},{11,15},{16,20},{17,... | collective-permute-start | bytes 2359304 | tf_op jit(solution)/shard_map/ppermute | solution.py:26
  734.5 40.9 %collective-permute-start.25 = (f32[128,2,768]{0,2,1:T(8,128)}, f32[128,2,768]{0,2,1:T(8,128)}, u32[]{:S(2)}, u32[]{:S(2)}) collective-permute-start(f32[128,2,768]{0,2,1:T(8,128)} %get-tuple-element.108), channel_id=1, source_target_pairs={{0,5},{1,6},{2,7},{8,13},{9,14},{10,15},{16,21},{17,22},{18,23},{2... | collective-permute-start | bytes 2359304 | tf_op jit(solution)/shard_map/ppermute | solution.py:26
  736.6 38.7 %collective-permute-start.26 = (f32[128,2,768]{0,2,1:T(8,128)}, f32[128,2,768]{0,2,1:T(8,128)}, u32[]{:S(2)}, u32[]{:S(2)}) collective-permute-start(f32[128,2,768]{0,2,1:T(8,128)} %get-tuple-element.110), channel_id=1, source_target_pairs={{0,6},{1,7},{8,14},{9,15},{16,22},{17,23},{24,30},{25,31}} | collective-permute-start | bytes 2359304 | tf_op jit(solution)/shard_map/ppermute | solution.py:26
  738.8 37.2 %collective-permute-start.27 = (f32[128,2,768]{0,2,1:T(8,128)}, f32[128,2,768]{0,2,1:T(8,128)}, u32[]{:S(2)}, u32[]{:S(2)}) collective-permute-start(f32[128,2,768]{0,2,1:T(8,128)} %get-tuple-element.109), channel_id=1, source_target_pairs={{0,7},{8,15},{16,23},{24,31}} | collective-permute-start | bytes 2359304 | tf_op jit(solution)/shard_map/ppermute | solution.py:26
  743.8 32.2 %slice-start.3 = ((s8[5898240]{0:T(1024)(128)(4,1)}), s8[1703936]{0:T(1024)(128)(4,1)S(1)}, s32[]{:S(2)}) async-start(s8[5898240]{0:T(1024)(128)(4,1)} %bitcast.128), calls=%async_computation.9 | async-start | bytes 3407872
  748.7 27.3 %slice-start.4 = ((s8[5898240]{0:T(1024)(128)(4,1)}), s8[4194304]{0:T(1024)(128)(4,1)S(1)}, s32[]{:S(2)}) async-start(s8[5898240]{0:T(1024)(128)(4,1)} %bitcast.128), calls=%async_computation.10 | async-start | bytes 8388608
  748.7 27.3 %copy-start.23 = (f32[128,2,768]{0,2,1:T(8,128)S(1)}, f32[128,2,768]{0,2,1:T(8,128)}, u32[]{:S(2)}) copy-start(f32[128,2,768]{0,2,1:T(8,128)} %copy-done.22) | copy-start | bytes 2359300
  748.7 27.3 %copy-start.25 = (f32[128,2,768]{0,2,1:T(8,128)S(1)}, f32[128,2,768]{0,2,1:T(8,128)}, u32[]{:S(2)}) copy-start(f32[128,2,768]{0,2,1:T(8,128)} %copy-done.24) | copy-start | bytes 2359300
  754.6 25.6 %copy-start.12 = (bf16[128,768]{1,0:T(8,128)(2,1)S(1)}, bf16[128,768]{1,0:T(8,128)(2,1)}, u32[]{:S(2)}) copy-start(bf16[128,768]{1,0:T(8,128)(2,1)} %param.14) | copy-start | bytes 589828
  754.6 25.6 %copy-start.31 = (f32[768]{0:T(1024)S(1)}, f32[768]{0:T(1024)}, u32[]{:S(2)}) copy-start(f32[768]{0:T(1024)} %param.15) | copy-start | bytes 9220
  754.6 25.6 %copy-start.38 = (f32[128]{0:T(128)S(1)}, f32[128]{0:T(128)}, u32[]{:S(2)}) copy-start(f32[128]{0:T(128)} %copy-done.37) | copy-start | bytes 1540
  864.9 77.1 %copy-start.14 = (f32[128,768]{1,0:T(8,128)S(1)}, f32[128,768]{1,0:T(8,128)}, u32[]{:S(2)}) copy-start(f32[128,768]{1,0:T(8,128)} %copy-done.13) | copy-start | bytes 1179652
  864.9 77.1 %copy-start.43 = (f32[128]{0:T(128)S(1)}, f32[128]{0:T(128)}, u32[]{:S(2)}) copy-start(f32[128]{0:T(128)} %get-tuple-element.160) | copy-start | bytes 1540
  (20 other events, 104.9 us)
Sparse Core Ops, SparseCore 0:
  11.5 66.3 all-gather.5
  337.1 30.8 all-gather.7
  715.1 132.2 all-reduce.3
  853.1 138.0 reduce-scatter.1

commit v2 on v1

--- a/solution.py
+++ b/solution.py
@@ -723,6 +723,596 @@
     )(rows, slot_row, slot_col, w1, w2)
 
 
+def nn(a, b):
+    return jnp.dot(a, b, preferred_element_type=f32)
+
+
+class Place:
+    def __init__(self):
+        self.gx, self.gy = lax.axis_index("gx"), lax.axis_index("gy")
+        self.core, self.chip = lax.rem(self.gy, 2), self.gy // 2
+        self.pair = (self.gx, self.gy + 1 - 2 * self.core)
+        self.line = [lax.rem(self.gx + k, 4) for k in (1, 2, 3)]
+        self.chips = [lax.rem(self.chip + k, 4) for k in (1, 2, 3)]
+        self.line_from = [lax.rem(self.gx + 4 - k, 4) for k in (1, 2, 3)]
+        self.chips_from = [lax.rem(self.chip + 4 - k, 4) for k in (1, 2, 3)]
+
+    def on_line(self, k):
+        return (self.line[k], self.gy)
+
+    def on_plane(self, k):
+        return (self.gx, 2 * self.chips[k] + self.core)
+
+    def greet_all(self):
+        greet([self.on_line(k) for k in range(3)] + [self.on_plane(k) for k in range(3)] + [self.pair])
+
+
+def near_buckets(rows):
+    offset = (
+        lax.broadcasted_iota(jnp.int32, (rows, 3 * rows), 1)
+        - rows
+        - lax.broadcasted_iota(jnp.int32, (rows, 3 * rows), 0)
+    )
+    return bucket_ids(offset)
+
+
+def fill_bias(bias_ref, table_ref, chip, heads):
+    rows = bias_ref.shape[1]
+    span = bias_ref.shape[2]
+    mid = span // 2
+    buckets = near_buckets(rows)
+    for h in range(heads):
+        column = chip * heads + h
+        near = jnp.zeros(buckets.shape, f32)
+        for b in range(table_ref.shape[0]):
+            near = jnp.where(buckets == b, table_ref[b, column], near)
+        bias_ref[h, :, 0:mid - rows] = jnp.full((rows, mid - rows), table_ref[15, column], f32)
+        bias_ref[h, :, mid - rows:mid + 2 * rows] = near
+        bias_ref[h, :, mid + 2 * rows:] = jnp.full((rows, span - mid - 2 * rows), table_ref[31, column], f32)
+
+
+def unit_scores(q_block, keys, bias_ref, h, block_at, allowed):
+    rows = q_block.shape[0]
+    seq = keys.shape[0]
+    lanes = lax.broadcasted_iota(jnp.int32, q_block.shape, 1) // HSIZE
+    masked = jnp.where(lanes == h, q_block, jnp.zeros_like(q_block))
+    start = pl.multiple_of(seq - rows * block_at, rows)
+    return jnp.where(allowed, nt(masked, keys) + bias_ref[h, :, pl.ds(start, seq)], -1000000000.0)
+
+
+def front_kernel(heads, experts,
+                 x_ref, gain1_ref, wqkv_ref, wout_ref, table_ref, small_ref, doc_row, doc_col, choice_ref, grad_ref,
+                 rows_ref, hidden_ref, normed_ref, router_ref, gate_ref, at_ref, q_ref, kv_ref, lse_ref, xn_ref,
+                 wqkv_all, wout_all, small_all, bias_ref,
+                 wq_st, wo_st, sm_st, at_in, rows_out,
+                 xn_s, xn_r, wq_s, wq_r, wqp_s, wqp_r, sm_s, sm_r, wo_s, wo_r, woc_s, woc_r, wop_s, wop_r,
+                 kv_s, kv_r, at_s, at_r, rz_s, rz_r, rc_s, rc_r, rp_s, rp_r):
+    me = Place()
+    gx, gy, core, chip = me.gx, me.gy, me.core, me.chip
+    width = wqkv_ref.shape[0]
+    cols = wqkv_ref.shape[1] // 3
+    local = x_ref.shape[0]
+    x = x_ref[...].astype(f32)
+    r1 = lax.rsqrt(jnp.mean(x * x, axis=-1, keepdims=True) + epsilon)
+    xn_ref[chip] = (x * r1 * gain1_ref[...]).astype(bf16)
+    me.greet_all()
+
+    def wq_line(k):
+        return remote(wqkv_ref, wq_st.at[core, gx], wq_s.at[k], wq_r.at[k], me.on_line(k))
+
+    def xn_plane(k):
+        return remote(xn_ref.at[chip], xn_ref.at[chip], xn_s.at[k], xn_r.at[k], me.on_plane(k))
+
+    def sm_line(k):
+        return remote(small_ref, sm_st.at[gx], sm_s.at[k], sm_r.at[k], me.on_line(k))
+
+    def wo_line(k):
+        return remote(wout_ref, wo_st.at[gy, gx], wo_s.at[k], wo_r.at[k], me.on_line(k))
+
+    def wq_pair(k):
+        src = wqkv_ref if k == 0 else wq_st.at[core, me.line_from[k - 1]]
+        z = gx if k == 0 else me.line_from[k - 1]
+        return remote(src, wq_st.at[core, z], wqp_s.at[k], wqp_r.at[k], me.pair)
+
+    def wo_plane(k):
+        return remote(wo_st.at[gy], wo_st.at[gy], woc_s.at[k], woc_r.at[k], me.on_plane(k))
+
+    def wo_pair(k):
+        c = chip if k == 0 else me.chips_from[k - 1]
+        return remote(wo_st.at[2 * c + core], wo_st.at[2 * c + core], wop_s.at[k], wop_r.at[k], me.pair)
+
+    for k in range(3):
+        wq_line(k).start()
+        xn_plane(k).start()
+    wq_pair(0).start()
+    for k in range(3):
+        wo_line(k).start()
+        sm_line(k).start()
+    wq_st[core, gx] = wqkv_ref[...]
+    wo_st[gy, gx] = wout_ref[...]
+    sm_st[gx] = small_ref[...]
+    fill_bias(bias_ref, table_ref, chip, heads)
+    for k in range(3):
+        wq_line(k).wait_recv()
+        wq_pair(k + 1).start()
+    for k in range(3):
+        wo_line(k).wait_recv()
+    for k in range(3):
+        wo_plane(k).start()
+    wo_pair(0).start()
+    for k in range(4):
+        wq_pair(k).wait_recv()
+    for z in range(4):
+        parts = [wq_st[0, z], wq_st[1, z]]
+        wqkv_all[z * width:(z + 1) * width, :] = jnp.concatenate(
+            [parts[j][:, n * cols:(n + 1) * cols] for n in range(3) for j in range(2)], axis=1)
+
+    def kv_pair(c):
+        return remote(kv_ref.at[2 * c + core], kv_ref.at[2 * c + core], kv_s.at[c], kv_r.at[c], me.pair)
+
+    scale = HSIZE ** (-0.5)
+    hd = 2 * cols
+    for k in range(4):
+        c = chip if k == 0 else me.chips_from[k - 1]
+        if k > 0:
+            xn_plane(k - 1).wait_recv()
+        made = nn(xn_ref[c], wqkv_all[...])
+        q_ref[c] = (made[:, :hd].astype(bf16).astype(f32) * scale).astype(bf16)
+        kv_ref[2 * c + core] = made[:, hd:].astype(bf16)
+        kv_pair(c).start()
+    for k in range(3):
+        wo_plane(k).wait_recv()
+        wo_pair(k + 1).start()
+    for c in range(4):
+        kv_pair(c).wait_recv()
+    seq = 8 * local
+    lanes = lax.broadcasted_iota(jnp.int32, (local, hd), 1) // HSIZE
+
+    def at_plane(k):
+        return remote(at_ref.at[me.chips[k]], at_in.at[chip], at_s.at[k], at_r.at[k], me.on_plane(k))
+
+    for k in range(4):
+        c = me.chips[k] if k < 3 else chip
+        block_at = 2 * c + core
+        allowed = doc_col[pl.ds(pl.multiple_of(block_at * local, local), local), :] == doc_row[...]
+        keys = kv_ref[:, :, :hd].reshape(seq, hd)
+        values = kv_ref[:, :, hd:].reshape(seq, hd)
+        total = jnp.zeros((local, hd), f32)
+        for h in range(heads):
+            scores = unit_scores(q_ref[c], keys, bias_ref, h, block_at, allowed)
+            peak = jnp.max(scores, axis=-1, keepdims=True)
+            shifted = jnp.exp(scores - peak)
+            summed = jnp.sum(shifted, axis=-1, keepdims=True)
+            lse_ref[c, h] = jnp.broadcast_to(peak + jnp.log(summed), (local, 128))
+            low = (shifted * (1.0 / summed)).astype(bf16)
+            total = jnp.where(lanes == h, nn(low, values), total)
+        at_ref[c] = total.astype(bf16)
+        if k < 3:
+            at_plane(k).start()
+        else:
+            at_in[chip] = total.astype(bf16)
+    for k in range(3):
+        sm_line(k).wait_recv()
+    small_all[...] = jnp.concatenate([sm_st[z] for z in range(4)], axis=1)
+    for k in range(4):
+        wo_pair(k).wait_recv()
+    for g in range(8):
+        wout_all[g * cols:(g + 1) * cols, :] = jnp.concatenate([wo_st[g, z] for z in range(4)], axis=1)
+    for k in range(3):
+        at_plane(k).wait_recv()
+    attended = jnp.concatenate([at_in[c] for c in range(4)], axis=1)
+    hidden = x + nn(attended, wout_all[...]).astype(bf16).astype(f32)
+    hidden_ref[...] = hidden
+    r2 = lax.rsqrt(jnp.mean(hidden * hidden, axis=-1, keepdims=True) + epsilon)
+    normed = hidden * r2 * small_all[experts:experts + 1, :]
+    normed_ref[...] = normed
+    logits = lax.dot_general(normed, small_all[:experts, :], (((1,), (1,)), ((), ())),
+                             precision=lax.Precision.HIGHEST, preferred_element_type=f32)
+    lifted = jnp.exp(logits - jnp.max(logits, axis=-1, keepdims=True))
+    router = lifted / jnp.sum(lifted, axis=-1, keepdims=True)
+    router_ref[...] = router
+    picked = choice_ref[...] == lax.broadcasted_iota(jnp.int32, router.shape, 1)
+    gate = jnp.sum(jnp.where(picked, router, 0.0), axis=-1, keepdims=True)
+    gate_ref[...] = gate
+    low = normed.astype(bf16)
+    route = (gate * grad_ref[...].astype(f32)).astype(bf16)
+    for z in range(4):
+        rows_out[z] = jnp.concatenate([low[:, z * width:(z + 1) * width], route[:, z * width:(z + 1) * width]], axis=1)
+
+    def rows_line(k):
+        return remote(rows_out.at[me.line[k]], rows_ref.at[gx * 8 + gy], rz_s.at[k], rz_r.at[k], me.on_line(k))
+
+    def rows_plane(z, k, m):
+        at = z * 8 + gy
+        return remote(rows_ref.at[at], rows_ref.at[at], rc_s.at[m, k], rc_r.at[m, k], me.on_plane(k))
+
+    def rows_pair(z, k, m):
+        c = chip if k == 0 else me.chips_from[k - 1]
+        at = z * 8 + 2 * c + core
+        return remote(rows_ref.at[at], rows_ref.at[at], rp_s.at[m, k], rp_r.at[m, k], me.pair)
+
+    for k in range(3):
+        rows_line(k).start()
+    rows_ref[gx * 8 + gy] = rows_out[gx]
+    zs = [gx] + me.line_from
+    for m in range(4):
+        if m > 0:
+            rows_line(m - 1).wait_recv()
+        for k in range(3):
+            rows_plane(zs[m], k, m).start()
+        rows_pair(zs[m], 0, m).start()
+    for m in range(4):
+        for k in range(3):
+            rows_plane(zs[m], k, m).wait_recv()
+            rows_pair(zs[m], k + 1, m).start()
+    for m in range(4):
+        for k in range(4):
+            rows_pair(zs[m], k, m).wait_recv()
+    for m in range(4):
+        for k in range(4):
+            rows_pair(zs[m], k, m).wait_send()
+        for k in range(3):
+            rows_plane(zs[m], k, m).wait_send()
+    for k in range(3):
+        rows_line(k).wait_send()
+        at_plane(k).wait_send()
+        wo_plane(k).wait_send()
+        wo_line(k).wait_send()
+        sm_line(k).wait_send()
+        wq_line(k).wait_send()
+        xn_plane(k).wait_send()
+    for k in range(4):
+        wq_pair(k).wait_send()
+        wo_pair(k).wait_send()
+        kv_pair(k).wait_send()
+
+
+def front(x_in, gain1, wqkv, wout, table, small, doc_row, doc_col, choice, grad_out, collective_id):
+    local, features = x_in.shape
+    width = wqkv.shape[0]
+    cols = wqkv.shape[1] // 3
+    hd = 2 * cols
+    heads = hd // HSIZE
+    experts = table.shape[0] if False else EXPERTS
+    tokens = 32 * local
+    vm = pl.BlockSpec(memory_space=pltpu.VMEM)
+    sm = pl.BlockSpec(memory_space=pltpu.SMEM)
+    dma = pltpu.SemaphoreType.DMA
+    shape = jax.ShapeDtypeStruct
+    return pl.pallas_call(
+        functools.partial(front_kernel, heads, experts),
+        out_shape=(
+            shape((32, local, 2 * width), bf16),
+            shape((local, features), f32),
+            shape((local, features), f32),
+            shape((local, experts), f32),
+            shape((local, 1), f32),
+            shape((4, local, hd), bf16),
+            shape((4, local, hd), bf16),
+            shape((8, local, 2 * hd), bf16),
+            shape((4, heads, local, 128), f32),
+            shape((4, local, features), bf16),
+            shape((features, 3 * hd), bf16),
+            shape((features, features), bf16),
+            shape((small.shape[0], features), f32),
+            shape((heads, local, 16 * local), f32),
+        ),
+        in_specs=[vm, vm, vm, vm, sm, vm, vm, vm, vm, vm],
+        out_specs=(vm,) * 14,
+        scratch_shapes=[
+            pltpu.VMEM((2, 4, width, 3 * cols), bf16),
+            pltpu.VMEM((8, 4, cols, width), bf16),
+            pltpu.VMEM((4, *small.shape), f32),
+            pltpu.VMEM((4, local, hd), bf16),
+            pltpu.VMEM((4, local, 2 * width), bf16),
+        ] + [dma((n,)) for n in (3, 3, 3, 3, 4, 4, 3, 3, 3, 3, 3, 3, 4, 4, 4, 4, 3, 3, 3, 3)]
+        + [dma((4, 3)), dma((4, 3)), dma((4, 4)), dma((4, 4))],
+        compiler_params=pltpu.CompilerParams(
+            collective_id=collective_id, has_side_effects=True, vmem_limit_bytes=60 * 2**20),
+        cost_estimate=pl.CostEstimate(flops=4 * 10**9, bytes_accessed=20 * 10**6, transcendentals=2 * 10**6),
+    )(x_in, gain1, wqkv, wout, table, small, doc_row, doc_col, choice, grad_out)
+
+
+HIGH = lax.Precision.HIGHEST
+
+
+def back_kernel(heads, experts,
+                x_ref, gain1_ref, grad_ref, choice_ref, doc_row, doc_col,
+                hidden_ref, normed_ref, router_ref, gate_ref, at_ref, q_ref, kv_ref, lse_ref, xn_ref,
+                wqkv_all, wout_all, small_all, bias_ref, ret_ref,
+                out_ref, gin_ref, wgrad_ref, ograd_ref, small_out, tail_out,
+                ag_ref, dq_ref, dk_ref, dv_ref, near_ref, go_ref, fg_ref, top_ref,
+                sp_out, sp_in, sc_out, sc_in, sz_out, sz_in,
+                kv_out, kv_in, kv_sum, fg_out, fg_in, wp_out, wp_in, wz_out, wz_in,
+                op_out, op_in, oz_out, oz_in, tp_out, tp_in, tc_out, tc_in, tz_out, tz_in,
+                ag_s, ag_r, sp_s, sp_r, sc_s, sc_r, sz_s, sz_r, kv_s, kv_r, fg_s, fg_r, wp_s, wp_r,
+                wz_s, wz_r, op_s, op_r, oz_s, oz_r, tp_s, tp_r, tc_s, tc_r, tz_s, tz_r):
+    me = Place()
+    gx, gy, core, chip = me.gx, me.gy, me.core, me.chip
+    local, features = x_ref.shape
+    width = features // 4
+    hd = q_ref.shape[2]
+    cols = hd // 2
+    seq = 8 * local
+    hidden = hidden_ref[...]
+    r2 = lax.rsqrt(jnp.mean(hidden * hidden, axis=-1, keepdims=True) + epsilon)
+    grads = grad_ref[...].astype(f32)
+    gate = gate_ref[...]
+    routed = jnp.concatenate([ret_ref[z][:, :width] for z in range(4)], axis=1)
+    back = jnp.concatenate([ret_ref[z][:, width:] for z in range(4)], axis=1)
+    out_ref[...] = hidden + gate * routed
+    gate_grad = jnp.sum(grads * routed, axis=-1, keepdims=True)
+    router = router_ref[...]
+    picked = (choice_ref[...] == lax.broadcasted_iota(jnp.int32, router.shape, 1)).astype(f32)
+    logit_grad = router * (gate_grad * picked - gate * gate_grad)
+    second = back + jnp.dot(logit_grad, small_all[:experts, :], precision=HIGH, preferred_element_type=f32)
+    gained = second * small_all[experts:experts + 1, :]
+    dot2 = jnp.sum(gained * hidden, axis=-1, keepdims=True)
+    hidden_grad = grads + r2 * gained - hidden * (r2 * r2 * r2) * (dot2 / features)
+    ag_ref[chip] = hidden_grad.astype(bf16)
+    me.greet_all()
+
+    def ag_plane(k):
+        return remote(ag_ref.at[chip], ag_ref.at[chip], ag_s.at[k], ag_r.at[k], me.on_plane(k))
+
+    for k in range(3):
+        ag_plane(k).start()
+
+    routed_grad = lax.dot_general(logit_grad, normed_ref[...], (((0,), (0,)), ((), ())), precision=HIGH,
+                                  preferred_element_type=f32)
+    norm2 = jnp.sum(second * hidden * r2, axis=0, keepdims=True)
+    own_small = jnp.concatenate([routed_grad, norm2, jnp.zeros((7, features), f32)], axis=0)
+    sp_out[...] = own_small
+    small_pair = remote(sp_out, sp_in, sp_s.at[0], sp_r.at[0], me.pair)
+    small_pair.start()
+
+    def small_plane(k):
+        return remote(sc_out, sc_in.at[k], sc_s.at[k], sc_r.at[k], me.on_plane(k))
+
+    def small_line(k):
+        return remote(sz_out.at[me.line[k]], sz_in.at[k], sz_s.at[k], sz_r.at[k], me.on_line(k))
+
+    dk_ref[...] = jnp.zeros_like(dk_ref)
+    dv_ref[...] = jnp.zeros_like(dv_ref)
+    near_ref[...] = jnp.zeros_like(near_ref)
+    go_ref[...] = jnp.zeros_like(go_ref)
+    scale = HSIZE ** (-0.5)
+    lanes = lax.broadcasted_iota(jnp.int32, (local, hd), 1) // HSIZE
+
+    def attend_block(c):
+        block_at = 2 * c + core
+        allowed = doc_col[pl.ds(pl.multiple_of(block_at * local, local), local), :] == doc_row[...]
+        keys = kv_ref[:, :, :hd].reshape(seq, hd)
+        values = kv_ref[:, :, hd:].reshape(seq, hd)
+        rows_out = pl.ds(pl.multiple_of(chip * hd, 16), hd)
+        att_grad = nt(ag_ref[c], wout_all[rows_out, :]).astype(bf16)
+        go_ref[...] += tn(at_ref[c], ag_ref[c])
+        q_block = q_ref[c]
+        q_turn = jnp.transpose(q_block.astype(f32)).astype(bf16)
+        g_turn = jnp.transpose(att_grad.astype(f32)).astype(bf16)
+        dq = jnp.zeros((local, hd), f32)
+        for h in range(heads):
+            scores = unit_scores(q_block, keys, bias_ref, h, block_at, allowed)
+            probs = jnp.exp(scores - lse_ref[c, h][:, :1])
+            masked = jnp.where(lanes == h, att_grad, jnp.zeros_like(att_grad))
+            prob_grad = nt(masked, values)
+            weighted = probs * prob_grad
+            score_grad = (weighted - probs * jnp.sum(weighted, axis=-1, keepdims=True)).astype(bf16)
+            part = slice(h * HSIZE, (h + 1) * HSIZE)
+            dv_ref[part, :] += nn(g_turn[part, :], probs.astype(bf16))
+            dk_ref[part, :] += nn(q_turn[part, :], score_grad)
+            dq = jnp.where(lanes == h, nn(score_grad, keys), dq)
+            start = pl.multiple_of(seq - local * block_at, local)
+            near_ref[h, :, pl.ds(start, seq)] += score_grad.astype(f32)
+        dq_ref[c] = (dq * scale).astype(bf16)
+
+    attend_block(chip)
+    small_pair.wait_recv()
+    sc_out[...] = own_small + sp_in[...]
+    for k in range(3):
+        small_plane(k).start()
+    for k in range(3):
+        ag_plane(k).wait_recv()
+        attend_block(me.chips_from[k])
+        if k == 0:
+            total = sc_out[...]
+            for j in range(3):
+                small_plane(j).wait_recv()
+                total = total + sc_in[j]
+            for z in range(4):
+                sz_out[z] = total[:, z * width:(z + 1) * width]
+            for j in range(3):
+                small_line(j).start()
+
+    both = jnp.concatenate([dk_ref[...], dv_ref[...]], axis=0)
+    for j in range(8):
+        turned = jnp.transpose(both[:, j * local:(j + 1) * local])
+        @pl.when(core == j % 2)
+        def _():
+            kv_sum[j // 2] = turned
+        @pl.when(core != j % 2)
+        def _():
+            kv_out[j // 2] = turned.astype(bf16)
+    kv_pair = remote(kv_out, kv_in, kv_s.at[0], kv_r.at[0], me.pair)
+    kv_pair.start()
+
+    op_out[...] = go_ref[pl.ds(pl.multiple_of((1 - core) * cols, 16), cols), :].astype(bf16)
+    op_pair = remote(op_out, op_in, op_s.at[0], op_r.at[0], me.pair)
+    op_pair.start()
+
+    def op_line(k):
+        return remote(oz_out.at[me.line[k]], oz_in.at[k], oz_s.at[k], oz_r.at[k], me.on_line(k))
+
+    buckets = near_buckets(local)
+    table = jnp.zeros((experts, 128), f32)
+    lane = lax.broadcasted_iota(jnp.int32, (experts, 128), 1)
+    row = lax.broadcasted_iota(jnp.int32, (experts, 1), 0)
+    for h in range(heads):
+        close = near_ref[h, :, seq - local:seq + 2 * local]
+        for b in range(experts):
+            top_ref[b:b + 1, :] = jnp.sum(jnp.where(buckets == b, close, 0.0), axis=0, keepdims=True)
+        column = jnp.sum(top_ref[...], axis=1, keepdims=True)
+        left = jnp.sum(near_ref[h, :, :seq - local])
+        right = jnp.sum(near_ref[h, :, seq + 2 * local:])
+        column = column + jnp.where(row == 15, left, 0.0) + jnp.where(row == 31, right, 0.0)
+        table = jnp.where(lane == chip * heads + h, column, table)
+
+    kv_pair.wait_recv()
+    made = []
+    for c in range(4):
+        keyval = (kv_sum[c] + kv_in[c].astype(f32)).astype(bf16)
+        made.append(jnp.concatenate([dq_ref[c], keyval], axis=1))
+
+    def fg_plane(k):
+        return remote(fg_out.at[me.chips[k]], fg_in.at[k], fg_s.at[k], fg_r.at[k], me.on_plane(k))
+
+    for c in range(4):
+        fg_ref[c] = nt(made[c], wqkv_all[...])
+        fg_out[c] = fg_ref[c].astype(bf16)
+    for k in range(3):
+        fg_plane(k).start()
+    weight_grad = jnp.zeros((features, 3 * hd), f32)
+    weight_grad = tn(xn_ref[...].reshape(4 * local, features), jnp.concatenate(made, axis=0))
+    halves = [jnp.concatenate([weight_grad[:, n * hd + j * cols:n * hd + (j + 1) * cols] for n in range(3)], axis=1)
+              for j in range(2)]
+    wp_out[...] = jnp.where(core == 0, halves[1], halves[0]).astype(bf16)
+    w_pair = remote(wp_out, wp_in, wp_s.at[0], wp_r.at[0], me.pair)
+    w_pair.start()
+    own_w = jnp.where(core == 0, halves[0], halves[1])
+
+    def w_line(k):
+        return remote(wz_out.at[me.line[k]], wz_in.at[k], wz_s.at[k], wz_r.at[k], me.on_line(k))
+
+    op_pair.wait_recv()
+    own_o = go_ref[pl.ds(pl.multiple_of(core * cols, 16), cols), :] + op_in[...].astype(f32)
+    for z in range(4):
+        oz_out[z] = own_o[:, z * width:(z + 1) * width].astype(bf16)
+    for k in range(3):
+        op_line(k).start()
+    w_pair.wait_recv()
+    own_w = own_w + wp_in[...].astype(f32)
+    for z in range(4):
+        wz_out[z] = own_w[z * width:(z + 1) * width, :].astype(bf16)
+    for k in range(3):
+        w_line(k).start()
+
+    first = fg_ref[chip]
+    for k in range(3):
+        fg_plane(k).wait_recv()
+        first = first + fg_in[k].astype(f32)
+    x = x_ref[...].astype(f32)
+    r1 = lax.rsqrt(jnp.mean(x * x, axis=-1, keepdims=True) + epsilon)
+    norm1 = jnp.sum(first * x * r1, axis=0, keepdims=True)
+    gained1 = first * gain1_ref[...]
+    dot1 = jnp.sum(gained1 * x, axis=-1, keepdims=True)
+    gin_ref[...] = hidden_grad + r1 * gained1 - x * (r1 * r1 * r1) * (dot1 / features)
+
+    tail = jnp.concatenate([table] + [norm1[:, n * 128:(n + 1) * 128] for n in range(6)] + [jnp.zeros((2, 128), f32)],
+                           axis=0)
+    tp_out[...] = tail
+    t_pair = remote(tp_out, tp_in, tp_s.at[0], tp_r.at[0], me.pair)
+    t_pair.start()
+
+    def t_plane(k):
+        return remote(tc_out, tc_in.at[k], tc_s.at[k], tc_r.at[k], me.on_plane(k))
+
+    def t_line(k):
+        return remote(tz_out, tz_in.at[k], tz_s.at[k], tz_r.at[k], me.on_line(k))
+
+    t_pair.wait_recv()
+    tail = jnp.where(core == 0, tail + tp_in[...], tp_in[...] + tail)
+    tc_out[...] = tail
+    for k in range(3):
+        t_plane(k).start()
+    for k in range(3):
+        t_plane(k).wait_recv()
+    tail = jnp.zeros_like(tail)
+    for c in range(4):
+        part = jnp.where(chip == c, tc_out[...], 0.0)
+        for k in range(3):
+            part = jnp.where(me.chips_from[k] == c, tc_in[k], part)
+        tail = tail + part
+    tz_out[...] = tail
+    for k in range(3):
+        t_line(k).start()
+
+    total = sz_out[gx]
+    for k in range(3):
+        small_line(k).wait_recv()
+        total = total + sz_in[k]
+    small_out[...] = total
+    total = oz_out[gx].astype(f32)
+    for k in range(3):
+        op_line(k).wait_recv()
+        total = total + oz_in[k].astype(f32)
+    ograd_ref[...] = total
+    total = wz_out[gx].astype(f32)
+    for k in range(3):
+        w_line(k).wait_recv()
+        total = total + wz_in[k].astype(f32)
+    wgrad_ref[...] = total
+    for k in range(3):
+        t_line(k).wait_recv()
+    tail = jnp.zeros_like(tail)
+    for z in range(4):
+        part = jnp.where(gx == z, tz_out[...], 0.0)
+        for k in range(3):
+            part = jnp.where(me.line_from[k] == z, tz_in[k], part)
+        tail = tail + part
+    tail_out[...] = tail
+    for copy in (small_pair, kv_pair, op_pair, w_pair, t_pair):
+        copy.wait_send()
+    for k in range(3):
+        for copy in (ag_plane, small_plane, small_line, fg_plane, op_line, w_line, t_plane, t_line):
+            copy(k).wait_send()
+
+
+def back_pass(x_in, gain1, grad_out, choice, doc_row, doc_col, saved, returned, collective_id):
+    local, features = x_in.shape
+    width = features // 4
+    hidden, normed, router, gate, attended, queries, keyvals, lse, xn, wqkv, wout, small, bias = saved
+    hd = queries.shape[2]
+    cols = hd // 2
+    heads = hd // HSIZE
+    seq = 8 * local
+    rows = small.shape[0]
+    vm = pl.BlockSpec(memory_space=pltpu.VMEM)
+    dma = pltpu.SemaphoreType.DMA
+    shape = jax.ShapeDtypeStruct
+    V = pltpu.VMEM
+    return pl.pallas_call(
+        functools.partial(back_kernel, heads, EXPERTS),
+        out_shape=(
+            shape((local, features), f32),
+            shape((local, features), f32),
+            shape((width, 3 * cols), f32),
+            shape((cols, width), f32),
+            shape((rows, width), f32),
+            shape((40, 128), f32),
+        ),
+        in_specs=[vm] * 20,
+        out_specs=(vm,) * 6,
+        scratch_shapes=[
+            V((4, local, features), bf16), V((4, local, hd), bf16), V((hd, seq), f32), V((hd, seq), f32),
+            V((heads, local, 2 * seq), f32), V((hd, features), f32), V((4, local, features), f32),
+            V((EXPERTS, 3 * local), f32),
+            V((rows, features), f32), V((rows, features), f32), V((rows, features), f32), V((3, rows, features), f32),
+            V((4, rows, width), f32), V((3, rows, width), f32),
+            V((4, local, 2 * hd), bf16), V((4, local, 2 * hd), bf16), V((4, local, 2 * hd), f32),
+            V((4, local, features), bf16), V((3, local, features), bf16),
+            V((features, 3 * cols), bf16), V((features, 3 * cols), bf16),
+            V((4, width, 3 * cols), bf16), V((3, width, 3 * cols), bf16),
+            V((cols, features), bf16), V((cols, features), bf16), V((4, cols, width), bf16), V((3, cols, width), bf16),
+            V((40, 128), f32), V((40, 128), f32), V((40, 128), f32), V((3, 40, 128), f32),
+            V((40, 128), f32), V((3, 40, 128), f32),
+        ] + [dma((n,)) for n in (3, 3, 1, 1, 3, 3, 3, 3, 1, 1, 3, 3, 1, 1, 3, 3, 1, 1, 3, 3, 1, 1, 3, 3, 3, 3)],
+        compiler_params=pltpu.CompilerParams(
+            collective_id=collective_id, has_side_effects=True, vmem_limit_bytes=60 * 2**20),
+        cost_estimate=pl.CostEstimate(flops=6 * 10**9, bytes_accessed=20 * 10**6, transcendentals=2 * 10**6),
+    )(x_in, gain1, grad_out, choice, doc_row, doc_col, hidden, normed, router, gate, attended, queries, keyvals, lse, xn,
+      wqkv, wout, small, bias, returned)
+
+
 def fits(mesh):
     return mesh.shape["gx"] == 4 and mesh.shape["gy"] == 8
 
@@ -759,225 +1349,63 @@
     grad_out,
 ):
     token_devs = lax.axis_size("gy")
-    width_devs = lax.axis_size("gx")
-    member = lax.axis_index("gy")
-    column = lax.axis_index("gx")
+    member, column = lax.axis_index("gy"), lax.axis_index("gx")
     local_count = x_in.shape[0]
-    width_cols = w_router.shape[0]
-    own_rows = local_count * width_devs
-    all_tokens = own_rows * token_devs
-    seq_len = local_count * token_devs
-    experts = EXPERTS
+    width_cols, experts = w_router.shape
+    all_tokens = expert_choice.shape[0]
     capacity = all_tokens * 5 // (4 * experts)
-    score_scale = HSIZE ** (-0.5)
-    reach = min((WINDOW + local_count - 2) // local_count, token_devs - 1)
-    key_count = (2 * reach + 1) * local_count
-    all_weights = lax.all_gather(
-        jnp.concatenate([w_query, w_key, w_value, w_out.reshape(w_query.shape)], axis=1)[None],
-        ("gx", "gy"),
-        axis=0,
-        tiled=True,
-    )
     head_cols = w_query.shape[1]
-    qkv_full = jnp.concatenate(
-        [
-            rows_cols(all_weights[:, :, k * head_cols : (k + 1) * head_cols], width_devs, token_devs)
-            for k in range(3)
-        ],
-        axis=1,
-    )
-    out_full = cols_rows(
-        all_weights[:, :, 3 * head_cols :].reshape(-1, *w_out.shape), width_devs, token_devs
-    )
-    head_width = out_full.shape[0]
-    inputs_row = x_in.astype(jnp.float32)
-    scale_first = lax.rsqrt(jnp.mean(inputs_row * inputs_row, axis=-1, keepdims=True) + epsilon)
-    normed_first = (inputs_row * scale_first * norm1_gain).astype(jnp.bfloat16)
-    qkv_rows = jnp.dot(normed_first, qkv_full, preferred_element_type=jnp.float32).astype(
-        jnp.bfloat16
-    )
-    query_heads = qkv_rows[:, :head_width].reshape(local_count, HEADS, HSIZE)
-    pair_window = collect_window(
-        qkv_rows[:, head_width:].reshape(local_count, 2, head_width), reach
-    )
-    key_heads = pair_window[:, 0].reshape(key_count, HEADS, HSIZE)
-    value_heads = pair_window[:, 1].reshape(key_count, HEADS, HSIZE)
-    query_pos = member * local_count + jnp.arange(local_count, dtype=jnp.int32)
-    key_pos = (member - reach) * local_count + jnp.arange(key_count, dtype=jnp.int32)
-    offset = key_pos[None, :] - query_pos[:, None]
-    buckets = bucket_ids(offset)
-    bias_terms = sum(
-        jnp.where(buckets[None] == b, relative_bias_table[b][:, None, None], 0.0)
-        for b in range(relative_bias_table.shape[0])
-    )
-    no_doc = jnp.full((reach * local_count,), -1, jnp.int32)
-    doc_padded = jnp.concatenate([no_doc, doc_ids, no_doc], axis=0)
-    key_docs = lax.dynamic_slice_in_dim(doc_padded, member * local_count, key_count, 0)
-    query_docs = lax.dynamic_slice_in_dim(doc_ids, member * local_count, local_count, 0)
-    allowed = (jnp.abs(offset) < WINDOW) & (query_docs[:, None] == key_docs[None, :])
-    attention_scores = head_scores(query_heads, key_heads, bias_terms, allowed, score_scale)
-    row_peak = jnp.max(attention_scores, axis=-1, keepdims=True)
-    shifted = jnp.exp(attention_scores - row_peak)
-    row_sum = jnp.sum(shifted, axis=-1, keepdims=True)
-    log_total = row_peak + jnp.log(row_sum)
-    weights_reduced_precision = (shifted / row_sum).astype(jnp.bfloat16)
-    attended = jnp.einsum(
-        "hqk,khd->qhd", weights_reduced_precision, value_heads, preferred_element_type=jnp.float32
-    )
-    attended_low = attended.reshape(local_count, head_width).astype(jnp.bfloat16)
-    attn_low = jnp.dot(attended_low, out_full, preferred_element_type=jnp.float32).astype(
-        jnp.bfloat16
-    )
-
-    hidden_first = inputs_row + attn_low.astype(jnp.float32)
-    grad_rows = grad_out.astype(jnp.float32)
-    scale_second = lax.rsqrt(
-        jnp.mean(hidden_first * hidden_first, axis=-1, keepdims=True) + epsilon
-    )
-    gain_second = lax.all_gather(norm2_gain, "gx", axis=0, tiled=True)
-    router_full = lax.all_gather(w_router, "gx", axis=0, tiled=True)
-    normed_second = hidden_first * scale_second * gain_second
-    logits = jnp.dot(normed_second, router_full, precision=highest)
-    router = jax.nn.softmax(logits, axis=-1)
+    gain_row = norm1_gain[None, :]
+    wqkv = jnp.concatenate([w_query, w_key, w_value], axis=1)
+    small = jnp.concatenate(
+        [w_router.T, norm2_gain[None, :], jnp.zeros((7, width_cols), jnp.float32)], axis=0
+    )
     own_choice = lax.dynamic_slice_in_dim(
         expert_choice, (column * token_devs + member) * local_count, local_count, 0
-    )
-    picked = (own_choice[:, None] == jnp.arange(experts, dtype=jnp.int32)[None, :]).astype(
-        jnp.float32
-    )
-    gate_value = jnp.sum(picked * router, axis=-1, keepdims=True)
+    )[:, None]
+    doc_row, doc_col = doc_ids[None, :], doc_ids[:, None]
     slot_all = expert_slots(expert_choice, experts, capacity)
-    pair_rows = jnp.stack(
-        [normed_second.astype(jnp.bfloat16), (grad_rows * gate_value).astype(jnp.bfloat16)], axis=1
-    ).reshape(local_count, 2, width_devs, width_cols)
-    pair_rows = jnp.transpose(pair_rows, (2, 0, 1, 3)).reshape(
-        width_devs, local_count, 2 * width_cols
-    )
-    moved = lax.all_to_all(pair_rows, "gx", split_axis=0, concat_axis=0, tiled=True)
-    everyone = lax.all_gather(moved[:, None], "gy", axis=1, tiled=True)
-    dispatch_rows = everyone.reshape(all_tokens, 2 * width_cols)
     hidden_weight = jnp.transpose(w_hidden.reshape(width_cols, -1, experts), (2, 0, 1))
     back_weight = jnp.transpose(w_back.reshape(width_cols, -1, experts), (2, 0, 1))
+    rows, *saved = front(
+        x_in,
+        gain_row,
+        wqkv,
+        w_out,
+        relative_bias_table,
+        small,
+        doc_row,
+        doc_col,
+        own_choice,
+        grad_out,
+        2,
+    )
     returned, hidden_grads, back_grads = moe(
-        dispatch_rows, slot_all[None, :], slot_all[:, None], hidden_weight, back_weight, 1
+        rows.reshape(all_tokens, 2 * width_cols),
+        slot_all[None, :],
+        slot_all[:, None],
+        hidden_weight,
+        back_weight,
+        1,
     )
     grad_hidden = jnp.transpose(hidden_grads, (1, 2, 0)).reshape(width_cols, -1)
     grad_back = jnp.transpose(back_grads, (1, 2, 0)).reshape(width_cols, -1)
-    returned = jnp.transpose(
-        returned.reshape(width_devs, local_count, 2, width_cols), (2, 1, 0, 3)
-    ).reshape(2, local_count, width_devs * width_cols)
-    routed, back_routed = returned[0], returned[1]
-    out_rows = hidden_first + gate_value * routed
-    gate_grad = jnp.sum(grad_rows * routed, axis=-1, keepdims=True)
-    logit_grad = router * (gate_grad * picked - gate_value * gate_grad)
-    second_grad = back_routed + jnp.einsum("re,de->rd", logit_grad, router_full, precision=highest)
-    router_part = jnp.einsum("rd,re->de", normed_second, logit_grad, precision=highest)
-    norm2_part = jnp.sum(second_grad * hidden_first * scale_second, axis=0)
-    gained_second = second_grad * gain_second
-    row_dot_second = jnp.sum(gained_second * hidden_first, axis=-1, keepdims=True)
-    hidden_rows = (
-        grad_rows
-        + scale_second * gained_second
-        - hidden_first * scale_second**3 * row_dot_second / D
-    )
-    attn_grad = hidden_rows.astype(jnp.bfloat16)
-    grad_out_full = jnp.einsum(
-        "rf,rd->fd", attended_low, attn_grad, preferred_element_type=jnp.float32
-    )
-    attended_grad = (
-        jnp.einsum("rd,fd->rf", attn_grad, out_full, preferred_element_type=jnp.float32)
-        .astype(jnp.bfloat16)
-        .reshape(local_count, HEADS, HSIZE)
-    )
-    scores_again = head_scores(query_heads, key_heads, bias_terms, allowed, score_scale)
-    probs_again = jnp.exp(scores_again - log_total)
-    value_grad = jnp.einsum(
-        "hqk,qhd->khd",
-        probs_again.astype(jnp.bfloat16),
-        attended_grad,
-        preferred_element_type=jnp.float32,
-    )
-    prob_grad = jnp.einsum(
-        "qhd,khd->hqk", attended_grad, value_heads, preferred_element_type=jnp.float32
-    )
-    score_gradient = (
-        probs_again * (prob_grad - jnp.sum(probs_again * prob_grad, axis=-1, keepdims=True))
-    ).astype(jnp.bfloat16)
-    query_grad = (
-        jnp.einsum("hqk,khd->qhd", score_gradient, key_heads, preferred_element_type=jnp.float32)
-        * score_scale
-    ).astype(jnp.bfloat16)
-    key_grad = (
-        jnp.einsum("hqk,qhd->khd", score_gradient, query_heads, preferred_element_type=jnp.float32)
-        * score_scale
-    )
-    band_low = max(0, reach * local_count - 90)
-    band_high = min(key_count, reach * local_count + local_count + 90)
-    bucket_iota = jnp.arange(relative_bias_table.shape[0], dtype=jnp.int32)
-    band_onehot = (buckets[None, :, band_low:band_high] == bucket_iota[:, None, None]).astype(
-        jnp.bfloat16
-    )
-    table_near = jnp.einsum(
-        "ivt,zvt->zi",
-        score_gradient[:, :, band_low:band_high],
-        band_onehot,
-        preferred_element_type=jnp.float32,
-    )
-    left_far = jnp.sum(score_gradient[:, :, :band_low].astype(jnp.float32), axis=(1, 2))
-    right_far = jnp.sum(score_gradient[:, :, band_high:].astype(jnp.float32), axis=(1, 2))
-    table_part = (
-        table_near
-        + (bucket_iota == 15).astype(jnp.float32)[:, None] * left_far[None, :]
-        + (bucket_iota == 31).astype(jnp.float32)[:, None] * right_far[None, :]
-    )
-    pair_grads = return_window(
-        jnp.stack(
-            [key_grad.reshape(key_count, head_width), value_grad.reshape(key_count, head_width)],
-            axis=1,
-        ),
-        reach,
-        local_count,
-    )
-    qkv_grad = jnp.concatenate(
-        [
-            query_grad.reshape(local_count, head_width),
-            pair_grads.astype(jnp.bfloat16).reshape(local_count, 2 * head_width),
-        ],
-        axis=1,
-    )
-    qkv_grads = jnp.einsum("rd,rc->dc", normed_first, qkv_grad, preferred_element_type=jnp.float32)
-    first_grad = jnp.einsum("rc,dc->rd", qkv_grad, qkv_full, preferred_element_type=jnp.float32)
-    norm1_part = jnp.sum(first_grad * inputs_row * scale_first, axis=0)
-    gained_first = first_grad * norm1_gain
-    row_dot_first = jnp.sum(gained_first * inputs_row, axis=-1, keepdims=True)
-    input_rows = (
-        hidden_rows + scale_first * gained_first - inputs_row * scale_first**3 * row_dot_first / D
-    )
-    summed = lax.psum((norm1_part, table_part, norm2_part, router_part), ("gx", "gy"))
-    grad_norm2 = lax.dynamic_slice_in_dim(summed[2], column * width_cols, width_cols, 0)
-    grad_router = lax.dynamic_slice_in_dim(summed[3], column * width_cols, width_cols, 0)
-    weight_blocks = jnp.concatenate(
-        [
-            grid_rows_cols(qkv_grads[:, k * head_width : (k + 1) * head_width], width_devs, token_devs)
-            for k in range(3)
-        ]
-        + [grid_cols_rows(grad_out_full, width_devs, token_devs).reshape(-1, *w_query.shape)],
-        axis=2,
-    )
-    weight_part = lax.psum_scatter(
-        weight_blocks, ("gx", "gy"), scatter_dimension=0, tiled=True
-    )[0]
+    out_rows, input_rows, weight_part, out_part, small_part, tail = back_pass(
+        x_in, gain_row, grad_out, own_choice, doc_row, doc_col, saved, returned, 3
+    )
+    heads = relative_bias_table.shape[1]
+    features = x_in.shape[1]
     return (
         out_rows,
         input_rows,
-        summed[0],
+        tail[experts : experts + features // 128].reshape(features),
         weight_part[:, :head_cols],
         weight_part[:, head_cols : 2 * head_cols],
-        weight_part[:, 2 * head_cols : 3 * head_cols],
-        summed[1],
-        weight_part[:, 3 * head_cols :].reshape(w_out.shape),
-        grad_norm2,
-        grad_router,
+        weight_part[:, 2 * head_cols :],
+        tail[:experts, :heads],
+        out_part,
+        small_part[experts],
+        small_part[:experts].T,
         grad_hidden,
         grad_back,
     )

time: 1010 us -> 469 us (0.46)
  waiting for transfers between devices: 212 us -> 0 us
  Pallas kernels: 231 us -> 360 us
  local copies, waits for them, and re-layouts: 219 us -> 99.2 us
  blocking collectives: 102 us -> 0 us
  matrix products: 98 us -> 0.94 us
  starting transfers between devices: 64.8 us -> 0 us
  other arithmetic: 58.5 us -> 5.55 us
  between operations: 16.1 us -> 0.71 us
    pallas_call x0 -> x2, Pallas kernels: none -> 127 us  [the longest x1 71.3 us: front(): pl.pallas_call(functools.partial(front_kernel, heads, experts), out_shape...]
    ppermute x28 -> x0, waiting for transfers between devices: 100 us -> none  [passed_along(): lax.ppermute(value, axis, [(source, source + steps) for source in range(f...]
    dot_general x16 -> x0, matrix products: 97.7 us -> none  [the longest x1 57.8 us: head_scores(): jnp.einsum('qhd,khd->hqk', query_heads, key_heads, preferred_element_type...]
    psum x1 -> x0, blocking collectives: 65.8 us -> none  [fast(): lax.psum((norm1_part, table_part, norm2_part, router_part), ('gx', 'gy'))]
    ppermute x28 -> x0, starting transfers between devices: 64.6 us -> none  [passed_along(): lax.ppermute(value, axis, [(source, source + steps) for source in range(f...]
    all_gather x2 -> x0, waiting for transfers between devices: 63.3 us -> none  [the longest x1 63.3 us: fast(): lax.all_gather(jnp.concatenate([w_query, w_key, w_value, w_out.reshape(w_...]
    reduce_scatter x1 -> x0, waiting for transfers between devices: 48.2 us -> none  [fast(): lax.psum_scatter(weight_blocks, ('gx', 'gy'), scatter_dimension=0, tiled=...]
    slice x16 -> x3, local copies, waits for them, and re-layouts: 49.4 us -> 3.87 us  [the longest x1 1.89 us: fast(): weight_part[:, 2 * head_cols:]]
  transfers between devices with their start and end apart: 32 -> 0, of which waited for: 11 -> 0; matrix products, arithmetic and copies ran while one was open for 18% -> 0% of each run, Pallas kernels for 0% -> 0%
where the time goes in v2:
time: 469 us; the launch traced here: 467 us
  Pallas kernels  360 us (77%)
  local copies, waits for them, and re-layouts  99.2 us (21%)
  other arithmetic  5.55 us (1%)
    pallas_call x1, Pallas kernels, moe(): pl.pallas_call(functools.partial(moe_kernel, experts, capacity, width, un...  233 us
    pallas_call x1, Pallas kernels, front(): pl.pallas_call(functools.partial(front_kernel, heads, experts), out_shape...  71.3 us
    pallas_call x1, Pallas kernels, back_pass(): pl.pallas_call(functools.partial(back_kernel, heads, EXPERTS), out_shape=...  55.9 us
    unnamed x17, local copies, waits for them, and re-layouts  43.2 us
    transpose x1, local copies, waits for them, and re-layouts, fast(): grad_hidden = jnp.transpose(hidden_grads, (1, 2, 0)).reshape(width_cols, -1)  12.7 us
    transpose x1, local copies, waits for them, and re-layouts, fast(): grad_back = jnp.transpose(back_grads, (1, 2, 0)).reshape(width_cols, -1)  12.7 us

profile of v2, /device:TPU:0, one launch (start us, length us, event | category | flops | bytes accessed | tf_op | source)
XLA Modules:
  0.0 466.9 jit_solution(5735859313523640067)
XLA Ops:
  0.6 0.8 dynamic-slice_bitcast_fusion
  1.4 0.1 pad.2.clone
  1.5 1.3 broadcast_in_dim.37.gain1_ref
  2.8 1.4 copy.32.table_ref
  4.1 1.5 maximum_maximum_fusion.small_ref
  5.6 0.7 copy.42.choice_ref
  6.3 1.6 pad_maximum_fusion.wqkv_ref
  8.0 0.9 fusion.3
  8.9 1.7 copy.43.doc_col
  10.6 0.2 slice.32
  10.8 0.3 fusion.1
  11.2 0.5 fusion
  11.7 0.9 select_reduce_fusion
  12.6 0.7 fusion.7
  13.3 0.0 copy-start.3
  13.3 2.0 copy.41.slot_col
  15.3 7.9 %copy.37 = bf16[192,12288]{0,1:T(8,128)(2,1)} copy(bf16[192,12288]{1,0:T(8,128)(2,1)} %param.23) | data formatting | bytes 9437184 | tf_op args[9]
  23.2 0.0 copy-done.3
  23.2 8.7 %copy.38 = bf16[192,384,32]{1,0,2:T(8,128)(2,1)} copy(bf16[192,384,32]{0,2,1:T(8,128)(2,1)} %bitcast.35) | data formatting | bytes 9437184 | tf_op jit(solution)/shard_map/reshape | solution.py:1368
  31.9 7.9 %copy.39 = bf16[192,12288]{0,1:T(8,128)(2,1)} copy(bf16[192,12288]{1,0:T(8,128)(2,1)} %param.24) | data formatting | bytes 9437184 | tf_op args[10]
  39.8 8.7 %copy.40 = bf16[192,384,32]{1,0,2:T(8,128)(2,1)} copy(bf16[192,384,32]{0,2,1:T(8,128)(2,1)} %bitcast.36) | data formatting | bytes 9437184 | tf_op jit(solution)/shard_map/reshape | solution.py:1369
  48.5 71.3 %shard_map.229 = (bf16[32,128,384]{2,1,0:T(8,128)(2,1)}, f32[128,768]{1,0:T(8,128)}, f32[128,768]{1,0:T(8,128)}, f32[128,32]{1,0:T(8,128)}, f32[128,1]{1,0:T(8,1...) custom-call(bf16[128,768]{1,0:T(8,128)(2,1)} %x_ref.3, ...), custom_call_target="tpu_custom_call" | custom-call | flops 4000000000 | bytes 20000000 | tf_op jit(solution)/shard_map/pallas_call | solution.py:982
  119.8 233.3 %shard_map.230 = (f32[4,128,384]{2,1,0:T(8,128)}, f32[32,192,384]{2,1,0:T(8,128)}, f32[32,192,384]{2,1,0:T(8,128)}) custom-call(bf16[4096,384]{1,0:T(8,128)(2,1)} %bitcast.51, s32[1,4096]{1,0:T(1,128)} %bitcast.44, s32[4096,1]{1,0:T(8,128)} %copy.41.slot_col, bf16[32,192,384]{2,1,0:T(8,128)(2,1)} %bitcast.39, bf16[32,192,384]{2,1,0:T(8,128)(2,1)} %bitcast.40), custom_call_target="tpu_custom_call" | custom-call | flops 20000000000 | bytes 50000000 | tf_op jit(solution)/shard_map/pallas_call | solution.py:694
  353.1 55.9 %shard_map.231 = (f32[128,768]{1,0:T(8,128)}, f32[128,768]{1,0:T(8,128)}, f32[192,288]{1,0:T(8,128)}, f32[96,192]{1,0:T(8,128)}, f32[40,192]{1,0:T(8,128)}, /*index=5*/f32[40,128]{1,0:T(8,128)}) custom-call(bf16[128,768]{1,0:T(8,128)(2,1)} %x_ref.3, f32[1,768]{1,0:T(1,128)} %broadcast_in_dim.37.gain1_ref, bf16[128,768]{1,0:T(8,128)(2,1)} %grad_ref.3, ...), custom_call_target="tpu_custom_call" | custom-call | flops 6000000000 | bytes 20000000 | tf_op jit(solution)/shard_map/pallas_call | solution.py:1283
  408.9 1.3 slice.30
  410.2 1.4 slice_bitcast_fusion
  411.6 1.3 slice_bitcast_fusion.1
  412.8 0.7 slice.29
  413.6 0.7 copy.46
  414.2 1.9 fusion.8
  416.1 12.7 %copy.44 = f32[192,384,32]{0,2,1:T(8,128)} copy(f32[192,384,32]{1,0,2:T(8,128)} %bitcast.38) | data formatting | bytes 18874368 | tf_op jit(solution)/shard_map/transpose | solution.py:1391
  428.9 11.5 %copy.47 = f32[192,12288]{1,0:T(8,128)} copy(f32[192,12288]{0,1:T(8,128)} %bitcast.33) | data formatting | bytes 18874368
  440.4 12.7 %copy.45 = f32[192,384,32]{0,2,1:T(8,128)} copy(f32[192,384,32]{1,0,2:T(8,128)} %bitcast.37) | data formatting | bytes 18874368 | tf_op jit(solution)/shard_map/transpose | solution.py:1392
  453.1 0.0 copy-start.1
  453.1 0.0 copy-start
  453.1 0.0 copy-start.2
  453.1 11.6 %copy.48 = f32[192,12288]{1,0:T(8,128)} copy(f32[192,12288]{0,1:T(8,128)} %bitcast.34) | data formatting | bytes 18874368
  464.8 0.0 copy-done.1
  464.8 0.7 copy.57
  465.5 0.0 copy-done
  465.5 0.7 copy.58
  466.3 0.0 copy-done.2
  466.3 0.6 copy.59
  (1 shorter events, 0.0 us)
Async XLA Ops:
  13.3 9.9 %copy-start.3 = (s32[4096]{0:T(1024)}, s32[4096]{0:T(1024)S(1)}, u32[]{:S(2)}) copy-start(s32[4096]{0:T(1024)S(1)} %fusion.7) | copy-start | bytes 49156
  453.1 11.6 %copy-start.1 = (f32[128,768]{1,0:T(8,128)S(1)}, f32[128,768]{1,0:T(8,128)}, u32[]{:S(2)}) copy-start(f32[128,768]{1,0:T(8,128)} %get-tuple-element.97) | copy-start | bytes 1179652
  453.1 12.4 %copy-start = (f32[128,768]{1,0:T(8,128)S(1)}, f32[128,768]{1,0:T(8,128)}, u32[]{:S(2)}) copy-start(f32[128,768]{1,0:T(8,128)} %get-tuple-element.98) | copy-start | bytes 1179652
  453.1 13.1 %copy-start.2 = (f32[96,192]{1,0:T(8,128)S(1)}, f32[96,192]{1,0:T(8,128)}, u32[]{:S(2)}) copy-start(f32[96,192]{1,0:T(8,128)} %get-tuple-element.104) | copy-start | bytes 221188

commit v3 on v2

--- a/solution.py
+++ b/solution.py
@@ -463,6 +463,10 @@
 f32, bf16 = jnp.float32, jnp.bfloat16
 
 
+def nn(a, b):
+    return jnp.dot(a, b, preferred_element_type=f32)
+
+
 def nt(a, b):
     return lax.dot_general(a, b, (((1,), (1,)), ((), ())), preferred_element_type=f32)
 
@@ -475,256 +479,6 @@
     return pltpu.make_async_remote_copy(
         src_ref=src, dst_ref=dst, send_sem=send_sem, recv_sem=recv_sem,
         device_id=device, device_id_type=MESH)
-
-
-def greet(devices):
-    barrier = pltpu.get_barrier_semaphore()
-    for device in devices:
-        pl.semaphore_signal(barrier, inc=1, device_id=device, device_id_type=MESH)
-    pl.semaphore_wait(barrier, len(devices))
-
-
-RING = 8
-GROUP = 8
-LAG_B, LAG_C, LAG_D = 2, 4, 6
-
-
-def moe_kernel(experts, capacity, width, units, tokens,
-               r_ref, slot_row, slot_col, w1_ref, w2_ref,
-               out_ref, gh_ref, gb_ref,
-               x_sl, g_sl, p_ref, re_ref, rm_ref, c_ref, y_ref, gh_st, gb_st,
-               pair_out, pair_in, chip_out, chip_in, line_out, line_in,
-               p_sem, re_sem, rm_sem, t_sem, gh_sem, gb_sem,
-               po_sem, pi_sem, co_sem, ci_sem, lo_sem, li_sem):
-    gx, gy = lax.axis_index("gx"), lax.axis_index("gy")
-    core, chip = lax.rem(gy, 2), gy // 2
-    peer = gy + 1 - 2 * core
-    is_mid = jnp.logical_and(gx > 0, gx < 3)
-    is_end = jnp.logical_not(is_mid)
-    mid_of = jnp.where(gx < 2, 1, 2)
-    other_mid = 3 - mid_of
-    end_of = jnp.where(gx < 2, 0, 3)
-    line = [lax.rem(gx + k, 4) for k in (1, 2, 3)]
-    chips = [lax.rem(chip + k, 4) for k in (1, 2, 3)]
-    greet([(z, gy) for z in line] + [(gx, 2 * c + core) for c in chips] + [(gx, peer)])
-
-    def send_p(e):
-        return remote(p_ref.at[lax.rem(e, RING)], re_ref.at[e], p_sem.at[lax.rem(e, RING)], re_sem.at[e], (mid_of, gy))
-
-    def send_s(e):
-        return remote(p_ref.at[lax.rem(e, RING)], rm_ref.at[e], p_sem.at[lax.rem(e, RING)], rm_sem.at[e], (other_mid, gy))
-
-    def send_t(e):
-        return remote(re_ref.at[e], re_ref.at[e], t_sem.at[e], re_sem.at[e], (end_of, gy))
-
-    def grad_copy(stage, target, sems, e):
-        return pltpu.make_async_copy(stage.at[lax.rem(e, 2)], target.at[e], sems.at[lax.rem(e, 2)])
-
-    kblock = 1024
-
-    def step(i, carry):
-        @pl.when(i < experts)
-        def _():
-            e = i
-            sl = lax.rem(e, RING)
-
-            @pl.when(e >= RING)
-            def _():
-                send_p(e - RING).wait_send()
-            ids = lax.broadcasted_iota(jnp.int32, (capacity, kblock), 0) + e * capacity
-            acc = jnp.zeros((capacity, 2 * width), f32)
-            for kb in range(tokens // kblock):
-                hot = (slot_row[:, kb * kblock:(kb + 1) * kblock] == ids).astype(f32).astype(bf16)
-                acc = acc + jnp.dot(hot, r_ref[kb * kblock:(kb + 1) * kblock, :], preferred_element_type=f32)
-            xs = acc[:, :width].astype(bf16)
-            gs = acc[:, width:].astype(bf16)
-            x_sl[sl] = xs
-            g_sl[sl] = gs
-            p_ref[sl, 0:capacity, :] = jnp.dot(xs, w1_ref[e], preferred_element_type=f32).astype(bf16)
-            p_ref[sl, capacity:2 * capacity, :] = jnp.dot(gs, w2_ref[e], preferred_element_type=f32).astype(bf16)
-
-            @pl.when(is_end)
-            def _():
-                send_p(e).start()
-
-        eb = i - LAG_B
-
-        @pl.when(jnp.logical_and(is_mid, jnp.logical_and(eb >= 0, eb < experts)))
-        def _():
-            sl = lax.rem(eb, RING)
-            send_p(eb).wait_recv()
-            p_ref[sl] = (p_ref[sl].astype(f32) + re_ref[eb].astype(f32)).astype(bf16)
-            send_s(eb).start()
-
-        ec = i - LAG_C
-
-        @pl.when(jnp.logical_and(is_mid, jnp.logical_and(ec >= 0, ec < experts)))
-        def _():
-            sl = lax.rem(ec, RING)
-            send_s(ec).wait_recv()
-            re_ref[ec] = (p_ref[sl].astype(f32) + rm_ref[ec].astype(f32)).astype(bf16)
-            send_t(ec).start()
-
-        ed = i - LAG_D
-
-        @pl.when(ed >= 0)
-        def _():
-            e = ed
-            sl = lax.rem(e, RING)
-
-            @pl.when(is_end)
-            def _():
-                send_t(e).wait_recv()
-            u = re_ref[e, 0:capacity, :].astype(f32)
-            ag = re_ref[e, capacity:2 * capacity, :].astype(f32)
-            u2 = u * u
-            th = jnp.tanh(GELU_C * (u + 0.044715 * (u2 * u)))
-            half = 0.5 * (1.0 + th)
-            act = (u * half).astype(bf16)
-            dg = half + 0.5 * u * (1.0 - th * th) * (GELU_C * (1.0 + 3 * 0.044715 * u2))
-            pg = (ag * dg).astype(bf16)
-            y1 = nt(act, w2_ref[e])
-            y2 = nt(pg, w1_ref[e])
-            row = pl.multiple_of(lax.rem(e, GROUP) * capacity, 32)
-            y_ref[pl.ds(row, capacity), :] = jnp.concatenate([y1, y2], axis=1).astype(bf16)
-
-            @pl.when(e >= 2)
-            def _():
-                grad_copy(gh_st, gh_ref, gh_sem, e - 2).wait()
-                grad_copy(gb_st, gb_ref, gb_sem, e - 2).wait()
-            gh_st[lax.rem(e, 2)] = tn(x_sl[sl], pg)
-            gb_st[lax.rem(e, 2)] = tn(g_sl[sl], act)
-            grad_copy(gh_st, gh_ref, gh_sem, e).start()
-            grad_copy(gb_st, gb_ref, gb_sem, e).start()
-
-            @pl.when(lax.rem(e, GROUP) == GROUP - 1)
-            def _():
-                rows = 512
-                base = (e - (GROUP - 1)) * capacity
-
-                def block(b, c):
-                    at = pl.ds(pl.multiple_of(b * rows, rows), rows)
-                    cols = lax.broadcasted_iota(jnp.int32, (rows, GROUP * capacity), 1) + base
-                    hot = (slot_col[at, :] == cols).astype(f32).astype(bf16)
-                    add = jnp.dot(hot, y_ref[...], preferred_element_type=f32)
-
-                    @pl.when(e == GROUP - 1)
-                    def _():
-                        c_ref[at, :] = add
-
-                    @pl.when(e > GROUP - 1)
-                    def _():
-                        c_ref[at, :] = c_ref[at, :] + add
-                    return c
-                lax.fori_loop(0, tokens // rows, block, 0)
-        return carry
-
-    lax.fori_loop(0, experts + LAG_D, step, 0)
-
-    def drain(e, carry):
-        send_p(e).wait_send()
-        return carry
-    lax.fori_loop(experts - RING, experts, drain, 0)
-
-    @pl.when(is_mid)
-    def _():
-        lax.fori_loop(0, experts, lambda e, c: (send_t(e).wait_send(), c)[1], 0)
-    for e in (experts - 2, experts - 1):
-        grad_copy(gh_st, gh_ref, gh_sem, e).wait()
-        grad_copy(gb_st, gb_ref, gb_sem, e).wait()
-
-    local = tokens // 32
-
-    def c_block(z, c, k):
-        return pl.ds(pl.multiple_of((z * 8 + 2 * c + k) * local, local), local)
-
-    def pair_copy(z):
-        return remote(pair_out.at[z], pair_in.at[z], po_sem.at[z], pi_sem.at[z], (gx, peer))
-
-    def chip_copy(z, k):
-        return remote(chip_out.at[z, k], chip_in.at[z, k], co_sem.at[z, k], ci_sem.at[z, k],
-                      (gx, 2 * chips[k] + core))
-
-    def line_copy(k):
-        return remote(line_out.at[k], line_in.at[k], lo_sem.at[k], li_sem.at[k], (line[k], gy))
-
-    order = [lax.rem(gx + 1 + k, 4) for k in range(4)]
-    for k in range(4):
-        z = order[k]
-        for c in range(4):
-            pair_out[k, c] = c_ref[c_block(z, c, 1 - core), :].astype(bf16)
-        pair_copy(k).start()
-    for k in range(4):
-        z = order[k]
-        pair_copy(k).wait_recv()
-        for j in range(3):
-            chip_out[k, j] = (c_ref[c_block(z, chips[j], core), :] + pair_in[k, chips[j]].astype(f32)).astype(bf16)
-            chip_copy(k, j).start()
-    for k in range(4):
-        z = order[k]
-        total = c_ref[c_block(z, chip, core), :] + pair_in[k, chip].astype(f32)
-        for j in range(3):
-            chip_copy(k, j).wait_recv()
-            total = total + chip_in[k, j].astype(f32)
-        if k < 3:
-            line_out[k] = total.astype(bf16)
-            line_copy(k).start()
-        else:
-            out_ref[gx] = total
-    for k in range(3):
-        line_copy(k).wait_recv()
-        src = lax.rem(gx + 3 - k, 4)
-        out_ref[src] = line_in[k].astype(f32)
-    for k in range(4):
-        pair_copy(k).wait_send()
-        for j in range(3):
-            chip_copy(k, j).wait_send()
-    for k in range(3):
-        line_copy(k).wait_send()
-
-
-def moe(rows, slot_row, slot_col, w1, w2, collective_id):
-    experts, width, units = w1.shape
-    tokens = rows.shape[0]
-    capacity = tokens * 5 // (4 * experts)
-    local = tokens // 32
-    vm = pl.BlockSpec(memory_space=pltpu.VMEM)
-    hbm = pl.BlockSpec(memory_space=pl.ANY)
-    dma = pltpu.SemaphoreType.DMA
-    return pl.pallas_call(
-        functools.partial(moe_kernel, experts, capacity, width, units, tokens),
-        out_shape=(jax.ShapeDtypeStruct((4, local, 2 * width), f32),
-                   jax.ShapeDtypeStruct((experts, width, units), f32),
-                   jax.ShapeDtypeStruct((experts, width, units), f32)),
-        in_specs=[vm] * 5,
-        out_specs=(vm, hbm, hbm),
-        scratch_shapes=[
-            pltpu.VMEM((RING, capacity, width), bf16),
-            pltpu.VMEM((RING, capacity, width), bf16),
-            pltpu.VMEM((RING, 2 * capacity, units), bf16),
-            pltpu.VMEM((experts, 2 * capacity, units), bf16),
-            pltpu.VMEM((experts, 2 * capacity, units), bf16),
-            pltpu.VMEM((tokens, 2 * width), f32),
-            pltpu.VMEM((GROUP * capacity, 2 * width), bf16),
-            pltpu.VMEM((2, width, units), f32),
-            pltpu.VMEM((2, width, units), f32),
-            pltpu.VMEM((4, 4, local, 2 * width), bf16),
-            pltpu.VMEM((4, 4, local, 2 * width), bf16),
-            pltpu.VMEM((4, 3, local, 2 * width), bf16),
-            pltpu.VMEM((4, 3, local, 2 * width), bf16),
-            pltpu.VMEM((3, local, 2 * width), bf16),
-            pltpu.VMEM((3, local, 2 * width), bf16),
-            dma((RING,)), dma((experts,)), dma((experts,)), dma((experts,)), dma((2,)), dma((2,)),
-            dma((4,)), dma((4,)), dma((4, 3)), dma((4, 3)), dma((3,)), dma((3,)),
-        ],
-        compiler_params=pltpu.CompilerParams(
-            collective_id=collective_id, has_side_effects=True, vmem_limit_bytes=62 * 2**20),
-        cost_estimate=pl.CostEstimate(flops=20 * 10**9, bytes_accessed=50 * 10**6, transcendentals=2 * 10**6),
-    )(rows, slot_row, slot_col, w1, w2)
-
-
-def nn(a, b):
-    return jnp.dot(a, b, preferred_element_type=f32)
 
 
 class Place:
@@ -736,6 +490,11 @@
         self.chips = [lax.rem(self.chip + k, 4) for k in (1, 2, 3)]
         self.line_from = [lax.rem(self.gx + 4 - k, 4) for k in (1, 2, 3)]
         self.chips_from = [lax.rem(self.chip + 4 - k, 4) for k in (1, 2, 3)]
+        self.is_mid = jnp.logical_and(self.gx > 0, self.gx < 3)
+        self.is_end = jnp.logical_not(self.is_mid)
+        self.mid = (jnp.where(self.gx < 2, 1, 2), self.gy)
+        self.other_mid = (jnp.where(self.gx < 2, 2, 1), self.gy)
+        self.end = (jnp.where(self.gx < 2, 0, 3), self.gy)
 
     def on_line(self, k):
         return (self.line[k], self.gy)
@@ -744,7 +503,340 @@
         return (self.gx, 2 * self.chips[k] + self.core)
 
     def greet_all(self):
-        greet([self.on_line(k) for k in range(3)] + [self.on_plane(k) for k in range(3)] + [self.pair])
+        devices = [self.on_line(k) for k in range(3)] + [self.on_plane(k) for k in range(3)] + [self.pair]
+        barrier = pltpu.get_barrier_semaphore()
+        for device in devices:
+            pl.semaphore_signal(barrier, inc=1, device_id=device, device_id_type=MESH)
+        pl.semaphore_wait(barrier, len(devices))
+
+
+def as_column(row):
+    n = row.shape[1]
+    same = lax.broadcasted_iota(jnp.int32, (n, n), 0) == lax.broadcasted_iota(jnp.int32, (n, n), 1)
+    return jnp.sum(jnp.where(same, row.astype(f32), 0.0), axis=1, keepdims=True)
+
+
+def pick_rows(slot_row, base, capacity, rows_ref, tokens):
+    kblock = 1024
+    ids = lax.broadcasted_iota(jnp.int32, (capacity, kblock), 0) + base
+    total = None
+    for kb in range(tokens // kblock):
+        hot = (slot_row[:, kb * kblock:(kb + 1) * kblock] == ids).astype(f32).astype(bf16)
+        part = nn(hot, rows_ref[kb * kblock:(kb + 1) * kblock, :])
+        total = part if total is None else total + part
+    return total
+
+
+class LineSum:
+    def __init__(self, me, own, got, other, own_sem, got_sem, other_sem, out_sem, experts):
+        self.me, self.own, self.got, self.other = me, own, got, other
+        self.sems = (own_sem, got_sem, other_sem, out_sem)
+        self.ring, self.experts = own.shape[0], experts
+
+    def to_mid(self, e):
+        sl = lax.rem(e, self.ring)
+        return remote(self.own.at[sl], self.got.at[e], self.sems[0].at[sl], self.sems[1].at[e], self.me.mid)
+
+    def across(self, e):
+        sl = lax.rem(e, self.ring)
+        return remote(self.own.at[sl], self.other.at[e], self.sems[0].at[sl], self.sems[2].at[e], self.me.other_mid)
+
+    def to_end(self, e):
+        return remote(self.got.at[e], self.got.at[e], self.sems[3].at[e], self.sems[1].at[e], self.me.end)
+
+    def slot_free(self, e):
+        @pl.when(e >= self.ring)
+        def _():
+            self.to_mid(e - self.ring).wait_send()
+
+    def put(self, e, value):
+        self.own[lax.rem(e, self.ring)] = value
+
+        @pl.when(self.me.is_end)
+        def _():
+            self.to_mid(e).start()
+
+    def half(self, e):
+        @pl.when(jnp.logical_and(self.me.is_mid, jnp.logical_and(e >= 0, e < self.experts)))
+        def _():
+            sl = lax.rem(e + self.ring, self.ring)
+            self.to_mid(e).wait_recv()
+            self.own[sl] = (self.own[sl].astype(f32) + self.got[e].astype(f32)).astype(bf16)
+            self.across(e).start()
+
+    def whole(self, e):
+        @pl.when(jnp.logical_and(self.me.is_mid, jnp.logical_and(e >= 0, e < self.experts)))
+        def _():
+            sl = lax.rem(e + self.ring, self.ring)
+            self.across(e).wait_recv()
+            self.got[e] = (self.own[sl].astype(f32) + self.other[e].astype(f32)).astype(bf16)
+            self.to_end(e).start()
+
+    def await_total(self, e):
+        @pl.when(self.me.is_end)
+        def _():
+            self.to_end(e).wait_recv()
+
+    def drain(self):
+        def sent(e, carry):
+            self.to_mid(e).wait_send()
+            return carry
+        lax.fori_loop(self.experts - self.ring, self.experts, sent, 0)
+
+        @pl.when(self.me.is_mid)
+        def _():
+            def out(e, carry):
+                self.to_end(e).wait_send()
+                return carry
+            lax.fori_loop(0, self.experts, out, 0)
+
+
+RING = 8
+GROUP = 4
+LAG_B, LAG_C, LAG_D = 2, 4, 6
+
+
+def moe_kernel(experts, capacity, width, units, tokens,
+               rows_ref, slot_row, w1_ref, w2_ref, gs_ref, ag_ref,
+               out_ref, gh_ref, gb_ref,
+               xs_ref, p_ref, got_ref, other_ref, gh_st, gb_st,
+               y_own, y_out, y_in, s_out, s_in, yt_ref, line_out, line_in,
+               p_sem, got_sem, other_sem, t_sem, gh_sem, gb_sem,
+               yo_s, yo_r, so_s, so_r, ya_s, ya_r, yp_s, yp_r, lo_s, lo_r):
+    me = Place()
+    gx, gy, core, chip = me.gx, me.gy, me.core, me.chip
+    half = capacity // 2
+    me.greet_all()
+    line = LineSum(me, p_ref, got_ref, other_ref, p_sem, got_sem, other_sem, t_sem, experts)
+    groups = experts // GROUP
+
+    def grad_copy(stage, target, sems, e):
+        return pltpu.make_async_copy(stage.at[lax.rem(e, 2)], target.at[e], sems.at[lax.rem(e, 2)])
+
+    def pair_half(j):
+        return remote(y_out.at[j], y_in.at[j], yo_s.at[j], yo_r.at[j], me.pair)
+
+    def to_owner(j, k):
+        return remote(s_out.at[j, me.chips[k]], s_in.at[j, k], so_s.at[j, k], so_r.at[j, k], me.on_plane(k))
+
+    own_half = pl.ds(pl.multiple_of(core * half, 16), half)
+
+    def from_owner(j, k):
+        at = yt_ref.at[j * GROUP + chip, own_half]
+        return remote(at, at, ya_s.at[j, k], ya_r.at[j, k], me.on_plane(k))
+
+    def pair_total(j, k):
+        c = chip if k == 0 else me.chips_from[k - 1]
+        at = yt_ref.at[j * GROUP + c, own_half]
+        return remote(at, at, yp_s.at[j, k], yp_r.at[j, k], me.pair)
+
+    def stage_two(j):
+        pair_half(j).wait_recv()
+        for m in range(GROUP):
+            s_out[j, m] = (y_own[j, m].astype(f32) + y_in[j, m].astype(f32)).astype(bf16)
+        for k in range(3):
+            to_owner(j, k).start()
+
+    def stage_three(j):
+        total = s_out[j, chip].astype(f32)
+        for k in range(3):
+            to_owner(j, k).wait_recv()
+            total = total + s_in[j, k].astype(f32)
+        yt_ref[j * GROUP + chip, own_half] = total.astype(bf16)
+        for k in range(3):
+            from_owner(j, k).start()
+        pair_total(j, 0).start()
+
+    def stage_four(j):
+        for k in range(3):
+            from_owner(j, k).wait_recv()
+            pair_total(j, k + 1).start()
+
+    def step(i, carry):
+        @pl.when(i < experts)
+        def _():
+            line.slot_free(i)
+            xs = pick_rows(slot_row, i * capacity, capacity, rows_ref, tokens).astype(bf16)
+            xs_ref[lax.rem(i, RING)] = xs
+            line.put(i, nn(xs[:, :width], w1_ref[i]).astype(bf16))
+        line.half(i - LAG_B)
+        line.whole(i - LAG_C)
+        e = i - LAG_D
+
+        @pl.when(e >= 0)
+        def _():
+            line.await_total(e)
+            xs = xs_ref[lax.rem(e, RING)]
+            pieces = xs[:, width:].astype(f32)
+            gate = pieces[:, 0:1] + pieces[:, 1:2] + pieces[:, 2:3]
+            u = got_ref[e].astype(f32)
+            ag = gate * ag_ref[e].astype(f32)
+            u2 = u * u
+            th = jnp.tanh(GELU_C * (u + 0.044715 * (u2 * u)))
+            part = 0.5 * (1.0 + th)
+            act = (u * part).astype(bf16)
+            dg = part + 0.5 * u * (1.0 - th * th) * (GELU_C * (1.0 + 3 * 0.044715 * u2))
+            pg = (ag * dg).astype(bf16)
+            y = jnp.concatenate([nt(act, w2_ref[e]), nt(pg, w1_ref[e])], axis=1).astype(bf16)
+            j, m = e // GROUP, lax.rem(e, GROUP)
+
+            @pl.when(core == 0)
+            def _():
+                y_own[j, m] = y[:half]
+                y_out[j, m] = y[half:]
+
+            @pl.when(core == 1)
+            def _():
+                y_own[j, m] = y[half:]
+                y_out[j, m] = y[:half]
+
+            @pl.when(e >= 2)
+            def _():
+                grad_copy(gh_st, gh_ref, gh_sem, e - 2).wait()
+                grad_copy(gb_st, gb_ref, gb_sem, e - 2).wait()
+            slot_grad = (gate * gs_ref[e].astype(f32)).astype(bf16)
+            gh_st[lax.rem(e, 2)] = tn(xs[:, :width], pg).astype(bf16)
+            gb_st[lax.rem(e, 2)] = tn(slot_grad, act).astype(bf16)
+            grad_copy(gh_st, gh_ref, gh_sem, e).start()
+            grad_copy(gb_st, gb_ref, gb_sem, e).start()
+
+            @pl.when(m == GROUP - 1)
+            def _():
+                pair_half(j).start()
+
+            @pl.when(jnp.logical_and(m == 0, j >= 1))
+            def _():
+                stage_two(j - 1)
+
+            @pl.when(jnp.logical_and(m == 2, j >= 1))
+            def _():
+                stage_three(j - 1)
+
+            @pl.when(jnp.logical_and(m == 1, j >= 2))
+            def _():
+                stage_four(j - 2)
+        return carry
+
+    lax.fori_loop(0, experts + LAG_D, step, 0)
+    last = groups - 1
+    stage_two(last)
+    stage_four(last - 1)
+    slots = [as_column(slot_row[:, pl.ds(pl.multiple_of((z * 8 + gy) * 128, 128), 128)]) for z in range(4)]
+    own_slots = jnp.concatenate(slots, axis=0).astype(jnp.int32)
+    many = 8
+    cols = lax.broadcasted_iota(jnp.int32, (own_slots.shape[0], many * capacity), 1)
+
+    def picked(b):
+        hot = (own_slots == cols + b * many * capacity).astype(f32).astype(bf16)
+        return nn(hot, yt_ref[b * many:(b + 1) * many].reshape(many * capacity, 2 * width))
+
+    per = many // GROUP
+    stage_three(last)
+    total = None
+    for b in range(experts // many - 1):
+        for j in range(b * per, (b + 1) * per):
+            for k in range(4):
+                pair_total(j, k).wait_recv()
+        part = picked(b)
+        total = part if total is None else total + part
+    stage_four(last)
+    for j in range(groups - per, groups):
+        for k in range(4):
+            pair_total(j, k).wait_recv()
+    total = total + picked(experts // many - 1)
+    local = tokens // 32
+
+    def line_copy(k):
+        return remote(line_out.at[me.line[k]], line_in.at[k], lo_s.at[k], lo_r.at[k], me.on_line(k))
+
+    for z in range(4):
+        line_out[z] = total[z * local:(z + 1) * local].astype(bf16)
+    for k in range(3):
+        line_copy(k).start()
+    out_ref[gx] = line_out[gx].astype(f32)
+    for k in range(3):
+        line_copy(k).wait_recv()
+        out_ref[me.line_from[k]] = line_in[k].astype(f32)
+    line.drain()
+    for e in (experts - 2, experts - 1):
+        grad_copy(gh_st, gh_ref, gh_sem, e).wait()
+        grad_copy(gb_st, gb_ref, gb_sem, e).wait()
+
+    def sent(j, carry):
+        pair_half(j).wait_send()
+        for k in range(3):
+            to_owner(j, k).wait_send()
+            from_owner(j, k).wait_send()
+        for k in range(4):
+            pair_total(j, k).wait_send()
+        return carry
+    lax.fori_loop(0, groups, sent, 0)
+    for k in range(3):
+        line_copy(k).wait_send()
+
+
+def moe(rows, slot_row, w1, w2, slot_grads, act_grads, collective_id):
+    experts, width, units = w1.shape
+    tokens = rows.shape[0]
+    capacity = slot_grads.shape[1]
+    local = tokens // 32
+    groups = experts // GROUP
+    half = capacity // 2
+    vm = pl.BlockSpec(memory_space=pltpu.VMEM)
+    hbm = pl.BlockSpec(memory_space=pl.ANY)
+    dma = pltpu.SemaphoreType.DMA
+    V = pltpu.VMEM
+    return pl.pallas_call(
+        functools.partial(moe_kernel, experts, capacity, width, units, tokens),
+        out_shape=(jax.ShapeDtypeStruct((4, local, 2 * width), f32),
+                   jax.ShapeDtypeStruct((experts, width, units), bf16),
+                   jax.ShapeDtypeStruct((experts, width, units), bf16)),
+        in_specs=[vm] * 6,
+        out_specs=(vm, hbm, hbm),
+        scratch_shapes=[
+            V((RING, capacity, rows.shape[1]), bf16),
+            V((RING, capacity, units), bf16),
+            V((experts, capacity, units), bf16),
+            V((experts, capacity, units), bf16),
+            V((2, width, units), bf16),
+            V((2, width, units), bf16),
+            V((groups, GROUP, half, 2 * width), bf16),
+            V((groups, GROUP, half, 2 * width), bf16),
+            V((groups, GROUP, half, 2 * width), bf16),
+            V((groups, GROUP, half, 2 * width), bf16),
+            V((groups, 3, half, 2 * width), bf16),
+            V((experts, capacity, 2 * width), bf16),
+            V((4, local, 2 * width), bf16),
+            V((3, local, 2 * width), bf16),
+            dma((RING,)), dma((experts,)), dma((experts,)), dma((experts,)), dma((2,)), dma((2,)),
+            dma((groups,)), dma((groups,)), dma((groups, 3)), dma((groups, 3)), dma((groups, 3)), dma((groups, 3)),
+            dma((groups, 4)), dma((groups, 4)), dma((3,)), dma((3,)),
+        ],
+        compiler_params=pltpu.CompilerParams(
+            collective_id=collective_id, has_side_effects=True, vmem_limit_bytes=62 * 2**20),
+        cost_estimate=pl.CostEstimate(flops=20 * 10**9, bytes_accessed=50 * 10**6, transcendentals=2 * 10**6),
+    )(rows, slot_row, w1, w2, slot_grads, act_grads)
+
+
+def place_one(lane):
+    register, unit, expert = lane // 128, lax.rem(lane // 32, 4), lax.rem(lane, 32)
+    return expert // 4 * 128 + lax.rem(expert, 4) * 32 + register * 4 + unit
+
+
+def place_two(lane):
+    register, expert, unit = lane // 128, lax.rem(lane // 32, 4), lax.rem(lane, 32)
+    return expert * 128 + register * 32 + unit
+
+
+def fill_moves(one_ref, two_ref, inward):
+    for ref, place in ((one_ref, place_one), (two_ref, place_two)):
+        n = ref.shape[0]
+        if inward:
+            moved = place(lax.broadcasted_iota(jnp.int32, (n, 1), 0))
+            ref[...] = (moved == lax.broadcasted_iota(jnp.int32, (n, n), 1)).astype(f32).astype(bf16)
+        else:
+            moved = place(lax.broadcasted_iota(jnp.int32, (1, n), 1))
+            ref[...] = (moved == lax.broadcasted_iota(jnp.int32, (n, n), 0)).astype(f32).astype(bf16)
 
 
 def near_buckets(rows):
@@ -771,6 +863,11 @@
         bias_ref[h, :, mid + 2 * rows:] = jnp.full((rows, span - mid - 2 * rows), table_ref[31, column], f32)
 
 
+def allowed_pairs(doc_row, block_at, local):
+    start = pl.multiple_of(block_at * local, local)
+    return as_column(doc_row[:, pl.ds(start, local)]) == doc_row[...].astype(f32)
+
+
 def unit_scores(q_block, keys, bias_ref, h, block_at, allowed):
     rows = q_block.shape[0]
     seq = keys.shape[0]
@@ -780,39 +877,167 @@
     return jnp.where(allowed, nt(masked, keys) + bias_ref[h, :, pl.ds(start, seq)], -1000000000.0)
 
 
-def front_kernel(heads, experts,
-                 x_ref, gain1_ref, wqkv_ref, wout_ref, table_ref, small_ref, doc_row, doc_col, choice_ref, grad_ref,
-                 rows_ref, hidden_ref, normed_ref, router_ref, gate_ref, at_ref, q_ref, kv_ref, lse_ref, xn_ref,
-                 wqkv_all, wout_all, small_all, bias_ref,
+def fill_slots(slot_ref, choice_row, experts, capacity):
+    tokens = choice_row.shape[1]
+    expert = lax.broadcasted_iota(jnp.int32, (experts, 128), 0)
+    upper = (lax.broadcasted_iota(jnp.int32, (128, 128), 0)
+             <= lax.broadcasted_iota(jnp.int32, (128, 128), 1)).astype(f32).astype(bf16)
+    before = jnp.zeros((experts, 1), f32)
+    for b in range(tokens // 128):
+        choice = choice_row[:, b * 128:(b + 1) * 128]
+        chosen = (expert == choice).astype(f32)
+        count = nn(chosen.astype(bf16), upper)
+        place = jnp.sum(chosen * (count + before), axis=0, keepdims=True).astype(jnp.int32) - 1
+        slot_ref[:, b * 128:(b + 1) * 128] = jnp.where(place < capacity, choice * capacity + place, -1)
+        before = before + count[:, 127:128]
+
+
+def front_kernel(heads, experts, capacity,
+                 x_ref, gain1_ref, wq_ref, wk_ref, wv_ref, wout_ref, table_ref, wr_ref, gain2_ref, doc_row, choice_row,
+                 grad_ref, wh_hbm, wb_hbm,
+                 rows_ref, slot_ref, w1_hbm, w2_hbm, ag_ref, gs_ref,
+                 hidden_ref, normed_ref, router_ref, gate_ref, at_ref, q_ref, kv_ref, lse_ref, xn_ref,
+                 wqkv_all, wout_all, small_all,
+                 bias_ref, w2_ref, nat_ref, half_ref, one_ref, two_ref, wt_ref, g_ref, g_out, own_ref, other_ref,
                  wq_st, wo_st, sm_st, at_in, rows_out,
+                 nat_sem, wt_sem, w2_sem, own_sem, got_sem, other_sem, t_sem,
                  xn_s, xn_r, wq_s, wq_r, wqp_s, wqp_r, sm_s, sm_r, wo_s, wo_r, woc_s, woc_r, wop_s, wop_r,
-                 kv_s, kv_r, at_s, at_r, rz_s, rz_r, rc_s, rc_r, rp_s, rp_r):
+                 kv_s, kv_r, at_s, at_r, gz_s, gz_r, rz_s, rz_r, gc_s, gc_r, gp_s, gp_r, rc_s, rc_r, rp_s, rp_r):
     me = Place()
     gx, gy, core, chip = me.gx, me.gy, me.core, me.chip
-    width = wqkv_ref.shape[0]
-    cols = wqkv_ref.shape[1] // 3
+    width, cols = wq_ref.shape
     local = x_ref.shape[0]
+    tokens = 32 * local
+    units = wh_hbm.shape[1] // experts
+    hd = 2 * cols
+    seq = 8 * local
+    zs = [gx] + me.line_from
+    spans = units // 128
+
+    def load_span(source, g, q):
+        at = source.at[:, pl.ds(pl.multiple_of(g * 4096 + q * 1024, 1024), 1024)]
+        return pltpu.make_async_copy(at, nat_ref.at[q], nat_sem.at[q])
+
+    def turn_span(source, g, put):
+        for q in range(4):
+            load_span(source, g, q).wait()
+            moved = nn(nat_ref[q], one_ref[...]).astype(bf16)
+            for r in range(8):
+                half_ref[r, :, q * 128:(q + 1) * 128] = moved[:, r * 128:(r + 1) * 128]
+        for r in range(8):
+            moved = nn(half_ref[r], two_ref[...]).astype(bf16)
+            put(r, [moved[:, n * 128:(n + 1) * 128] for n in range(4)])
+
+    def turn_back_weights():
+        def body(g, carry):
+            lanes = pl.ds(pl.multiple_of(g * 128, 128), 128)
+
+            def put(r, blocks):
+                for n, block in enumerate(blocks):
+                    w2_ref[4 * r + n, :, lanes] = block
+            turn_span(wb_hbm, g, put)
+
+            @pl.when(g + 1 < spans)
+            def _():
+                for q in range(4):
+                    load_span(wb_hbm, g + 1, q).start()
+            return carry
+        lax.fori_loop(0, spans, body, 0)
+        w2_copy().start()
+
+    def w2_copy():
+        return pltpu.make_async_copy(w2_ref, w2_hbm, w2_sem.at[0])
+
+    def store_span(g, r):
+        lanes = pl.ds(pl.multiple_of(g * 128, 128), 128)
+        return pltpu.make_async_copy(wt_ref.at[r], w1_hbm.at[pl.ds(4 * r, 4), :, lanes], wt_sem.at[r])
+
+    def turn_hidden_weights(g):
+        def put(r, blocks):
+            if g > 0:
+                store_span(g - 1, r).wait()
+            for n, block in enumerate(blocks):
+                wt_ref[r, n] = block
+            store_span(g, r).start()
+        turn_span(wh_hbm, g, put)
+        if g + 1 < spans:
+            for q in range(4):
+                load_span(wh_hbm, g + 1, q).start()
+
+    def dispatcher(out, dst, zsem_s, zsem_r, csem_s, csem_r, psem_s, psem_r):
+        def to_line(k):
+            return remote(out.at[me.line[k]], dst.at[gx * 8 + gy], zsem_s.at[k], zsem_r.at[k], me.on_line(k))
+
+        def to_plane(m, k):
+            at = dst.at[zs[m] * 8 + gy]
+            return remote(at, at, csem_s.at[m, k], csem_r.at[m, k], me.on_plane(k))
+
+        def to_pair(m, k):
+            c = chip if k == 0 else me.chips_from[k - 1]
+            at = dst.at[zs[m] * 8 + 2 * c + core]
+            return remote(at, at, psem_s.at[m, k], psem_r.at[m, k], me.pair)
+        return to_line, to_plane, to_pair
+
+    def start_plane(to_line, to_plane, to_pair, m):
+        if m > 0:
+            to_line(m - 1).wait_recv()
+        for k in range(3):
+            to_plane(m, k).start()
+        to_pair(m, 0).start()
+
+    g_line, g_plane, g_pair = dispatcher(g_out, g_ref, gz_s, gz_r, gc_s, gc_r, gp_s, gp_r)
+    r_line, r_plane, r_pair = dispatcher(rows_out, rows_ref, rz_s, rz_r, rc_s, rc_r, rp_s, rp_r)
+    acts = LineSum(me, own_ref, ag_ref, other_ref, own_sem, got_sem, other_sem, t_sem, experts)
+
+    def act_step(i, carry):
+        @pl.when(i < experts)
+        def _():
+            acts.slot_free(i)
+            gs = pick_rows(slot_ref, i * capacity, capacity, g_ref_rows, tokens).astype(bf16)
+            gs_ref[i] = gs
+            acts.put(i, nn(gs, w2_ref[i]).astype(bf16))
+        acts.half(i - LAG_B)
+        acts.whole(i - LAG_C)
+        return carry
+
+    class Rows:
+        def __getitem__(self, at):
+            rows = at[0]
+            return g_ref[rows.start // local:rows.stop // local].reshape(rows.stop - rows.start, width)
+
+    g_ref_rows = Rows()
+
+    def act_steps(first, last):
+        lax.fori_loop(first, last, act_step, 0)
+
+    for z in range(4):
+        g_out[z] = grad_ref[:, z * width:(z + 1) * width]
     x = x_ref[...].astype(f32)
     r1 = lax.rsqrt(jnp.mean(x * x, axis=-1, keepdims=True) + epsilon)
     xn_ref[chip] = (x * r1 * gain1_ref[...]).astype(bf16)
+    wq_st[core, gx] = jnp.concatenate([wq_ref[...], wk_ref[...], wv_ref[...]], axis=1)
+    wo_st[gy, gx] = wout_ref[...]
+    wr_wide = jnp.concatenate([wr_ref[...], jnp.zeros((width, 128 - experts), f32)], axis=1)
+    sm_st[gx] = jnp.concatenate([jnp.transpose(wr_wide)[:experts], gain2_ref[...], jnp.zeros((7, width), f32)], axis=0)
+    g_ref[gx * 8 + gy] = g_out[gx]
     me.greet_all()
 
     def wq_line(k):
-        return remote(wqkv_ref, wq_st.at[core, gx], wq_s.at[k], wq_r.at[k], me.on_line(k))
+        at = wq_st.at[core, gx]
+        return remote(at, at, wq_s.at[k], wq_r.at[k], me.on_line(k))
 
     def xn_plane(k):
         return remote(xn_ref.at[chip], xn_ref.at[chip], xn_s.at[k], xn_r.at[k], me.on_plane(k))
 
     def sm_line(k):
-        return remote(small_ref, sm_st.at[gx], sm_s.at[k], sm_r.at[k], me.on_line(k))
+        return remote(sm_st.at[gx], sm_st.at[gx], sm_s.at[k], sm_r.at[k], me.on_line(k))
 
     def wo_line(k):
-        return remote(wout_ref, wo_st.at[gy, gx], wo_s.at[k], wo_r.at[k], me.on_line(k))
+        return remote(wo_st.at[gy, gx], wo_st.at[gy, gx], wo_s.at[k], wo_r.at[k], me.on_line(k))
 
     def wq_pair(k):
-        src = wqkv_ref if k == 0 else wq_st.at[core, me.line_from[k - 1]]
-        z = gx if k == 0 else me.line_from[k - 1]
-        return remote(src, wq_st.at[core, z], wqp_s.at[k], wqp_r.at[k], me.pair)
+        at = wq_st.at[core, zs[k]]
+        return remote(at, at, wqp_s.at[k], wqp_r.at[k], me.pair)
 
     def wo_plane(k):
         return remote(wo_st.at[gy], wo_st.at[gy], woc_s.at[k], woc_r.at[k], me.on_plane(k))
@@ -822,16 +1047,30 @@
         return remote(wo_st.at[2 * c + core], wo_st.at[2 * c + core], wop_s.at[k], wop_r.at[k], me.pair)
 
     for k in range(3):
+        g_line(k).start()
+    for k in range(3):
         wq_line(k).start()
+    start_plane(g_line, g_plane, g_pair, 0)
+    for k in range(3):
         xn_plane(k).start()
     wq_pair(0).start()
     for k in range(3):
         wo_line(k).start()
         sm_line(k).start()
-    wq_st[core, gx] = wqkv_ref[...]
-    wo_st[gy, gx] = wout_ref[...]
-    sm_st[gx] = small_ref[...]
+    for q in range(4):
+        load_span(wb_hbm, 0, q).start()
+    fill_moves(one_ref, two_ref, True)
+    fill_slots(slot_ref, choice_row, experts, capacity)
     fill_bias(bias_ref, table_ref, chip, heads)
+    for m in (1, 2, 3):
+        start_plane(g_line, g_plane, g_pair, m)
+    turn_back_weights()
+    for q in range(4):
+        load_span(wh_hbm, 0, q).start()
+    for m in range(4):
+        for k in range(3):
+            g_plane(m, k).wait_recv()
+            g_pair(m, k + 1).start()
     for k in range(3):
         wq_line(k).wait_recv()
         wq_pair(k + 1).start()
@@ -840,6 +1079,10 @@
     for k in range(3):
         wo_plane(k).start()
     wo_pair(0).start()
+    for m in range(4):
+        for k in range(4):
+            g_pair(m, k).wait_recv()
+    act_steps(0, 4)
     for k in range(4):
         wq_pair(k).wait_recv()
     for z in range(4):
@@ -851,7 +1094,6 @@
         return remote(kv_ref.at[2 * c + core], kv_ref.at[2 * c + core], kv_s.at[c], kv_r.at[c], me.pair)
 
     scale = HSIZE ** (-0.5)
-    hd = 2 * cols
     for k in range(4):
         c = chip if k == 0 else me.chips_from[k - 1]
         if k > 0:
@@ -863,9 +1105,9 @@
     for k in range(3):
         wo_plane(k).wait_recv()
         wo_pair(k + 1).start()
+    act_steps(4, 7)
     for c in range(4):
         kv_pair(c).wait_recv()
-    seq = 8 * local
     lanes = lax.broadcasted_iota(jnp.int32, (local, hd), 1) // HSIZE
 
     def at_plane(k):
@@ -874,7 +1116,7 @@
     for k in range(4):
         c = me.chips[k] if k < 3 else chip
         block_at = 2 * c + core
-        allowed = doc_col[pl.ds(pl.multiple_of(block_at * local, local), local), :] == doc_row[...]
+        allowed = allowed_pairs(doc_row, block_at, local)
         keys = kv_ref[:, :, :hd].reshape(seq, hd)
         values = kv_ref[:, :, hd:].reshape(seq, hd)
         total = jnp.zeros((local, hd), f32)
@@ -891,6 +1133,7 @@
             at_plane(k).start()
         else:
             at_in[chip] = total.astype(bf16)
+        act_steps(7 + 2 * k, 9 + 2 * k)
     for k in range(3):
         sm_line(k).wait_recv()
     small_all[...] = jnp.concatenate([sm_st[z] for z in range(4)], axis=1)
@@ -911,78 +1154,87 @@
     lifted = jnp.exp(logits - jnp.max(logits, axis=-1, keepdims=True))
     router = lifted / jnp.sum(lifted, axis=-1, keepdims=True)
     router_ref[...] = router
-    picked = choice_ref[...] == lax.broadcasted_iota(jnp.int32, router.shape, 1)
+    own_tokens = pl.ds(pl.multiple_of((gx * 8 + gy) * local, local), local)
+    picked = as_column(choice_row[:, own_tokens]) == lax.broadcasted_iota(jnp.int32, router.shape, 1).astype(f32)
     gate = jnp.sum(jnp.where(picked, router, 0.0), axis=-1, keepdims=True)
     gate_ref[...] = gate
+    first = gate.astype(bf16).astype(f32)
+    second = (gate - first).astype(bf16).astype(f32)
+    third = gate - first - second
+    lane = lax.broadcasted_iota(jnp.int32, (local, 64), 1)
+    pieces = jnp.where(lane == 0, first, jnp.where(lane == 1, second, jnp.where(lane == 2, third, 0.0))).astype(bf16)
     low = normed.astype(bf16)
-    route = (gate * grad_ref[...].astype(f32)).astype(bf16)
     for z in range(4):
-        rows_out[z] = jnp.concatenate([low[:, z * width:(z + 1) * width], route[:, z * width:(z + 1) * width]], axis=1)
-
-    def rows_line(k):
-        return remote(rows_out.at[me.line[k]], rows_ref.at[gx * 8 + gy], rz_s.at[k], rz_r.at[k], me.on_line(k))
-
-    def rows_plane(z, k, m):
-        at = z * 8 + gy
-        return remote(rows_ref.at[at], rows_ref.at[at], rc_s.at[m, k], rc_r.at[m, k], me.on_plane(k))
-
-    def rows_pair(z, k, m):
-        c = chip if k == 0 else me.chips_from[k - 1]
-        at = z * 8 + 2 * c + core
-        return remote(rows_ref.at[at], rows_ref.at[at], rp_s.at[m, k], rp_r.at[m, k], me.pair)
-
-    for k in range(3):
-        rows_line(k).start()
+        rows_out[z] = jnp.concatenate([low[:, z * width:(z + 1) * width], pieces], axis=1)
+    for k in range(3):
+        r_line(k).start()
     rows_ref[gx * 8 + gy] = rows_out[gx]
-    zs = [gx] + me.line_from
-    for m in range(4):
-        if m > 0:
-            rows_line(m - 1).wait_recv()
-        for k in range(3):
-            rows_plane(zs[m], k, m).start()
-        rows_pair(zs[m], 0, m).start()
+    start_plane(r_line, r_plane, r_pair, 0)
+    act_steps(15, 18)
+    for m in (1, 2, 3):
+        start_plane(r_line, r_plane, r_pair, m)
+    act_steps(18, 21)
     for m in range(4):
         for k in range(3):
-            rows_plane(zs[m], k, m).wait_recv()
-            rows_pair(zs[m], k + 1, m).start()
+            r_plane(m, k).wait_recv()
+            r_pair(m, k + 1).start()
+    for n in range(spans):
+        turn_hidden_weights(n)
+        act_steps(21 + 3 * n, 24 + 3 * n)
+    act_steps(21 + 3 * spans, experts + LAG_C)
     for m in range(4):
         for k in range(4):
-            rows_pair(zs[m], k, m).wait_recv()
+            r_pair(m, k).wait_recv()
+
+    def arrived(e, carry):
+        acts.await_total(e)
+        return carry
+    lax.fori_loop(0, experts, arrived, 0)
+    acts.drain()
+    for r in range(8):
+        store_span(spans - 1, r).wait()
+    w2_copy().wait()
     for m in range(4):
         for k in range(4):
-            rows_pair(zs[m], k, m).wait_send()
+            g_pair(m, k).wait_send()
+            r_pair(m, k).wait_send()
         for k in range(3):
-            rows_plane(zs[m], k, m).wait_send()
-    for k in range(3):
-        rows_line(k).wait_send()
-        at_plane(k).wait_send()
-        wo_plane(k).wait_send()
-        wo_line(k).wait_send()
-        sm_line(k).wait_send()
-        wq_line(k).wait_send()
-        xn_plane(k).wait_send()
+            g_plane(m, k).wait_send()
+            r_plane(m, k).wait_send()
+    for k in range(3):
+        for copy in (g_line, r_line, at_plane, wo_plane, wo_line, sm_line, wq_line, xn_plane):
+            copy(k).wait_send()
     for k in range(4):
-        wq_pair(k).wait_send()
-        wo_pair(k).wait_send()
-        kv_pair(k).wait_send()
-
-
-def front(x_in, gain1, wqkv, wout, table, small, doc_row, doc_col, choice, grad_out, collective_id):
+        for copy in (wq_pair, wo_pair, kv_pair):
+            copy(k).wait_send()
+
+
+def front(x_in, gain1, wq, wk, wv, wout, table, wr, gain2, doc_row, choice_row, grad_out, w_hidden, w_back,
+          collective_id):
     local, features = x_in.shape
-    width = wqkv.shape[0]
-    cols = wqkv.shape[1] // 3
+    width, cols = wq.shape
     hd = 2 * cols
     heads = hd // HSIZE
-    experts = table.shape[0] if False else EXPERTS
-    tokens = 32 * local
+    experts = wr.shape[1]
+    tokens = choice_row.shape[1]
+    capacity = tokens * 5 // (4 * experts)
+    units = w_hidden.shape[1] // experts
     vm = pl.BlockSpec(memory_space=pltpu.VMEM)
     sm = pl.BlockSpec(memory_space=pltpu.SMEM)
+    hbm = pl.BlockSpec(memory_space=pl.ANY)
     dma = pltpu.SemaphoreType.DMA
     shape = jax.ShapeDtypeStruct
+    V = pltpu.VMEM
+    ring = 12
     return pl.pallas_call(
-        functools.partial(front_kernel, heads, experts),
+        functools.partial(front_kernel, heads, experts, capacity),
         out_shape=(
-            shape((32, local, 2 * width), bf16),
+            shape((32, local, width + 64), bf16),
+            shape((1, tokens), jnp.int32),
+            shape((experts, width, units), bf16),
+            shape((experts, width, units), bf16),
+            shape((experts, capacity, units), bf16),
+            shape((experts, capacity, width), bf16),
             shape((local, features), f32),
             shape((local, features), f32),
             shape((local, experts), f32),
@@ -994,33 +1246,37 @@
             shape((4, local, features), bf16),
             shape((features, 3 * hd), bf16),
             shape((features, features), bf16),
-            shape((small.shape[0], features), f32),
-            shape((heads, local, 16 * local), f32),
+            shape((experts + 8, features), f32),
         ),
-        in_specs=[vm, vm, vm, vm, sm, vm, vm, vm, vm, vm],
-        out_specs=(vm,) * 14,
+        in_specs=[vm] * 6 + [sm] + [vm] * 5 + [hbm] * 2,
+        out_specs=(vm, vm, hbm, hbm) + (vm,) * 14,
         scratch_shapes=[
-            pltpu.VMEM((2, 4, width, 3 * cols), bf16),
-            pltpu.VMEM((8, 4, cols, width), bf16),
-            pltpu.VMEM((4, *small.shape), f32),
-            pltpu.VMEM((4, local, hd), bf16),
-            pltpu.VMEM((4, local, 2 * width), bf16),
-        ] + [dma((n,)) for n in (3, 3, 3, 3, 4, 4, 3, 3, 3, 3, 3, 3, 4, 4, 4, 4, 3, 3, 3, 3)]
-        + [dma((4, 3)), dma((4, 3)), dma((4, 4)), dma((4, 4))],
+            V((heads, local, 16 * local), f32),
+            V((experts, width, units), bf16),
+            V((4, width, 1024), bf16), V((8, width, 512), bf16), V((1024, 1024), bf16), V((512, 512), bf16),
+            V((8, 4, width, 128), bf16),
+            V((32, local, width), bf16), V((4, local, width), bf16),
+            V((ring, capacity, units), bf16), V((experts, capacity, units), bf16),
+            V((2, 4, width, 3 * cols), bf16), V((8, 4, cols, width), bf16), V((4, experts + 8, width), f32),
+            V((4, local, hd), bf16), V((4, local, width + 64), bf16),
+            dma((4,)), dma((8,)), dma((1,)), dma((ring,)), dma((experts,)), dma((experts,)), dma((experts,)),
+        ] + [dma((n,)) for n in (3, 3, 3, 3, 4, 4, 3, 3, 3, 3, 3, 3, 4, 4, 4, 4, 3, 3, 3, 3, 3, 3)]
+        + [dma((4, 3)), dma((4, 3)), dma((4, 4)), dma((4, 4))] * 2,
         compiler_params=pltpu.CompilerParams(
-            collective_id=collective_id, has_side_effects=True, vmem_limit_bytes=60 * 2**20),
+            collective_id=collective_id, has_side_effects=True, vmem_limit_bytes=62 * 2**20),
         cost_estimate=pl.CostEstimate(flops=4 * 10**9, bytes_accessed=20 * 10**6, transcendentals=2 * 10**6),
-    )(x_in, gain1, wqkv, wout, table, small, doc_row, doc_col, choice, grad_out)
+    )(x_in, gain1, wq, wk, wv, wout, table, wr, gain2, doc_row, choice_row, grad_out, w_hidden, w_back)
 
 
 HIGH = lax.Precision.HIGHEST
 
 
 def back_kernel(heads, experts,
-                x_ref, gain1_ref, grad_ref, choice_ref, doc_row, doc_col,
+                x_ref, gain1_ref, grad_ref, choice_row, doc_row, table_ref,
                 hidden_ref, normed_ref, router_ref, gate_ref, at_ref, q_ref, kv_ref, lse_ref, xn_ref,
-                wqkv_all, wout_all, small_all, bias_ref, ret_ref,
+                wqkv_all, wout_all, small_all, ret_ref,
                 out_ref, gin_ref, wgrad_ref, ograd_ref, small_out, tail_out,
+                bias_ref,
                 ag_ref, dq_ref, dk_ref, dv_ref, near_ref, go_ref, fg_ref, top_ref,
                 sp_out, sp_in, sc_out, sc_in, sz_out, sz_in,
                 kv_out, kv_in, kv_sum, fg_out, fg_in, wp_out, wp_in, wz_out, wz_in,
@@ -1043,7 +1299,9 @@
     out_ref[...] = hidden + gate * routed
     gate_grad = jnp.sum(grads * routed, axis=-1, keepdims=True)
     router = router_ref[...]
-    picked = (choice_ref[...] == lax.broadcasted_iota(jnp.int32, router.shape, 1)).astype(f32)
+    own_tokens = pl.ds(pl.multiple_of((gx * 8 + gy) * local, local), local)
+    picked = (as_column(choice_row[:, own_tokens])
+              == lax.broadcasted_iota(jnp.int32, router.shape, 1).astype(f32)).astype(f32)
     logit_grad = router * (gate_grad * picked - gate * gate_grad)
     second = back + jnp.dot(logit_grad, small_all[:experts, :], precision=HIGH, preferred_element_type=f32)
     gained = second * small_all[experts:experts + 1, :]
@@ -1058,6 +1316,8 @@
     for k in range(3):
         ag_plane(k).start()
 
+    fill_bias(bias_ref, table_ref, chip, heads)
+
     routed_grad = lax.dot_general(logit_grad, normed_ref[...], (((0,), (0,)), ((), ())), precision=HIGH,
                                   preferred_element_type=f32)
     norm2 = jnp.sum(second * hidden * r2, axis=0, keepdims=True)
@@ -1081,7 +1341,7 @@
 
     def attend_block(c):
         block_at = 2 * c + core
-        allowed = doc_col[pl.ds(pl.multiple_of(block_at * local, local), local), :] == doc_row[...]
+        allowed = allowed_pairs(doc_row, block_at, local)
         keys = kv_ref[:, :, :hd].reshape(seq, hd)
         values = kv_ref[:, :, hd:].reshape(seq, hd)
         rows_out = pl.ds(pl.multiple_of(chip * hd, 16), hd)
@@ -1171,7 +1431,6 @@
         fg_out[c] = fg_ref[c].astype(bf16)
     for k in range(3):
         fg_plane(k).start()
-    weight_grad = jnp.zeros((features, 3 * hd), f32)
     weight_grad = tn(xn_ref[...].reshape(4 * local, features), jnp.concatenate(made, axis=0))
     halves = [jnp.concatenate([weight_grad[:, n * hd + j * cols:n * hd + (j + 1) * cols] for n in range(3)], axis=1)
               for j in range(2)]
@@ -1267,16 +1526,17 @@
             copy(k).wait_send()
 
 
-def back_pass(x_in, gain1, grad_out, choice, doc_row, doc_col, saved, returned, collective_id):
+def back_pass(x_in, gain1, grad_out, choice_row, doc_row, table, saved, returned, collective_id):
     local, features = x_in.shape
     width = features // 4
-    hidden, normed, router, gate, attended, queries, keyvals, lse, xn, wqkv, wout, small, bias = saved
+    hidden, normed, router, gate, attended, queries, keyvals, lse, xn, wqkv, wout, small = saved
     hd = queries.shape[2]
     cols = hd // 2
     heads = hd // HSIZE
     seq = 8 * local
     rows = small.shape[0]
     vm = pl.BlockSpec(memory_space=pltpu.VMEM)
+    sm = pl.BlockSpec(memory_space=pltpu.SMEM)
     dma = pltpu.SemaphoreType.DMA
     shape = jax.ShapeDtypeStruct
     V = pltpu.VMEM
@@ -1290,9 +1550,10 @@
             shape((rows, width), f32),
             shape((40, 128), f32),
         ),
-        in_specs=[vm] * 20,
+        in_specs=[vm] * 5 + [sm] + [vm] * 13,
         out_specs=(vm,) * 6,
         scratch_shapes=[
+            V((heads, local, 16 * local), f32),
             V((4, local, features), bf16), V((4, local, hd), bf16), V((hd, seq), f32), V((hd, seq), f32),
             V((heads, local, 2 * seq), f32), V((hd, features), f32), V((4, local, features), f32),
             V((EXPERTS, 3 * local), f32),
@@ -1309,27 +1570,88 @@
         compiler_params=pltpu.CompilerParams(
             collective_id=collective_id, has_side_effects=True, vmem_limit_bytes=60 * 2**20),
         cost_estimate=pl.CostEstimate(flops=6 * 10**9, bytes_accessed=20 * 10**6, transcendentals=2 * 10**6),
-    )(x_in, gain1, grad_out, choice, doc_row, doc_col, hidden, normed, router, gate, attended, queries, keyvals, lse, xn,
-      wqkv, wout, small, bias, returned)
+    )(x_in, gain1, grad_out, choice_row, doc_row, table, hidden, normed, router, gate, attended, queries, keyvals, lse, xn,
+      wqkv, wout, small, returned)
+
+
+def finish_kernel(heads, experts,
+                  out_ref, gin_ref, wgrad_ref, ograd_ref, small_ref, tail_ref, gh_hbm, gb_hbm,
+                  out_to, gin_to, norm1_to, query_to, key_to, value_to, table_to, proj_to, norm2_to, router_to,
+                  hidden_to, back_to,
+                  one_ref, two_ref, in_ref, half_ref, nat_ref, in_sem, nat_sem):
+    width, cols = query_to.shape
+    spans = gh_hbm.shape[2] // 128
+
+    def load(source, g, slot):
+        at = source.at[:, :, pl.ds(pl.multiple_of(g * 128, 128), 128)]
+        return pltpu.make_async_copy(at, in_ref.at[slot], in_sem.at[slot])
+
+    def store(target, g, q):
+        at = target.at[:, pl.ds(pl.multiple_of(g * 4096 + q * 1024, 1024), 1024)]
+        return pltpu.make_async_copy(nat_ref.at[q], at, nat_sem.at[q])
+
+    work = [(gh_hbm, hidden_to, g) for g in range(spans)] + [(gb_hbm, back_to, g) for g in range(spans)]
+    load(work[0][0], work[0][2], 0).start()
+    fill_moves(one_ref, two_ref, False)
+    for i, (source, target, g) in enumerate(work):
+        slot = i % 2
+        if i + 1 < len(work):
+            load(work[i + 1][0], work[i + 1][2], 1 - slot).start()
+        load(source, g, slot).wait()
+        for r in range(8):
+            block = jnp.concatenate([in_ref[slot, 4 * r + n] for n in range(4)], axis=1)
+            moved = nn(block, two_ref[...]).astype(bf16)
+            for q in range(4):
+                half_ref[q, :, r * 128:(r + 1) * 128] = moved[:, q * 128:(q + 1) * 128]
+        for q in range(4):
+            if i > 0:
+                store(work[i - 1][1], work[i - 1][2], q).wait()
+            nat_ref[q] = nn(half_ref[q], one_ref[...])
+            store(target, g, q).start()
+    out_to[...] = out_ref[...]
+    gin_to[...] = gin_ref[...]
+    for n in range(6):
+        norm1_to[:, n * 128:(n + 1) * 128] = tail_ref[experts + n:experts + n + 1, :]
+    query_to[...] = wgrad_ref[:, :cols]
+    key_to[...] = wgrad_ref[:, cols:2 * cols]
+    value_to[...] = wgrad_ref[:, 2 * cols:]
+    table_to[...] = tail_ref[:experts, :heads]
+    proj_to[...] = ograd_ref[...]
+    norm2_to[...] = small_ref[experts:experts + 1, :]
+    router_to[...] = jnp.transpose(small_ref[...])[:, :experts]
+    for q in range(4):
+        store(work[-1][1], work[-1][2], q).wait()
+
+
+def finish(out_rows, gin, wgrad, ograd, small, tail, gh, gb, heads):
+    experts, width, units = gh.shape
+    features = out_rows.shape[1]
+    cols = wgrad.shape[1] // 3
+    vm = pl.BlockSpec(memory_space=pltpu.VMEM)
+    hbm = pl.BlockSpec(memory_space=pl.ANY)
+    dma = pltpu.SemaphoreType.DMA
+    shape = lambda *dims: jax.ShapeDtypeStruct(dims, f32)
+    V = pltpu.VMEM
+    return pl.pallas_call(
+        functools.partial(finish_kernel, heads, experts),
+        out_shape=(
+            shape(*out_rows.shape), shape(*gin.shape), shape(1, features),
+            shape(width, cols), shape(width, cols), shape(width, cols), shape(experts, heads), shape(*ograd.shape),
+            shape(1, width), shape(width, experts), shape(width, experts * units), shape(width, experts * units),
+        ),
+        in_specs=[vm] * 6 + [hbm] * 2,
+        out_specs=(vm,) * 10 + (hbm,) * 2,
+        scratch_shapes=[
+            V((1024, 1024), bf16), V((512, 512), bf16), V((2, experts, width, 128), bf16), V((4, width, 1024), bf16),
+            V((4, width, 1024), f32), dma((2,)), dma((4,)),
+        ],
+        compiler_params=pltpu.CompilerParams(vmem_limit_bytes=48 * 2**20),
+        cost_estimate=pl.CostEstimate(flops=15 * 10**9, bytes_accessed=30 * 10**6, transcendentals=0),
+    )(out_rows, gin, wgrad, ograd, small, tail, gh, gb)
 
 
 def fits(mesh):
     return mesh.shape["gx"] == 4 and mesh.shape["gy"] == 8
-
-
-def expert_slots(expert_choice, experts, capacity):
-    all_tokens = expert_choice.shape[0]
-    tok_block = 128
-    chosen_rows = jnp.arange(experts, dtype=jnp.int32)[:, None] == expert_choice[None, :]
-    chosen_low = chosen_rows.astype(jnp.bfloat16).reshape(experts, all_tokens // tok_block, tok_block)
-    block_iota = jnp.arange(tok_block, dtype=jnp.int32)
-    upper = (block_iota[:, None] <= block_iota[None, :]).astype(jnp.bfloat16)
-    inside_count = jnp.einsum("ebi,ij->ebj", chosen_low, upper, preferred_element_type=jnp.float32)
-    block_totals = inside_count[:, :, tok_block - 1]
-    earlier_blocks = jnp.cumsum(block_totals, axis=1) - block_totals
-    counted = (inside_count + earlier_blocks[:, :, None]).reshape(experts, all_tokens)
-    position = (jnp.sum(jnp.where(chosen_rows, counted, 0.0), axis=0) - 1.0).astype(jnp.int32)
-    return jnp.where(position < capacity, expert_choice * capacity + position, -1)
 
 
 def fast(
@@ -1348,64 +1670,57 @@
     doc_ids,
     grad_out,
 ):
-    token_devs = lax.axis_size("gy")
-    member, column = lax.axis_index("gy"), lax.axis_index("gx")
-    local_count = x_in.shape[0]
-    width_cols, experts = w_router.shape
     all_tokens = expert_choice.shape[0]
-    capacity = all_tokens * 5 // (4 * experts)
-    head_cols = w_query.shape[1]
     gain_row = norm1_gain[None, :]
-    wqkv = jnp.concatenate([w_query, w_key, w_value], axis=1)
-    small = jnp.concatenate(
-        [w_router.T, norm2_gain[None, :], jnp.zeros((7, width_cols), jnp.float32)], axis=0
-    )
-    own_choice = lax.dynamic_slice_in_dim(
-        expert_choice, (column * token_devs + member) * local_count, local_count, 0
-    )[:, None]
-    doc_row, doc_col = doc_ids[None, :], doc_ids[:, None]
-    slot_all = expert_slots(expert_choice, experts, capacity)
-    hidden_weight = jnp.transpose(w_hidden.reshape(width_cols, -1, experts), (2, 0, 1))
-    back_weight = jnp.transpose(w_back.reshape(width_cols, -1, experts), (2, 0, 1))
-    rows, *saved = front(
+    choice_row, doc_row = expert_choice[None, :], doc_ids[None, :]
+    rows, slots, w1, w2, act_grads, slot_grads, *saved = front(
         x_in,
         gain_row,
-        wqkv,
+        w_query,
+        w_key,
+        w_value,
         w_out,
         relative_bias_table,
-        small,
+        w_router,
+        norm2_gain[None, :],
         doc_row,
-        doc_col,
-        own_choice,
+        choice_row,
         grad_out,
+        w_hidden,
+        w_back,
         2,
     )
     returned, hidden_grads, back_grads = moe(
-        rows.reshape(all_tokens, 2 * width_cols),
-        slot_all[None, :],
-        slot_all[:, None],
-        hidden_weight,
-        back_weight,
-        1,
-    )
-    grad_hidden = jnp.transpose(hidden_grads, (1, 2, 0)).reshape(width_cols, -1)
-    grad_back = jnp.transpose(back_grads, (1, 2, 0)).reshape(width_cols, -1)
-    out_rows, input_rows, weight_part, out_part, small_part, tail = back_pass(
-        x_in, gain_row, grad_out, own_choice, doc_row, doc_col, saved, returned, 3
-    )
-    heads = relative_bias_table.shape[1]
-    features = x_in.shape[1]
+        rows.reshape(all_tokens, rows.shape[2]), slots, w1, w2, slot_grads, act_grads, 1
+    )
+    results = back_pass(
+        x_in, gain_row, grad_out, choice_row, doc_row, relative_bias_table, saved, returned, 3
+    )
+    (
+        out_rows,
+        input_rows,
+        grad_norm1,
+        grad_query,
+        grad_key,
+        grad_value,
+        grad_table,
+        grad_out_proj,
+        grad_norm2,
+        grad_router,
+        grad_hidden,
+        grad_back,
+    ) = finish(*results, hidden_grads, back_grads, relative_bias_table.shape[1])
     return (
         out_rows,
         input_rows,
-        tail[experts : experts + features // 128].reshape(features),
-        weight_part[:, :head_cols],
-        weight_part[:, head_cols : 2 * head_cols],
-        weight_part[:, 2 * head_cols :],
-        tail[:experts, :heads],
-        out_part,
-        small_part[experts],
-        small_part[:experts].T,
+        grad_norm1[0],
+        grad_query,
+        grad_key,
+        grad_value,
+        grad_table,
+        grad_out_proj,
+        grad_norm2[0],
+        grad_router,
         grad_hidden,
         grad_back,
     )

time: 469 us -> 373 us (0.80)
  local copies, waits for them, and re-layouts: 99.2 us -> 13.2 us
  Pallas kernels: 360 us -> 355 us
  other arithmetic: 5.55 us -> 0.61 us
    pallas_call x1, Pallas kernels: 233 us -> 131 us  [moe(): pl.pallas_call(functools.partial(moe_kernel, experts, capacity, width, un...]
    pallas_call x1 -> x2, Pallas kernels: 71.3 us -> 168 us  [the longest x1 145 us: front(): pl.pallas_call(functools.partial(front_kernel, heads, experts, capacity),...]
    unnamed x17 -> x18, local copies, waits for them, and re-layouts: 43.2 us -> 11.9 us
    transpose x3 -> x0, local copies, waits for them, and re-layouts: 26.8 us -> none  [the longest x1 12.7 us: fast(): grad_hidden = jnp.transpose(hidden_grads, (1, 2, 0)).reshape(width_cols, -1)]
    reshape x3 -> x0, local copies, waits for them, and re-layouts: 18.6 us -> none  [the longest x1 8.68 us: fast(): w_back.reshape(width_cols, -1, experts)]
    broadcast_in_dim x5 -> x0, local copies, waits for them, and re-layouts: 5.2 us -> none  [the longest x1 1.97 us: fast(): slot_all[:, None]]
where the time goes in v3:
time: 373 us; the launch traced here: 369 us
  Pallas kernels  355 us (95%)
  local copies, waits for them, and re-layouts  13.2 us (4%)
    pallas_call x1, Pallas kernels, front(): pl.pallas_call(functools.partial(front_kernel, heads, experts, capacity),...  145 us
    pallas_call x1, Pallas kernels, moe(): pl.pallas_call(functools.partial(moe_kernel, experts, capacity, width, un...  131 us
    pallas_call x1, Pallas kernels, back_pass(): pl.pallas_call(functools.partial(back_kernel, heads, EXPERTS), out_shape=...  55.8 us
    pallas_call x1, Pallas kernels, finish(): pl.pallas_call(functools.partial(finish_kernel, heads, experts), out_shap...  23.3 us
    unnamed x18, local copies, waits for them, and re-layouts  11.9 us

profile of v3, /device:TPU:0, one launch (start us, length us, event | category | flops | bytes accessed | tf_op | source)
XLA Modules:
  0.0 369.5 jit_solution(11408771282060935985)
XLA Ops:
  0.6 1.3 broadcast_in_dim.12.gain1_ref
  1.9 1.4 copy.28.table_ref
  3.3 1.5 copy.27.wr_ref
  4.8 145.0 %shard_map.229 = (bf16[32,128,256]{2,1,0:T(8,128)(2,1)}, s32[1,4096]{1,0:T(1,128)}, bf16[32,192,384]{2,1,0:T(8,128)(2,1)}, bf16[32,192,384]{2,1,0:T(8,128)(2,1)}...) custom-call(bf16[128,768]{1,0:T(8,128)(2,1)} %x_ref.3, ...), custom_call_target="tpu_custom_call" | custom-call | flops 4000000000 | bytes 20000000 | tf_op jit(solution)/shard_map/pallas_call | solution.py:1229
  149.8 130.5 %shard_map.230 = (f32[4,128,384]{2,1,0:T(8,128)}, bf16[32,192,384]{2,1,0:T(8,128)(2,1)}, bf16[32,192,384]{2,1,0:T(8,128)(2,1)}) custom-call(bf16[4096,256]{1,0:T(8,128)(2,1)} %bitcast.10, s32[1,4096]{1,0:T(1,128)} %get-tuple-element.64.slot_row, bf16[32,192,384]{2,1,0:T(8,128)(2,1)} %get-tuple-element.65.w1_ref, ...), custom_call_target="tpu_custom_call" | custom-call | flops 20000000000 | bytes 50000000 | tf_op jit(solution)/shard_map/pallas_call | solution.py:789
  280.3 55.8 %shard_map.231 = (f32[128,768]{1,0:T(8,128)}, f32[128,768]{1,0:T(8,128)}, f32[192,288]{1,0:T(8,128)}, f32[96,192]{1,0:T(8,128)}, f32[40,192]{1,0:T(8,128)}, /*index=5*/f32[40,128]{1,0:T(8,128)}) custom-call(bf16[128,768]{1,0:T(8,128)(2,1)} %x_ref.3, f32[1,768]{1,0:T(1,128)} %broadcast_in_dim.12.gain1_ref, bf16[128,768]{1,0:T(8,128)(2,1)} %grad_ref.3, ...), custom_call_target="tpu_custom_call" | custom-call | flops 6000000000 | bytes 20000000 | tf_op jit(solution)/shard_map/pallas_call | solution.py:1543
  336.1 0.0 copy-start
  336.1 2.3 copy-done
  338.4 0.0 copy-start.1
  338.4 1.0 copy-done.1
  339.4 0.0 copy-start.2
  339.4 1.0 copy-done.2
  340.4 0.0 copy-start.3
  340.4 1.0 copy-done.3
  341.4 0.0 copy-start.4
  341.4 0.9 copy-done.4
  342.3 0.0 copy-start.5
  342.3 0.8 copy-done.5
  343.1 0.0 copy-start.6
  343.1 0.7 copy-done.6
  343.8 23.3 %shard_map.232 = (f32[128,768]{1,0:T(8,128)}, f32[128,768]{1,0:T(8,128)}, f32[1,768]{1,0:T(1,128)S(1)}, f32[192,96]{1,0:T(8,128)}, f32[192,96]{1,0:T(8,128)}, /*...) custom-call(f32[128,768]{1,0:T(8,128)S(1)} %copy-done.1, ...), custom_call_target="tpu_custom_call" | custom-call | flops 15000000512 | bytes 30000000 | tf_op jit(solution)/shard_map/pallas_call | solution.py:1635
  367.1 0.6 reduce
  367.7 0.7 copy.29
  368.4 0.7 copy.30
Async XLA Ops:
  336.1 2.3 copy-start
  338.4 1.0 copy-start.1
  339.4 1.0 copy-start.2
  340.4 1.0 copy-start.3
  341.4 0.9 copy-start.4
  342.3 0.8 copy-start.5
  343.1 0.7 copy-start.6

commit v4 on v0

--- a/solution.py
+++ b/solution.py
@@ -1,8 +1,11 @@
+import functools
 import math
 
 import jax
 import jax.numpy as jnp
 from jax import lax
+from jax.experimental import pallas as pl
+from jax.experimental.pallas import tpu as pltpu
 from jax.sharding import PartitionSpec as P
 
 D = 768
@@ -455,9 +458,1372 @@
     )
 
 
+MESH = pl.DeviceIdType.MESH
+GELU_C = math.sqrt(2.0 / math.pi)
+f32, bf16 = jnp.float32, jnp.bfloat16
+
+
+def nn(a, b):
+    return jnp.dot(a, b, preferred_element_type=f32)
+
+
+def nt(a, b):
+    return lax.dot_general(a, b, (((1,), (1,)), ((), ())), preferred_element_type=f32)
+
+
+def tn(a, b):
+    return lax.dot_general(a, b, (((0,), (0,)), ((), ())), preferred_element_type=f32)
+
+
+def remote(src, dst, send_sem, recv_sem, device):
+    return pltpu.make_async_remote_copy(
+        src_ref=src, dst_ref=dst, send_sem=send_sem, recv_sem=recv_sem,
+        device_id=device, device_id_type=MESH)
+
+
+class Place:
+    def __init__(self):
+        self.gx, self.gy = lax.axis_index("gx"), lax.axis_index("gy")
+        self.core, self.chip = lax.rem(self.gy, 2), self.gy // 2
+        self.pair = (self.gx, self.gy + 1 - 2 * self.core)
+        self.line = [lax.rem(self.gx + k, 4) for k in (1, 2, 3)]
+        self.chips = [lax.rem(self.chip + k, 4) for k in (1, 2, 3)]
+        self.line_from = [lax.rem(self.gx + 4 - k, 4) for k in (1, 2, 3)]
+        self.chips_from = [lax.rem(self.chip + 4 - k, 4) for k in (1, 2, 3)]
+        self.is_mid = jnp.logical_and(self.gx > 0, self.gx < 3)
+        self.is_end = jnp.logical_not(self.is_mid)
+        self.mid = (jnp.where(self.gx < 2, 1, 2), self.gy)
+        self.other_mid = (jnp.where(self.gx < 2, 2, 1), self.gy)
+        self.end = (jnp.where(self.gx < 2, 0, 3), self.gy)
+
+    def on_line(self, k):
+        return (self.line[k], self.gy)
+
+    def on_plane(self, k):
+        return (self.gx, 2 * self.chips[k] + self.core)
+
+    def greet_all(self):
+        devices = [self.on_line(k) for k in range(3)] + [self.on_plane(k) for k in range(3)] + [self.pair]
+        barrier = pltpu.get_barrier_semaphore()
+        for device in devices:
+            pl.semaphore_signal(barrier, inc=1, device_id=device, device_id_type=MESH)
+        pl.semaphore_wait(barrier, len(devices))
+
+
+def as_column(row):
+    n = row.shape[1]
+    same = lax.broadcasted_iota(jnp.int32, (n, n), 0) == lax.broadcasted_iota(jnp.int32, (n, n), 1)
+    return jnp.sum(jnp.where(same, row.astype(f32), 0.0), axis=1, keepdims=True)
+
+
+def pick_rows(slot_row, base, capacity, rows_ref, tokens):
+    kblock = 1024
+    ids = lax.broadcasted_iota(jnp.int32, (capacity, kblock), 0) + base
+    total = None
+    for kb in range(tokens // kblock):
+        hot = (slot_row[:, kb * kblock:(kb + 1) * kblock] == ids).astype(f32).astype(bf16)
+        part = nn(hot, rows_ref[kb * kblock:(kb + 1) * kblock, :])
+        total = part if total is None else total + part
+    return total
+
+
+class LineSum:
+    def __init__(self, me, own, got, other, own_sem, got_sem, other_sem, out_sem, experts):
+        self.me, self.own, self.got, self.other = me, own, got, other
+        self.sems = (own_sem, got_sem, other_sem, out_sem)
+        self.ring, self.experts = own.shape[0], experts
+
+    def to_mid(self, e):
+        sl = lax.rem(e, self.ring)
+        return remote(self.own.at[sl], self.got.at[e], self.sems[0].at[sl], self.sems[1].at[e], self.me.mid)
+
+    def across(self, e):
+        sl = lax.rem(e, self.ring)
+        return remote(self.own.at[sl], self.other.at[e], self.sems[0].at[sl], self.sems[2].at[e], self.me.other_mid)
+
+    def to_end(self, e):
+        return remote(self.got.at[e], self.got.at[e], self.sems[3].at[e], self.sems[1].at[e], self.me.end)
+
+    def slot_free(self, e):
+        @pl.when(e >= self.ring)
+        def _():
+            self.to_mid(e - self.ring).wait_send()
+
+    def put(self, e, value):
+        self.own[lax.rem(e, self.ring)] = value
+
+        @pl.when(self.me.is_end)
+        def _():
+            self.to_mid(e).start()
+
+    def half(self, e):
+        @pl.when(jnp.logical_and(self.me.is_mid, jnp.logical_and(e >= 0, e < self.experts)))
+        def _():
+            sl = lax.rem(e + self.ring, self.ring)
+            self.to_mid(e).wait_recv()
+            self.own[sl] = (self.own[sl].astype(f32) + self.got[e].astype(f32)).astype(bf16)
+            self.across(e).start()
+
+    def whole(self, e):
+        @pl.when(jnp.logical_and(self.me.is_mid, jnp.logical_and(e >= 0, e < self.experts)))
+        def _():
+            sl = lax.rem(e + self.ring, self.ring)
+            self.across(e).wait_recv()
+            self.got[e] = (self.own[sl].astype(f32) + self.other[e].astype(f32)).astype(bf16)
+            self.to_end(e).start()
+
+    def await_total(self, e):
+        @pl.when(self.me.is_end)
+        def _():
+            self.to_end(e).wait_recv()
+
+    def drain(self):
+        def sent(e, carry):
+            self.to_mid(e).wait_send()
+            return carry
+        lax.fori_loop(self.experts - self.ring, self.experts, sent, 0)
+
+        @pl.when(self.me.is_mid)
+        def _():
+            def out(e, carry):
+                self.to_end(e).wait_send()
+                return carry
+            lax.fori_loop(0, self.experts, out, 0)
+
+
+RING = 8
+GROUP = 4
+LAG_B, LAG_C, LAG_D = 2, 4, 6
+
+
+class LineGather:
+    def __init__(self, me, slot, right_s, right_r, left_s, left_r):
+        self.me, self.slot = me, slot
+        self.sems = (right_s, right_r, left_s, left_r)
+
+    def right(self, h):
+        at = self.slot(jnp.maximum(self.me.gx - h, 0))
+        return remote(at, at, self.sems[0].at[h], self.sems[1].at[h], (jnp.minimum(self.me.gx + 1, 3), self.me.gy))
+
+    def left(self, h):
+        at = self.slot(jnp.minimum(self.me.gx + h, 3))
+        return remote(at, at, self.sems[2].at[h], self.sems[3].at[h], (jnp.maximum(self.me.gx - 1, 0), self.me.gy))
+
+    def from_left(self, h):
+        at = self.slot(jnp.maximum(self.me.gx - 1 - h, 0))
+        return remote(at, at, self.sems[0].at[h], self.sems[1].at[h], (jnp.maximum(self.me.gx - 1, 0), self.me.gy))
+
+    def from_right(self, h):
+        at = self.slot(jnp.minimum(self.me.gx + 1 + h, 3))
+        return remote(at, at, self.sems[2].at[h], self.sems[3].at[h], (jnp.minimum(self.me.gx + 1, 3), self.me.gy))
+
+    def sends(self, h):
+        gx = self.me.gx
+        return jnp.logical_and(gx < 3, gx >= h), jnp.logical_and(gx > 0, gx + h <= 3)
+
+    def start(self):
+        self.pass_on(0)
+
+    def pass_on(self, h):
+        go_right, go_left = self.sends(h)
+
+        @pl.when(go_right)
+        def _():
+            self.right(h).start()
+
+        @pl.when(go_left)
+        def _():
+            self.left(h).start()
+
+    def receive(self, h):
+        @pl.when(self.me.gx >= h + 1)
+        def _():
+            self.from_left(h).wait_recv()
+
+        @pl.when(self.me.gx + h + 1 <= 3)
+        def _():
+            self.from_right(h).wait_recv()
+        if h < 2:
+            self.pass_on(h + 1)
+
+    def drain(self):
+        for h in range(3):
+            go_right, go_left = self.sends(h)
+
+            @pl.when(go_right)
+            def _():
+                self.right(h).wait_send()
+
+            @pl.when(go_left)
+            def _():
+                self.left(h).wait_send()
+
+
+def place_one(lane):
+    register, unit, expert = lane // 128, lax.rem(lane // 32, 4), lax.rem(lane, 32)
+    return expert // 4 * 128 + lax.rem(expert, 4) * 32 + register * 4 + unit
+
+
+def place_two(lane):
+    register, expert, unit = lane // 128, lax.rem(lane // 32, 4), lax.rem(lane, 32)
+    return expert * 128 + register * 32 + unit
+
+
+def fill_moves(one_ref, two_ref, inward):
+    for ref, place in ((one_ref, place_one), (two_ref, place_two)):
+        n = ref.shape[0]
+        if inward:
+            moved = place(lax.broadcasted_iota(jnp.int32, (n, 1), 0))
+            ref[...] = (moved == lax.broadcasted_iota(jnp.int32, (n, n), 1)).astype(f32).astype(bf16)
+        else:
+            moved = place(lax.broadcasted_iota(jnp.int32, (1, n), 1))
+            ref[...] = (moved == lax.broadcasted_iota(jnp.int32, (n, n), 0)).astype(f32).astype(bf16)
+
+
+def near_buckets(rows):
+    offset = (
+        lax.broadcasted_iota(jnp.int32, (rows, 3 * rows), 1)
+        - rows
+        - lax.broadcasted_iota(jnp.int32, (rows, 3 * rows), 0)
+    )
+    return bucket_ids(offset)
+
+
+def fill_bias(bias_ref, table_ref, chip, heads):
+    rows = bias_ref.shape[1]
+    span = bias_ref.shape[2]
+    mid = span // 2
+    buckets = near_buckets(rows)
+    for h in range(heads):
+        column = chip * heads + h
+        near = jnp.zeros(buckets.shape, f32)
+        for b in range(table_ref.shape[1]):
+            near = jnp.where(buckets == b, table_ref[column, b], near)
+        bias_ref[h, :, 0:mid - rows] = jnp.full((rows, mid - rows), table_ref[column, 15], f32)
+        bias_ref[h, :, mid - rows:mid + 2 * rows] = near
+        bias_ref[h, :, mid + 2 * rows:] = jnp.full((rows, span - mid - 2 * rows), table_ref[column, 31], f32)
+
+
+def allowed_pairs(doc_row, block_at, local):
+    start = pl.multiple_of(block_at * local, local)
+    return as_column(doc_row[:, pl.ds(start, local)]) == doc_row[...].astype(f32)
+
+
+def unit_scores(q_block, keys, bias_ref, h, block_at, allowed):
+    rows = q_block.shape[0]
+    seq = keys.shape[0]
+    lanes = lax.broadcasted_iota(jnp.int32, q_block.shape, 1) // HSIZE
+    masked = jnp.where(lanes == h, q_block, jnp.zeros_like(q_block))
+    start = pl.multiple_of(seq - rows * block_at, rows)
+    return jnp.where(allowed, nt(masked, keys) + bias_ref[h, :, pl.ds(start, seq)], -1000000000.0)
+
+
+def fill_slots(slot_ref, choice_row, experts, capacity):
+    tokens = choice_row.shape[1]
+    expert = lax.broadcasted_iota(jnp.int32, (experts, 128), 0)
+    upper = (lax.broadcasted_iota(jnp.int32, (128, 128), 0)
+             <= lax.broadcasted_iota(jnp.int32, (128, 128), 1)).astype(f32).astype(bf16)
+    before = jnp.zeros((experts, 1), f32)
+    for b in range(tokens // 128):
+        choice = choice_row[:, b * 128:(b + 1) * 128]
+        chosen = (expert == choice).astype(f32)
+        count = nn(chosen.astype(bf16), upper)
+        place = jnp.sum(chosen * (count + before), axis=0, keepdims=True).astype(jnp.int32) - 1
+        slot_ref[:, b * 128:(b + 1) * 128] = jnp.where(place < capacity, choice * capacity + place, -1)
+        before = before + count[:, 127:128]
+
+
+class BlockRows:
+    def __init__(self, ref):
+        self.ref = ref
+
+    def __getitem__(self, at):
+        rows = at[0]
+        size = self.ref.shape[1]
+        part = self.ref[rows.start // size:rows.stop // size]
+        return part.reshape(rows.stop - rows.start, self.ref.shape[2])
+
+
+class Dispatch:
+    def __init__(self, me, out, dst, line_s, line_r, plane_s, plane_r, pair_s, pair_r):
+        self.me, self.out, self.dst = me, out, dst
+        self.sems = (line_s, line_r, plane_s, plane_r, pair_s, pair_r)
+        self.zs = [me.gx] + me.line_from
+
+    def line(self, k):
+        at = self.dst.at[self.me.gx * 8 + self.me.gy]
+        return remote(self.out.at[self.me.line[k]], at, self.sems[0].at[k], self.sems[1].at[k], self.me.on_line(k))
+
+    def plane(self, m, k):
+        at = self.dst.at[self.zs[m] * 8 + self.me.gy]
+        return remote(at, at, self.sems[2].at[m, k], self.sems[3].at[m, k], self.me.on_plane(k))
+
+    def pair(self, m, k):
+        c = self.me.chip if k == 0 else self.me.chips_from[k - 1]
+        at = self.dst.at[self.zs[m] * 8 + 2 * c + self.me.core]
+        return remote(at, at, self.sems[4].at[m, k], self.sems[5].at[m, k], self.me.pair)
+
+    def start(self):
+        for k in range(3):
+            self.line(k).start()
+
+    def spread(self, m):
+        if m > 0:
+            self.line(m - 1).wait_recv()
+        for k in range(3):
+            self.plane(m, k).start()
+        self.pair(m, 0).start()
+
+    def share(self, m):
+        for k in range(3):
+            self.plane(m, k).wait_recv()
+            self.pair(m, k + 1).start()
+
+    def arrive(self):
+        for m in range(4):
+            for k in range(4):
+                self.pair(m, k).wait_recv()
+
+    def drain(self):
+        for m in range(4):
+            for k in range(4):
+                self.pair(m, k).wait_send()
+            for k in range(3):
+                self.plane(m, k).wait_send()
+        for k in range(3):
+            self.line(k).wait_send()
+
+
+def forward_kernel(heads, experts, capacity,
+                   x_ref, gain1_ref, wq_ref, wk_ref, wv_ref, wout_ref, table_ref, wr_ref, gain2_ref, doc_row,
+                   choice_row, grad_ref, wh_hbm, wb_hbm,
+                   out_ref, gh_hbm, gb_hbm,
+                   hidden_ref, normed_ref, router_ref, gate_ref, at_ref, q_ref, kv_ref, lse_ref, xb_ref,
+                   wqkv_all, wout_all, small_all,
+                   slot_ref, w1_ref, w2_ref, g_ref, g_out, rows_ref, rows_out, gs_ref,
+                   own_ref, ag_ref, other_ref, xs_ref, p_ref, got_ref, other2_ref,
+                   wq_st, wo_st, sm_st, at_in, y_in, s_in, line_out, line_in,
+                   nat_sem, own_sem, got_sem, other_sem, t_sem, p_sem, got2_sem, other2_sem, t2_sem, gh_sem, gb_sem,
+                   wqr_s, wqr_r, wql_s, wql_r, smr_s, smr_r, sml_s, sml_r,
+                   xb_s, xb_r, wqp_s, wqp_r, woc_s, woc_r, wop_s, wop_r, kv_s, kv_r, at_s, at_r,
+                   gz_s, gz_r, rz_s, rz_r, lo_s, lo_r, gc_s, gc_r, gp_s, gp_r, rc_s, rc_r, rp_s, rp_r,
+                   yo_s, yo_r, so_s, so_r, ya_s, ya_r, yp_s, yp_r):
+    me = Place()
+    gx, gy, core, chip = me.gx, me.gy, me.core, me.chip
+    width, cols = wq_ref.shape
+    local = x_ref.shape[0]
+    tokens = 32 * local
+    units = wh_hbm.shape[1] // experts
+    hd = 2 * cols
+    seq = 8 * local
+    zs = [gx] + me.line_from
+    spans = units // 128
+    scale = HSIZE ** (-0.5)
+    half = capacity // 2
+    groups = experts // GROUP
+    yt_ref = other_ref
+
+    give = Dispatch(me, g_out, g_ref, gz_s, gz_r, gc_s, gc_r, gp_s, gp_r)
+    rows = Dispatch(me, rows_out, rows_ref, rz_s, rz_r, rc_s, rc_r, rp_s, rp_r)
+    acts = LineSum(me, own_ref, ag_ref, other_ref, own_sem, got_sem, other_sem, t_sem, experts)
+    pres = LineSum(me, p_ref, got_ref, other2_ref, p_sem, got2_sem, other2_sem, t2_sem, experts)
+    weights = LineGather(me, lambda z: wq_st.at[core, z], wqr_s, wqr_r, wql_s, wql_r)
+    smalls = LineGather(me, lambda z: sm_st.at[z], smr_s, smr_r, sml_s, sml_r)
+
+    def act_step(i, carry):
+        @pl.when(i < experts)
+        def _():
+            acts.slot_free(i)
+            gs = pick_rows(slot_ref, i * capacity, capacity, BlockRows(g_ref), tokens).astype(bf16)
+            gs_ref[i] = gs
+            acts.put(i, nn(gs, w2_ref[i]).astype(bf16))
+        acts.half(i - LAG_B)
+        acts.whole(i - LAG_C)
+        return carry
+
+    done = [0]
+
+    def act_steps(count):
+        lax.fori_loop(done[0], done[0] + count, act_step, 0)
+        done[0] += count
+
+    def xb_plane(k):
+        return remote(xb_ref.at[chip], xb_ref.at[chip], xb_s.at[k], xb_r.at[k], me.on_plane(k))
+
+    def wq_pair(k):
+        at = wq_st.at[core, zs[k]]
+        return remote(at, at, wqp_s.at[k], wqp_r.at[k], me.pair)
+
+    def wo_plane(k):
+        return remote(wo_st.at[gy], wo_st.at[gy], woc_s.at[k], woc_r.at[k], me.on_plane(k))
+
+    def wo_pair(k):
+        c = me.chips_from[k]
+        return remote(wo_st.at[2 * c + core], wo_st.at[2 * c + core], wop_s.at[k], wop_r.at[k], me.pair)
+
+    def kv_pair(c):
+        return remote(kv_ref.at[2 * c + core], kv_ref.at[2 * c + core], kv_s.at[c], kv_r.at[c], me.pair)
+
+    def at_plane(k):
+        return remote(at_ref.at[me.chips[k]], at_in.at[chip], at_s.at[k], at_r.at[k], me.on_plane(k))
+
+    barrier = pltpu.get_barrier_semaphore()
+    friends = [me.on_line(k) for k in range(3)] + [me.on_plane(k) for k in range(3)] + [me.pair]
+    for device in friends:
+        pl.semaphore_signal(barrier, inc=1, device_id=device, device_id_type=MESH)
+
+    for z in range(4):
+        g_out[z] = grad_ref[:, z * width:(z + 1) * width]
+    xb_ref[chip] = x_ref[...]
+    wq_st[core, gx] = jnp.concatenate(
+        [wq_ref[...], wk_ref[...], wv_ref[...], jnp.transpose(wout_ref[...].astype(f32)).astype(bf16)], axis=1)
+    sm_st[gx] = jnp.concatenate([wr_ref[...], gain2_ref[...], jnp.zeros((7, width), f32)], axis=0)
+    g_ref[gx * 8 + gy] = g_out[gx]
+    pl.semaphore_wait(barrier, len(friends))
+    give.start()
+    weights.start()
+    give.spread(0)
+    for k in range(3):
+        xb_plane(k).start()
+    wq_pair(0).start()
+    smalls.start()
+
+    def front(bias_ref, nat_ref, half_ref, one_ref, two_ref):
+        def load_span(source, g, q):
+            at = source.at[:, pl.ds(pl.multiple_of(g * 4096 + q * 1024, 1024), 1024)]
+            return pltpu.make_async_copy(at, nat_ref.at[q], nat_sem.at[q])
+
+        def load_spans(source, g):
+            for q in range(4):
+                load_span(source, g, q).start()
+
+        def turn_span(source, target, g, following):
+            lanes = pl.ds(pl.multiple_of(g * 128, 128), 128)
+            for q in range(4):
+                load_span(source, g, q).wait()
+                moved = nn(nat_ref[q], one_ref[...]).astype(bf16)
+                for r in range(8):
+                    half_ref[r, :, q * 128:(q + 1) * 128] = moved[:, r * 128:(r + 1) * 128]
+            following()
+            for r in range(8):
+                moved = nn(half_ref[r], two_ref[...]).astype(bf16)
+                for n in range(4):
+                    target[4 * r + n, :, lanes] = moved[:, n * 128:(n + 1) * 128]
+
+        load_spans(wb_hbm, 0)
+        fill_moves(one_ref, two_ref, True)
+        fill_slots(slot_ref, choice_row, experts, capacity)
+        fill_bias(bias_ref, table_ref, chip, heads)
+        for m in (1, 2, 3):
+            give.spread(m)
+        for h in range(3):
+            weights.receive(h)
+            smalls.receive(h)
+
+        def back_body(g, carry):
+            def following():
+                @pl.when(g + 1 < spans)
+                def _():
+                    load_spans(wb_hbm, g + 1)
+            turn_span(wb_hbm, w2_ref, g, following)
+            return carry
+        lax.fori_loop(0, spans, back_body, 0)
+        load_spans(wh_hbm, 0)
+        for k in (1, 2, 3):
+            wq_pair(k).start()
+        for z in range(4):
+            wo_st[gy, z] = wq_st[core, z][:, 3 * cols:]
+        for k in range(3):
+            wo_plane(k).start()
+        for m in range(4):
+            give.share(m)
+        give.arrive()
+        act_steps(4)
+        for k in range(4):
+            wq_pair(k).wait_recv()
+        for z in range(4):
+            parts = [wq_st[0, z], wq_st[1, z]]
+            wqkv_all[z * width:(z + 1) * width, :] = jnp.concatenate(
+                [parts[j][:, n * cols:(n + 1) * cols] for n in range(3) for j in range(2)], axis=1)
+            wo_st[gy + 1 - 2 * core, z] = wq_st[1 - core, z][:, 3 * cols:]
+
+        for k in range(4):
+            c = chip if k == 0 else me.chips_from[k - 1]
+            if k > 0:
+                xb_plane(k - 1).wait_recv()
+            xc = xb_ref[c].astype(f32)
+            r1 = lax.rsqrt(jnp.mean(xc * xc, axis=-1, keepdims=True) + epsilon)
+            xn = (xc * r1 * gain1_ref[...]).astype(bf16)
+            made = nn(xn, wqkv_all[...])
+            q_ref[c] = (made[:, :hd].astype(bf16).astype(f32) * scale).astype(bf16)
+            kv_ref[2 * c + core] = made[:, hd:].astype(bf16)
+            kv_pair(c).start()
+        for k in range(3):
+            wo_plane(k).wait_recv()
+            wo_pair(k).start()
+        act_steps(2)
+        for c in range(4):
+            kv_pair(c).wait_recv()
+        lanes = lax.broadcasted_iota(jnp.int32, (local, hd), 1) // HSIZE
+        for k in range(4):
+            c = me.chips[k] if k < 3 else chip
+            block_at = 2 * c + core
+            allowed = allowed_pairs(doc_row, block_at, local)
+            keys = kv_ref[:, :, :hd].reshape(seq, hd)
+            values = kv_ref[:, :, hd:].reshape(seq, hd)
+            total = jnp.zeros((local, hd), f32)
+            for h in range(heads):
+                scores = unit_scores(q_ref[c], keys, bias_ref, h, block_at, allowed)
+                peak = jnp.max(scores, axis=-1, keepdims=True)
+                shifted = jnp.exp(scores - peak)
+                summed = jnp.sum(shifted, axis=-1, keepdims=True)
+                lse_ref[c, h] = jnp.broadcast_to(peak + jnp.log(summed), (local, 128))
+                low = (shifted * (1.0 / summed)).astype(bf16)
+                total = jnp.where(lanes == h, nn(low, values), total)
+            at_ref[c] = total.astype(bf16)
+            if k < 3:
+                at_plane(k).start()
+            else:
+                at_in[chip] = total.astype(bf16)
+            act_steps(3)
+        small_all[...] = jnp.concatenate([sm_st[z] for z in range(4)], axis=1)
+        for k in range(3):
+            wo_pair(k).wait_recv()
+        for z in range(4):
+            wout_all[z * width:(z + 1) * width, :] = jnp.concatenate([wo_st[g, z] for g in range(8)], axis=1)
+        for k in range(3):
+            at_plane(k).wait_recv()
+        attended = jnp.concatenate([at_in[c] for c in range(4)], axis=1)
+        hidden = x_ref[...].astype(f32) + nt(attended, wout_all[...]).astype(bf16).astype(f32)
+        hidden_ref[...] = hidden
+        r2 = lax.rsqrt(jnp.mean(hidden * hidden, axis=-1, keepdims=True) + epsilon)
+        normed = hidden * r2 * small_all[experts:experts + 1, :]
+        normed_ref[...] = normed
+        logits = lax.dot_general(normed, small_all[:experts, :], (((1,), (1,)), ((), ())),
+                                 precision=lax.Precision.HIGHEST, preferred_element_type=f32)
+        lifted = jnp.exp(logits - jnp.max(logits, axis=-1, keepdims=True))
+        router = lifted / jnp.sum(lifted, axis=-1, keepdims=True)
+        router_ref[...] = router
+        own_tokens = pl.ds(pl.multiple_of((gx * 8 + gy) * local, local), local)
+        picked = as_column(choice_row[:, own_tokens]) == lax.broadcasted_iota(jnp.int32, router.shape, 1).astype(f32)
+        gate = jnp.sum(jnp.where(picked, router, 0.0), axis=-1, keepdims=True)
+        gate_ref[...] = gate
+        first = gate.astype(bf16).astype(f32)
+        second = (gate - first).astype(bf16).astype(f32)
+        third = gate - first - second
+        lane = lax.broadcasted_iota(jnp.int32, (local, 64), 1)
+        pieces = jnp.where(lane == 0, first, jnp.where(lane == 1, second, jnp.where(lane == 2, third, 0.0)))
+        pieces = pieces.astype(bf16)
+        low = normed.astype(bf16)
+        for z in range(4):
+            rows_out[z] = jnp.concatenate([low[:, z * width:(z + 1) * width], pieces], axis=1)
+        rows.start()
+        rows_ref[gx * 8 + gy] = rows_out[gx]
+        rows.spread(0)
+        act_steps(2)
+        turn_span(wh_hbm, w1_ref, 0, lambda: load_spans(wh_hbm, 1))
+        for m in (1, 2, 3):
+            rows.spread(m)
+        act_steps(2)
+        for n in range(1, spans):
+            turn_span(wh_hbm, w1_ref, n, lambda: load_spans(wh_hbm, n + 1) if n + 1 < spans else None)
+            act_steps(1)
+        for m in range(4):
+            rows.share(m)
+        act_steps(1)
+        rows.arrive()
+
+    V = pltpu.VMEM
+    pl.run_scoped(front, V((heads, local, 16 * local), f32), V((4, width, 1024), bf16), V((8, width, 512), bf16),
+                  V((1024, 1024), bf16), V((512, 512), bf16))
+    first_left = done[0]
+    per_step = -(-(experts + LAG_C - first_left) // LAG_D)
+
+    def experts_part(y_own, y_out, s_out, gh_st, gb_st):
+        def grad_copy(stage, target, sems, e):
+            return pltpu.make_async_copy(stage.at[lax.rem(e, 2)], target.at[e], sems.at[lax.rem(e, 2)])
+
+        def pair_half(j):
+            return remote(y_out.at[j], y_in.at[j], yo_s.at[j], yo_r.at[j], me.pair)
+
+        def to_owner(j, k):
+            return remote(s_out.at[j, me.chips[k]], s_in.at[j, k], so_s.at[j, k], so_r.at[j, k], me.on_plane(k))
+
+        own_half = pl.ds(pl.multiple_of(core * half, 16), half)
+
+        def from_owner(j, k):
+            at = yt_ref.at[j * GROUP + chip, own_half]
+            return remote(at, at, ya_s.at[j, k], ya_r.at[j, k], me.on_plane(k))
+
+        def pair_total(j, k):
+            c = chip if k == 0 else me.chips_from[k - 1]
+            at = yt_ref.at[j * GROUP + c, own_half]
+            return remote(at, at, yp_s.at[j, k], yp_r.at[j, k], me.pair)
+
+        def stage_two(j):
+            pair_half(j).wait_recv()
+            for m in range(GROUP):
+                s_out[j, m] = (y_own[j, m].astype(f32) + y_in[j, m].astype(f32)).astype(bf16)
+            for k in range(3):
+                to_owner(j, k).start()
+
+        def stage_three(j):
+            total = s_out[j, chip].astype(f32)
+            for k in range(3):
+                to_owner(j, k).wait_recv()
+                total = total + s_in[j, k].astype(f32)
+            yt_ref[j * GROUP + chip, own_half] = total.astype(bf16)
+            for k in range(3):
+                from_owner(j, k).start()
+            pair_total(j, 0).start()
+
+        def stage_four(j):
+            for k in range(3):
+                from_owner(j, k).wait_recv()
+                pair_total(j, k + 1).start()
+
+        def step(i, carry):
+            @pl.when(i < LAG_D)
+            def _():
+                for n in range(per_step):
+                    act_step(first_left + per_step * i + n, 0)
+
+            @pl.when(i < experts)
+            def _():
+                pres.slot_free(i)
+                xs = pick_rows(slot_ref, i * capacity, capacity, BlockRows(rows_ref), tokens).astype(bf16)
+                xs_ref[lax.rem(i, RING)] = xs
+                pres.put(i, nn(xs[:, :width], w1_ref[i]).astype(bf16))
+            pres.half(i - LAG_B)
+            pres.whole(i - LAG_C)
+            e = i - LAG_D
+
+            @pl.when(e >= 0)
+            def _():
+                acts.await_total(e)
+                pres.await_total(e)
+                xs = xs_ref[lax.rem(e, RING)]
+                pieces = xs[:, width:].astype(f32)
+                gate = pieces[:, 0:1] + pieces[:, 1:2] + pieces[:, 2:3]
+                u = got_ref[e].astype(f32)
+                ag = gate * ag_ref[e].astype(f32)
+                u2 = u * u
+                th = jnp.tanh(GELU_C * (u + 0.044715 * (u2 * u)))
+                part = 0.5 * (1.0 + th)
+                act = (u * part).astype(bf16)
+                dg = part + 0.5 * u * (1.0 - th * th) * (GELU_C * (1.0 + 3 * 0.044715 * u2))
+                pg = (ag * dg).astype(bf16)
+                y = jnp.concatenate([nt(act, w2_ref[e]), nt(pg, w1_ref[e])], axis=1).astype(bf16)
+                j, m = e // GROUP, lax.rem(e, GROUP)
+
+                @pl.when(core == 0)
+                def _():
+                    y_own[j, m] = y[:half]
+                    y_out[j, m] = y[half:]
+
+                @pl.when(core == 1)
+                def _():
+                    y_own[j, m] = y[half:]
+                    y_out[j, m] = y[:half]
+
+                @pl.when(m == GROUP - 1)
+                def _():
+                    pair_half(j).start()
+
+                @pl.when(e >= 2)
+                def _():
+                    grad_copy(gh_st, gh_hbm, gh_sem, e - 2).wait()
+                    grad_copy(gb_st, gb_hbm, gb_sem, e - 2).wait()
+                slot_grad = (gate * gs_ref[e].astype(f32)).astype(bf16)
+                gh_st[lax.rem(e, 2)] = tn(xs[:, :width], pg).astype(bf16)
+                gb_st[lax.rem(e, 2)] = tn(slot_grad, act).astype(bf16)
+                grad_copy(gh_st, gh_hbm, gh_sem, e).start()
+                grad_copy(gb_st, gb_hbm, gb_sem, e).start()
+
+                @pl.when(jnp.logical_and(m == 0, j >= 1))
+                def _():
+                    stage_two(j - 1)
+
+                @pl.when(jnp.logical_and(m == 2, j >= 1))
+                def _():
+                    stage_three(j - 1)
+
+                @pl.when(jnp.logical_and(m == 1, j >= 2))
+                def _():
+                    stage_four(j - 2)
+            return carry
+
+        lax.fori_loop(0, experts + LAG_D, step, 0)
+        last = groups - 1
+        stage_two(last)
+        stage_four(last - 1)
+        slots = [as_column(slot_ref[:, pl.ds(pl.multiple_of((z * 8 + gy) * 128, 128), 128)]) for z in range(4)]
+        own_slots = jnp.concatenate(slots, axis=0).astype(jnp.int32)
+        many = 8
+        per = many // GROUP
+        places = lax.broadcasted_iota(jnp.int32, (own_slots.shape[0], many * capacity), 1)
+
+        def picked(b):
+            hot = (own_slots == places + b * many * capacity).astype(f32).astype(bf16)
+            return nn(hot, yt_ref[b * many:(b + 1) * many].reshape(many * capacity, 2 * width))
+
+        total = None
+        for b in range(experts // many - 1):
+            for j in range(b * per, (b + 1) * per):
+                for k in range(4):
+                    pair_total(j, k).wait_recv()
+            if b == 0:
+                stage_three(last)
+            part = picked(b)
+            total = part if total is None else total + part
+        stage_four(last)
+        for j in range(groups - per, groups):
+            for k in range(4):
+                pair_total(j, k).wait_recv()
+        total = total + picked(experts // many - 1)
+
+        def line_copy(k):
+            return remote(line_out.at[me.line[k]], line_in.at[k], lo_s.at[k], lo_r.at[k], me.on_line(k))
+
+        for z in range(4):
+            line_out[z] = total[z * local:(z + 1) * local].astype(bf16)
+        for k in range(3):
+            line_copy(k).start()
+        out_ref[gx] = line_out[gx].astype(f32)
+        acts.drain()
+        pres.drain()
+        for e in (experts - 2, experts - 1):
+            grad_copy(gh_st, gh_hbm, gh_sem, e).wait()
+            grad_copy(gb_st, gb_hbm, gb_sem, e).wait()
+
+        def sent(j, carry):
+            pair_half(j).wait_send()
+            for k in range(3):
+                to_owner(j, k).wait_send()
+                from_owner(j, k).wait_send()
+            for k in range(4):
+                pair_total(j, k).wait_send()
+            return carry
+        lax.fori_loop(0, groups, sent, 0)
+        give.drain()
+        rows.drain()
+        weights.drain()
+        smalls.drain()
+        for k in range(3):
+            for copy in (xb_plane, wo_plane, wo_pair, at_plane):
+                copy(k).wait_send()
+        for k in range(4):
+            for copy in (wq_pair, kv_pair):
+                copy(k).wait_send()
+        for k in range(3):
+            line_copy(k).wait_recv()
+            out_ref[me.line_from[k]] = line_in[k].astype(f32)
+        for k in range(3):
+            line_copy(k).wait_send()
+
+    block = (groups, GROUP, half, 2 * width)
+    pl.run_scoped(experts_part, V(block, bf16), V(block, bf16), V(block, bf16),
+                  V((2, width, units), bf16), V((2, width, units), bf16))
+
+
+def forward_pass(x_in, gain1, wq, wk, wv, wout, table, wr, gain2, doc_row, choice_row, grad_out, w_hidden, w_back,
+                 collective_id):
+    local, features = x_in.shape
+    width, cols = wq.shape
+    hd = 2 * cols
+    heads = hd // HSIZE
+    experts = wr.shape[0]
+    tokens = choice_row.shape[1]
+    capacity = tokens * 5 // (4 * experts)
+    units = w_hidden.shape[1] // experts
+    half = capacity // 2
+    groups = experts // GROUP
+    vm = pl.BlockSpec(memory_space=pltpu.VMEM)
+    sm = pl.BlockSpec(memory_space=pltpu.SMEM)
+    hbm = pl.BlockSpec(memory_space=pl.ANY)
+    dma = pltpu.SemaphoreType.DMA
+    shape = jax.ShapeDtypeStruct
+    V = pltpu.VMEM
+    ring = 8
+    return pl.pallas_call(
+        functools.partial(forward_kernel, heads, experts, capacity),
+        out_shape=(
+            shape((4, local, 2 * width), f32),
+            shape((experts, width, units), bf16),
+            shape((experts, width, units), bf16),
+            shape((local, features), f32),
+            shape((local, features), f32),
+            shape((local, experts), f32),
+            shape((local, 1), f32),
+            shape((4, local, hd), bf16),
+            shape((4, local, hd), bf16),
+            shape((8, local, 2 * hd), bf16),
+            shape((4, heads, local, 128), f32),
+            shape((4, local, features), bf16),
+            shape((features, 3 * hd), bf16),
+            shape((features, features), bf16),
+            shape((experts + 8, features), f32),
+        ),
+        in_specs=[vm] * 6 + [sm] + [vm] * 5 + [hbm] * 2,
+        out_specs=(vm, hbm, hbm) + (vm,) * 12,
+        scratch_shapes=[
+            V((1, tokens), jnp.int32),
+            V((experts, width, units), bf16), V((experts, width, units), bf16),
+            V((32, local, width), bf16), V((4, local, width), bf16),
+            V((32, local, width + 64), bf16), V((4, local, width + 64), bf16),
+            V((experts, capacity, width), bf16),
+            V((ring, capacity, units), bf16), V((experts, capacity, units), bf16), V((experts, capacity, units), bf16),
+            V((RING, capacity, width + 64), bf16),
+            V((RING, capacity, units), bf16), V((experts, capacity, units), bf16), V((experts, capacity, units), bf16),
+            V((2, 4, width, 4 * cols), bf16), V((8, 4, width, cols), bf16), V((4, experts + 8, width), f32),
+            V((4, local, hd), bf16),
+            V((groups, GROUP, half, 2 * width), bf16), V((groups, 3, half, 2 * width), bf16),
+            V((4, local, 2 * width), bf16), V((3, local, 2 * width), bf16),
+        ] + [dma((n,)) for n in (4, ring, experts, experts, experts, RING, experts, experts, experts, 2, 2)]
+        + [dma((3,))] * 8
+        + [dma((n,)) for n in (3, 3, 4, 4, 3, 3, 3, 3, 4, 4, 3, 3, 3, 3, 3, 3, 3, 3)]
+        + [dma((4, 3)), dma((4, 3)), dma((4, 4)), dma((4, 4))] * 2
+        + [dma((groups,)), dma((groups,)), dma((groups, 3)), dma((groups, 3)), dma((groups, 3)), dma((groups, 3)),
+           dma((groups, 4)), dma((groups, 4))],
+        compiler_params=pltpu.CompilerParams(
+            collective_id=collective_id, has_side_effects=True, vmem_limit_bytes=64 * 2**20),
+        cost_estimate=pl.CostEstimate(flops=25 * 10**9, bytes_accessed=50 * 10**6, transcendentals=4 * 10**6),
+    )(x_in, gain1, wq, wk, wv, wout, table, wr, gain2, doc_row, choice_row, grad_out, w_hidden, w_back)
+
+
+HIGH = lax.Precision.HIGHEST
+
+
+def back_kernel(heads, experts,
+                x_ref, gain1_ref, grad_ref, choice_row, doc_row, table_ref,
+                hidden_ref, normed_ref, router_ref, gate_ref, at_ref, q_ref, kv_ref, lse_ref, xb_ref,
+                wqkv_all, wout_all, small_all, ret_ref, gh_hbm, gb_hbm,
+                out_ref, gin_ref, wgrad_ref, small_out, tail_out, nh_hbm, nb_hbm,
+                bias_ref, ag_ref, dq_ref, dk_ref, dv_ref, near_ref, go_ref, fg_ref, top_ref,
+                one_ref, two_ref, in_ref, half_ref, nat_ref,
+                sp_out, sp_in, sc_out, sc_in, sz_out, sz_in,
+                kv_out, kv_in, kv_sum, fg_out, fg_in, wp_out, wp_in, wz_out, wz_in,
+                tp_out, tp_in, tc_out, tc_in, tz_out, tz_in,
+                in_sem, nat_sem,
+                ag_s, ag_r, sp_s, sp_r, sc_s, sc_r, sz_s, sz_r, kv_s, kv_r, fg_s, fg_r, wp_s, wp_r,
+                tp_s, tp_r, tc_s, tc_r, tz_s, tz_r, wz_s, wz_r):
+    me = Place()
+    gx, gy, core, chip = me.gx, me.gy, me.core, me.chip
+    local, features = x_ref.shape
+    width = features // 4
+    hd = q_ref.shape[2]
+    cols = hd // 2
+    seq = 8 * local
+    spans = gh_hbm.shape[2] // 128
+
+    barrier = pltpu.get_barrier_semaphore()
+    friends = [me.on_line(k) for k in range(3)] + [me.on_plane(k) for k in range(3)] + [me.pair]
+    for device in friends:
+        pl.semaphore_signal(barrier, inc=1, device_id=device, device_id_type=MESH)
+
+    work = [(gh_hbm, nh_hbm, g) for g in range(spans)] + [(gb_hbm, nb_hbm, g) for g in range(spans)]
+
+    def load(i):
+        at = work[i][0].at[:, :, work[i][2] * 128:(work[i][2] + 1) * 128]
+        return pltpu.make_async_copy(at, in_ref, in_sem.at[0])
+
+    def store(i, q):
+        at = work[i][1].at[:, work[i][2] * 4096 + q * 1024:work[i][2] * 4096 + (q + 1) * 1024]
+        return pltpu.make_async_copy(nat_ref.at[q], at, nat_sem.at[q])
+
+    def turn_span(i):
+        load(i).wait()
+        for r in range(8):
+            block = jnp.concatenate([in_ref[4 * r + n] for n in range(4)], axis=1)
+            moved = nn(block, two_ref[...]).astype(bf16)
+            for q in range(4):
+                half_ref[q, :, r * 128:(r + 1) * 128] = moved[:, q * 128:(q + 1) * 128]
+        if i + 1 < len(work):
+            load(i + 1).start()
+        for q in range(4):
+            if i > 0:
+                store(i - 1, q).wait()
+            nat_ref[q] = nn(half_ref[q], one_ref[...]).astype(bf16)
+            store(i, q).start()
+
+    load(0).start()
+    hidden = hidden_ref[...]
+    r2 = lax.rsqrt(jnp.mean(hidden * hidden, axis=-1, keepdims=True) + epsilon)
+    grads = grad_ref[...].astype(f32)
+    gate = gate_ref[...]
+    routed = jnp.concatenate([ret_ref[z][:, :width] for z in range(4)], axis=1)
+    back = jnp.concatenate([ret_ref[z][:, width:] for z in range(4)], axis=1)
+    out_ref[...] = hidden + gate * routed
+    gate_grad = jnp.sum(grads * routed, axis=-1, keepdims=True)
+    router = router_ref[...]
+    own_tokens = pl.ds(pl.multiple_of((gx * 8 + gy) * local, local), local)
+    picked = (as_column(choice_row[:, own_tokens])
+              == lax.broadcasted_iota(jnp.int32, router.shape, 1).astype(f32)).astype(f32)
+    logit_grad = router * (gate_grad * picked - gate * gate_grad)
+    second = back + jnp.dot(logit_grad, small_all[:experts, :], precision=HIGH, preferred_element_type=f32)
+    gained = second * small_all[experts:experts + 1, :]
+    dot2 = jnp.sum(gained * hidden, axis=-1, keepdims=True)
+    hidden_grad = grads + r2 * gained - hidden * (r2 * r2 * r2) * (dot2 / features)
+    gin_ref[...] = hidden_grad
+    ag_ref[chip] = hidden_grad.astype(bf16)
+    pl.semaphore_wait(barrier, len(friends))
+
+    def ag_plane(k):
+        return remote(ag_ref.at[chip], ag_ref.at[chip], ag_s.at[k], ag_r.at[k], me.on_plane(k))
+
+    for k in range(3):
+        ag_plane(k).start()
+
+    routed_grad = lax.dot_general(logit_grad, normed_ref[...], (((0,), (0,)), ((), ())), precision=HIGH,
+                                  preferred_element_type=f32)
+    norm2 = jnp.sum(second * hidden * r2, axis=0, keepdims=True)
+    sp_out[...] = jnp.concatenate([routed_grad, norm2, jnp.zeros((7, features), f32)], axis=0)
+    small_pair = remote(sp_out, sp_in, sp_s.at[0], sp_r.at[0], me.pair)
+    small_pair.start()
+
+    def small_plane(k):
+        return remote(sc_out, sc_in.at[k], sc_s.at[k], sc_r.at[k], me.on_plane(k))
+
+    def small_line(k):
+        return remote(sz_out.at[me.line[k]], sz_in.at[k], sz_s.at[k], sz_r.at[k], me.on_line(k))
+
+    fill_bias(bias_ref, table_ref, chip, heads)
+    dk_ref[...] = jnp.zeros_like(dk_ref)
+    dv_ref[...] = jnp.zeros_like(dv_ref)
+    near_ref[...] = jnp.zeros_like(near_ref)
+    scale = HSIZE ** (-0.5)
+    lanes = lax.broadcasted_iota(jnp.int32, (local, hd), 1) // HSIZE
+
+    def attend_block(c, fresh):
+        block_at = 2 * c + core
+        allowed = allowed_pairs(doc_row, block_at, local)
+        keys = kv_ref[:, :, :hd].reshape(seq, hd)
+        values = kv_ref[:, :, hd:].reshape(seq, hd)
+        att_grad = nn(ag_ref[c], wout_own).astype(bf16)
+        part_o = tn(at_ref[c], ag_ref[c])
+        go_ref[...] = part_o if fresh else go_ref[...] + part_o
+        q_block = q_ref[c]
+        q_turn = jnp.transpose(q_block.astype(f32)).astype(bf16)
+        g_turn = jnp.transpose(att_grad.astype(f32)).astype(bf16)
+        dq = jnp.zeros((local, hd), f32)
+        for h in range(heads):
+            scores = unit_scores(q_block, keys, bias_ref, h, block_at, allowed)
+            probs = jnp.exp(scores - lse_ref[c, h][:, :1])
+            masked = jnp.where(lanes == h, att_grad, jnp.zeros_like(att_grad))
+            prob_grad = nt(masked, values)
+            weighted = probs * prob_grad
+            score_grad = (weighted - probs * jnp.sum(weighted, axis=-1, keepdims=True)).astype(bf16)
+            part = slice(h * HSIZE, (h + 1) * HSIZE)
+            dv_ref[part, :] += nn(g_turn[part, :], probs.astype(bf16))
+            dk_ref[part, :] += nn(q_turn[part, :], score_grad)
+            dq = jnp.where(lanes == h, nn(score_grad, keys), dq)
+            start = pl.multiple_of(seq - local * block_at, local)
+            near_ref[h, :, pl.ds(start, seq)] += score_grad.astype(f32)
+        dq_ref[c] = (dq * scale).astype(bf16)
+
+    own_pieces = [wout_all[:, n * hd:(n + 1) * hd] for n in range(4)]
+    wout_own = own_pieces[3]
+    for n in range(3):
+        wout_own = jnp.where(chip == n, own_pieces[n], wout_own)
+
+    attend_block(chip, True)
+    small_pair.wait_recv()
+    sc_out[...] = sp_out[...] + sp_in[...]
+    for k in range(3):
+        small_plane(k).start()
+    fill_moves(one_ref, two_ref, False)
+    for k in range(3):
+        ag_plane(k).wait_recv()
+        attend_block(me.chips_from[k], False)
+        if k == 0:
+            total = sc_out[...]
+            for j in range(3):
+                small_plane(j).wait_recv()
+                total = total + sc_in[j]
+            for z in range(4):
+                sz_out[z] = total[:, z * width:(z + 1) * width]
+            for j in range(3):
+                small_line(j).start()
+
+    both = jnp.concatenate([dk_ref[...], dv_ref[...]], axis=0)
+    for j in range(8):
+        turned = jnp.transpose(both[:, j * local:(j + 1) * local])
+
+        @pl.when(core == j % 2)
+        def _():
+            kv_sum[j // 2] = turned
+
+        @pl.when(core != j % 2)
+        def _():
+            kv_out[j // 2] = turned.astype(bf16)
+    kv_pair = remote(kv_out, kv_in, kv_s.at[0], kv_r.at[0], me.pair)
+    kv_pair.start()
+
+    def xn_block(c):
+        xc = xb_ref[c].astype(f32)
+        return xc * lax.rsqrt(jnp.mean(xc * xc, axis=-1, keepdims=True) + epsilon)
+
+    xr = [xn_block(c) for c in range(4)]
+    xn = jnp.concatenate([(v * gain1_ref[...]).astype(bf16) for v in xr], axis=0)
+
+    def packed(value, z):
+        top, mid, bottom = z * width, z * width + width // 2, (z + 1) * width
+        return jnp.concatenate([value[top:mid], value[mid:bottom]], axis=1)
+
+    def w_pair(p):
+        return remote(wp_out.at[p], wp_in.at[p], wp_s.at[p], wp_r.at[p], me.pair)
+
+    def w_line(p, k):
+        return remote(wz_out.at[p, me.line[k]], wz_in.at[p, k], wz_s.at[p, k], wz_r.at[p, k], me.on_line(k))
+
+    def weight_part(p, a, b):
+        halves = [jnp.concatenate([a[:, j * cols:(j + 1) * cols], b[:, j * cols:(j + 1) * cols]], axis=1)
+                  for j in range(2)]
+        other = jnp.where(core == 0, halves[1], halves[0]).astype(bf16)
+        own = jnp.where(core == 0, halves[0], halves[1])
+        for z in range(4):
+            wp_out[p, z] = packed(other, z)
+        w_pair(p).start()
+        return own
+
+    def weight_line(p, own):
+        w_pair(p).wait_recv()
+        for z in range(4):
+            wz_out[p, z] = (packed(own, z) + wp_in[p, z].astype(f32)).astype(bf16)
+        for k in range(3):
+            w_line(p, k).start()
+
+    queries = jnp.concatenate([dq_ref[c] for c in range(4)], axis=0)
+    own_0 = weight_part(0, tn(xn, queries), jnp.transpose(go_ref[...]))
+    kv_pair.wait_recv()
+    keyval = [(kv_sum[c] + kv_in[c].astype(f32)).astype(bf16) for c in range(4)]
+
+    def fg_plane(k):
+        return remote(fg_out.at[me.chips[k]], fg_in.at[k], fg_s.at[k], fg_r.at[k], me.on_plane(k))
+
+    norm1 = jnp.zeros((1, features), f32)
+    for k in range(4):
+        c = me.chips[k] if k < 3 else chip
+        both = jnp.concatenate([dq_ref[c], (kv_sum[c] + kv_in[c].astype(f32)).astype(bf16)], axis=1)
+        part = nt(both, wqkv_all[...])
+        xc = xb_ref[c].astype(f32)
+        r1 = lax.rsqrt(jnp.mean(xc * xc, axis=-1, keepdims=True) + epsilon)
+        norm1 = norm1 + jnp.sum(part * (xc * r1), axis=0, keepdims=True)
+        if k < 3:
+            fg_out[c] = part.astype(bf16)
+            fg_plane(k).start()
+        else:
+            fg_ref[...] = part
+    weight_line(0, own_0)
+
+    buckets = near_buckets(local)
+    table = jnp.zeros((experts, 128), f32)
+    lane = lax.broadcasted_iota(jnp.int32, (experts, 128), 1)
+    row = lax.broadcasted_iota(jnp.int32, (experts, 1), 0)
+    for h in range(heads):
+        close = near_ref[h, :, seq - local:seq + 2 * local]
+        for b in range(experts):
+            top_ref[b:b + 1, :] = jnp.sum(jnp.where(buckets == b, close, 0.0), axis=0, keepdims=True)
+        column = jnp.sum(top_ref[...], axis=1, keepdims=True)
+        left = jnp.sum(near_ref[h, :, :seq - local])
+        right = jnp.sum(near_ref[h, :, seq + 2 * local:])
+        column = column + jnp.where(row == 15, left, 0.0) + jnp.where(row == 31, right, 0.0)
+        table = jnp.where(lane == chip * heads + h, column, table)
+
+    tp_out[...] = jnp.concatenate(
+        [table] + [norm1[:, n * 128:(n + 1) * 128] for n in range(6)] + [jnp.zeros((2, 128), f32)], axis=0)
+    t_pair = remote(tp_out, tp_in, tp_s.at[0], tp_r.at[0], me.pair)
+    t_pair.start()
+
+    def t_plane(k):
+        return remote(tc_out, tc_in.at[k], tc_s.at[k], tc_r.at[k], me.on_plane(k))
+
+    def t_line(k):
+        return remote(tz_out, tz_in.at[k], tz_s.at[k], tz_r.at[k], me.on_line(k))
+
+    keyvals = jnp.concatenate(keyval, axis=0)
+    grads_kv = tn(xn, keyvals)
+    own_1 = weight_part(1, grads_kv[:, :hd], grads_kv[:, hd:])
+    t_pair.wait_recv()
+    tc_out[...] = tp_out[...] + tp_in[...]
+    for k in range(3):
+        t_plane(k).start()
+    weight_line(1, own_1)
+    turn_span(0)
+    turn_span(1)
+    for k in range(3):
+        t_plane(k).wait_recv()
+    tail = jnp.zeros((40, 128), f32)
+    for c in range(4):
+        part = jnp.where(chip == c, tc_out[...], 0.0)
+        for k in range(3):
+            part = jnp.where(me.chips_from[k] == c, tc_in[k], part)
+        tail = tail + part
+    tz_out[...] = tail
+    for k in range(3):
+        t_line(k).start()
+    turn_span(2)
+    turn_span(3)
+
+    first = fg_ref[...]
+    for k in range(3):
+        fg_plane(k).wait_recv()
+        first = first + fg_in[k].astype(f32)
+    x = x_ref[...].astype(f32)
+    r1 = lax.rsqrt(jnp.mean(x * x, axis=-1, keepdims=True) + epsilon)
+    gained1 = first * gain1_ref[...]
+    dot1 = jnp.sum(gained1 * x, axis=-1, keepdims=True)
+    gin_ref[...] = gin_ref[...] + r1 * gained1 - x * (r1 * r1 * r1) * (dot1 / features)
+
+    total = sz_out[gx]
+    for k in range(3):
+        small_line(k).wait_recv()
+        total = total + sz_in[k]
+    small_out[...] = total
+    turn_span(4)
+    turn_span(5)
+    for p in range(2):
+        total = wz_out[p, gx].astype(f32)
+        for k in range(3):
+            w_line(p, k).wait_recv()
+            total = total + wz_in[p, k].astype(f32)
+        wgrad_ref[p] = total
+    for k in range(3):
+        t_line(k).wait_recv()
+    tail = jnp.zeros((40, 128), f32)
+    for z in range(4):
+        part = jnp.where(gx == z, tz_out[...], 0.0)
+        for k in range(3):
+            part = jnp.where(me.line_from[k] == z, tz_in[k], part)
+        tail = tail + part
+    tail_out[...] = tail
+    for q in range(4):
+        store(len(work) - 1, q).wait()
+    for copy in (small_pair, kv_pair, t_pair):
+        copy.wait_send()
+    for p in range(2):
+        w_pair(p).wait_send()
+        for k in range(3):
+            w_line(p, k).wait_send()
+    for k in range(3):
+        for copy in (ag_plane, small_plane, small_line, fg_plane, t_plane, t_line):
+            copy(k).wait_send()
+
+
+def back_pass(x_in, gain1, grad_out, choice_row, doc_row, table, saved, returned, gh, gb, collective_id):
+    local, features = x_in.shape
+    width = features // 4
+    hidden, normed, router, gate, attended, queries, keyvals, lse, xb, wqkv, wout, small = saved
+    experts, _, units = gh.shape
+    hd = queries.shape[2]
+    cols = hd // 2
+    heads = hd // HSIZE
+    seq = 8 * local
+    rows = small.shape[0]
+    vm = pl.BlockSpec(memory_space=pltpu.VMEM)
+    sm = pl.BlockSpec(memory_space=pltpu.SMEM)
+    hbm = pl.BlockSpec(memory_space=pl.ANY)
+    dma = pltpu.SemaphoreType.DMA
+    shape = jax.ShapeDtypeStruct
+    V = pltpu.VMEM
+    return pl.pallas_call(
+        functools.partial(back_kernel, heads, experts),
+        out_shape=(
+            shape((local, features), f32),
+            shape((local, features), f32),
+            shape((2, width // 2, 4 * cols), f32),
+            shape((rows, width), f32),
+            shape((40, 128), f32),
+            shape((width, experts * units), bf16),
+            shape((width, experts * units), bf16),
+        ),
+        in_specs=[vm] * 5 + [sm] + [vm] * 13 + [hbm] * 2,
+        out_specs=(vm,) * 5 + (hbm,) * 2,
+        scratch_shapes=[
+            V((heads, local, 16 * local), f32),
+            V((4, local, features), bf16), V((4, local, hd), bf16), V((hd, seq), f32), V((hd, seq), f32),
+            V((heads, local, 2 * seq), f32), V((hd, features), f32), V((local, features), f32),
+            V((experts, 3 * local), f32),
+            V((1024, 1024), bf16), V((512, 512), bf16), V((experts, width, 128), bf16), V((4, width, 1024), bf16),
+            V((4, width, 1024), bf16),
+            V((rows, features), f32), V((rows, features), f32), V((rows, features), f32), V((3, rows, features), f32),
+            V((4, rows, width), f32), V((3, rows, width), f32),
+            V((4, local, 2 * hd), bf16), V((4, local, 2 * hd), bf16), V((4, local, 2 * hd), f32),
+            V((4, local, features), bf16), V((3, local, features), bf16),
+            V((2, 4, width // 2, 4 * cols), bf16), V((2, 4, width // 2, 4 * cols), bf16),
+            V((2, 4, width // 2, 4 * cols), bf16), V((2, 3, width // 2, 4 * cols), bf16),
+            V((40, 128), f32), V((40, 128), f32), V((40, 128), f32), V((3, 40, 128), f32),
+            V((40, 128), f32), V((3, 40, 128), f32),
+        ] + [dma((n,)) for n in (1, 4, 3, 3, 1, 1, 3, 3, 3, 3, 1, 1, 3, 3, 2, 2, 1, 1, 3, 3, 3, 3)]
+        + [dma((2, 3)), dma((2, 3))],
+        compiler_params=pltpu.CompilerParams(
+            collective_id=collective_id, has_side_effects=True, vmem_limit_bytes=62 * 2**20),
+        cost_estimate=pl.CostEstimate(flops=20 * 10**9, bytes_accessed=40 * 10**6, transcendentals=2 * 10**6),
+    )(x_in, gain1, grad_out, choice_row, doc_row, table, hidden, normed, router, gate, attended, queries, keyvals, lse,
+      xb, wqkv, wout, small, returned, gh, gb)
+
+
+def finish_kernel(heads, experts,
+                  out_ref, gin_ref, wgrad_ref, small_ref, tail_ref, nh_hbm, nb_hbm,
+                  out_to, gin_to, norm1_to, query_to, key_to, value_to, table_to, proj_to, norm2_to, router_to,
+                  hidden_to, back_to,
+                  in_ref, nat_ref, in_sem, nat_sem):
+    width, cols = query_to.shape
+    span = in_ref.shape[2]
+    count = nh_hbm.shape[1] // span
+    work = [(nh_hbm, hidden_to, g) for g in range(count)] + [(nb_hbm, back_to, g) for g in range(count)]
+    ring = in_ref.shape[0]
+
+    def load(i):
+        source, _, g = work[i]
+        return pltpu.make_async_copy(source.at[:, g * span:(g + 1) * span], in_ref.at[i % ring], in_sem.at[i % ring])
+
+    def store(i):
+        _, target, g = work[i]
+        return pltpu.make_async_copy(nat_ref.at[i % ring], target.at[:, g * span:(g + 1) * span], nat_sem.at[i % ring])
+
+    for i in range(ring):
+        load(i).start()
+    out_to[...] = out_ref[...]
+    gin_to[...] = gin_ref[...]
+    for n in range(6):
+        norm1_to[:, n * 128:(n + 1) * 128] = tail_ref[experts + n:experts + n + 1, :]
+    parts = []
+    for p in range(2):
+        rows = wgrad_ref[p]
+        parts.append(jnp.concatenate([rows[:, :2 * cols], rows[:, 2 * cols:]], axis=0))
+    query_to[...] = parts[0][:, :cols]
+    proj_to[...] = jnp.transpose(parts[0])[cols:]
+    key_to[...] = parts[1][:, :cols]
+    value_to[...] = parts[1][:, cols:]
+    table_to[...] = jnp.transpose(jnp.concatenate([tail_ref[:experts, :], jnp.zeros((128 - experts, 128), f32)], axis=0)
+                                  )[:heads, :experts]
+    norm2_to[...] = small_ref[experts:experts + 1, :]
+    router_to[...] = small_ref[:experts, :]
+    for i in range(len(work)):
+        load(i).wait()
+        if i >= ring:
+            store(i - ring).wait()
+        nat_ref[i % ring] = in_ref[i % ring].astype(f32)
+        store(i).start()
+        if i + ring < len(work):
+            load(i + ring).start()
+    for i in range(len(work) - ring, len(work)):
+        store(i).wait()
+
+
+def finish(out_rows, gin, wgrad, small, tail, nh, nb, heads):
+    width, natural = nh.shape
+    local, features = out_rows.shape
+    cols = wgrad.shape[2] // 4
+    experts = EXPERTS
+    vm = pl.BlockSpec(memory_space=pltpu.VMEM)
+    hbm = pl.BlockSpec(memory_space=pl.ANY)
+    dma = pltpu.SemaphoreType.DMA
+    shape = lambda *dims: jax.ShapeDtypeStruct(dims, f32)
+    V = pltpu.VMEM
+    ring, span = 4, 2048
+    return pl.pallas_call(
+        functools.partial(finish_kernel, heads, experts),
+        out_shape=(
+            shape(local, features), shape(local, features), shape(1, features),
+            shape(width, cols), shape(width, cols), shape(width, cols), shape(heads, experts), shape(cols, width),
+            shape(1, width), shape(experts, width), shape(width, natural), shape(width, natural),
+        ),
+        in_specs=[vm] * 5 + [hbm] * 2,
+        out_specs=(vm,) * 10 + (hbm,) * 2,
+        scratch_shapes=[V((ring, width, span), bf16), V((ring, width, span), f32), dma((ring,)), dma((ring,))],
+        compiler_params=pltpu.CompilerParams(vmem_limit_bytes=63 * 2**20),
+        cost_estimate=pl.CostEstimate(flops=10**7, bytes_accessed=30 * 10**6, transcendentals=0),
+    )(out_rows, gin, wgrad, small, tail, nh, nb)
+
+
+def fits(mesh):
+    return mesh.shape["gx"] == 4 and mesh.shape["gy"] == 8
+
+
+def fast(
+    x_in,
+    norm1_gain,
+    w_query,
+    w_key,
+    w_value,
+    relative_bias_table,
+    w_out,
+    norm2_gain,
+    w_router,
+    w_hidden,
+    w_back,
+    expert_choice,
+    doc_ids,
+    grad_out,
+):
+    gain_row = norm1_gain[None, :]
+    choice_row, doc_row = expert_choice[None, :], doc_ids[None, :]
+    table = relative_bias_table.T
+    returned, hidden_grads, back_grads, *saved = forward_pass(
+        x_in,
+        gain_row,
+        w_query,
+        w_key,
+        w_value,
+        w_out,
+        table,
+        w_router.T,
+        norm2_gain[None, :],
+        doc_row,
+        choice_row,
+        grad_out,
+        w_hidden,
+        w_back,
+        1,
+    )
+    results = back_pass(
+        x_in,
+        gain_row,
+        grad_out,
+        choice_row,
+        doc_row,
+        table,
+        saved,
+        returned,
+        hidden_grads,
+        back_grads,
+        2,
+    )
+    (
+        out_rows,
+        input_rows,
+        grad_norm1,
+        grad_query,
+        grad_key,
+        grad_value,
+        grad_table,
+        grad_out_proj,
+        grad_norm2,
+        grad_router,
+        grad_hidden,
+        grad_back,
+    ) = finish(*results, table.shape[0])
+    return (
+        out_rows,
+        input_rows,
+        grad_norm1[0],
+        grad_query,
+        grad_key,
+        grad_value,
+        grad_table.T,
+        grad_out_proj,
+        grad_norm2[0],
+        grad_router.T,
+        grad_hidden,
+        grad_back,
+    )
+
+
 def solution(mesh):
     return jax.shard_map(
-        local,
+        fast if fits(mesh) else local,
         mesh=mesh,
         in_specs=(
             P(("gx", "gy"), None),

time: 2610 us -> 340 us (0.13)
  local copies, waits for them, and re-layouts: 1200 us -> 1.27 us
  waiting for transfers between devices: 1090 us -> 0 us
  Pallas kernels: 0 us -> 332 us
  matrix products: 90.9 us -> 0 us
  blocking collectives: 73.2 us -> 0 us
  starting transfers between devices: 59.6 us -> 0 us
  other arithmetic: 57.6 us -> 1.29 us
    gather x10 -> x0, local copies, waits for them, and re-layouts: 996 us -> none  [the longest x2 879 us: local(): bias_terms = jnp.take(jnp.transpose(relative_bias_table), buckets, axis=1)]
    reduce_scatter x8 -> x0, waiting for transfers between devices: 628 us -> none  [the longest x2 252 us: width_sums(): lax.psum_scatter(term_fn(jnp.int32(0), lax.axis_size('gx') * row_number),...]
    pallas_call x0 -> x3, Pallas kernels: none -> 332 us  [the longest x1 259 us: forward_pass(): pl.pallas_call(functools.partial(forward_kernel, heads, experts, capacity...]
    all_gather x8 -> x0, waiting for transfers between devices: 256 us -> none  [the longest x2 97.3 us: width_rows(): return lax.all_gather(block_part, 'gx', axis=0, tiled=True)]
    ppermute x28 -> x0, waiting for transfers between devices: 151 us -> none  [passed_along(): lax.ppermute(value, axis, [(source, source + steps) for source in range(f...]
    dot_general x23 -> x0, matrix products: 90.9 us -> none  [the longest x1 11.9 us: local(): jnp.einsum('qhd,khd->hqk', attended_grad, value_heads, preferred_element_...]
    psum x4 -> x0, blocking collectives: 73.2 us -> none  [the longest x1 40 us: local(): lax.psum((norm1_part, table_part, spread_rows(norm2_part, column, width_d...]
    unnamed x130 -> x0, local copies, waits for them, and re-layouts: 61.1 us -> none
  transfers between devices with their start and end apart: 49 -> 0, of which waited for: 26 -> 0; matrix products, arithmetic and copies ran while one was open for 45% -> 0% of each run, Pallas kernels for 0% -> 0%
where the time goes in v4:
time: 340 us; the launch traced here: 336 us
  Pallas kernels  332 us (98%)
    pallas_call x1, Pallas kernels, forward_pass(): pl.pallas_call(functools.partial(forward_kernel, heads, experts, capacity...  259 us
    pallas_call x1, Pallas kernels, back_pass(): pl.pallas_call(functools.partial(back_kernel, heads, experts), out_shape=...  61.2 us
    pallas_call x1, Pallas kernels, finish(): pl.pallas_call(functools.partial(finish_kernel, heads, experts), out_shap...  12.1 us

profile of v4, /device:TPU:0, one launch (start us, length us, event | category | flops | bytes accessed | tf_op | source)
XLA Modules:
  0.0 336.0 jit_solution(329758211377822873)
XLA Ops:
  0.6 1.3 broadcast_in_dim.12.gain1_ref
  1.9 259.1 %shard_map.229 = (f32[4,128,384]{2,1,0:T(8,128)}, bf16[32,192,384]{2,1,0:T(8,128)(2,1)}, bf16[32,192,384]{2,1,0:T(8,128)(2,1)}, f32[128,768]{1,0:T(8,128)}, f32[...) custom-call(bf16[128,768]{1,0:T(8,128)(2,1)} %x_ref.3, ...), custom_call_target="tpu_custom_call" | custom-call | flops 24999999488 | bytes 50000000 | tf_op jit(solution)/shard_map/pallas_call | solution.py:1248
  261.0 61.2 %shard_map.230 = (f32[128,768]{1,0:T(8,128)}, f32[128,768]{1,0:T(8,128)}, f32[2,96,384]{2,1,0:T(8,128)}, f32[40,192]{1,0:T(8,128)}, f32[40,128]{1,0:T(8,128)}, /...) custom-call(bf16[128,768]{1,0:T(8,128)(2,1)} %x_ref.3, f32[1,768]{1,0:T(1,128)} %broadcast_in_dim.12.gain1_ref, ...), custom_call_target="tpu_custom_call" | custom-call | flops 20000000000 | bytes 40000000 | tf_op jit(solution)/shard_map/pallas_call | solution.py:1629
  322.2 12.1 %shard_map.231 = (f32[128,768]{1,0:T(8,128)}, f32[128,768]{1,0:T(8,128)}, f32[1,768]{1,0:T(1,128)}, f32[192,96]{1,0:T(8,128)}, f32[192,96]{1,0:T(8,128)}, /*inde...) custom-call(f32[128,768]{1,0:T(8,128)} %get-tuple-element.61.out_ref, ...), custom_call_target="tpu_custom_call" | custom-call | flops 10000000 | bytes 30000000 | tf_op jit(solution)/shard_map/pallas_call | solution.py:1726
  334.2 1.3 reduce

commit v5 on v4

--- a/solution.py
+++ b/solution.py
@@ -544,33 +544,48 @@
     def to_end(self, e):
         return remote(self.got.at[e], self.got.at[e], self.sems[3].at[e], self.sems[1].at[e], self.me.end)
 
-    def slot_free(self, e):
-        @pl.when(e >= self.ring)
-        def _():
-            self.to_mid(e - self.ring).wait_send()
-
     def put(self, e, value):
         self.own[lax.rem(e, self.ring)] = value
 
-        @pl.when(self.me.is_end)
+    def valid(self, e):
+        return jnp.logical_and(e >= 0, e < self.experts)
+
+    def send(self, e):
+        @pl.when(jnp.logical_and(self.me.is_end, self.valid(e)))
         def _():
+            @pl.when(e >= PACE)
+            def _():
+                self.to_mid(e - PACE).wait_send()
             self.to_mid(e).start()
 
     def half(self, e):
-        @pl.when(jnp.logical_and(self.me.is_mid, jnp.logical_and(e >= 0, e < self.experts)))
+        @pl.when(jnp.logical_and(self.me.is_mid, self.valid(e)))
         def _():
             sl = lax.rem(e + self.ring, self.ring)
             self.to_mid(e).wait_recv()
             self.own[sl] = (self.own[sl].astype(f32) + self.got[e].astype(f32)).astype(bf16)
+
+            @pl.when(e >= PACE)
+            def _():
+                self.across(e - PACE).wait_send()
             self.across(e).start()
 
     def whole(self, e):
-        @pl.when(jnp.logical_and(self.me.is_mid, jnp.logical_and(e >= 0, e < self.experts)))
+        @pl.when(jnp.logical_and(self.me.is_mid, self.valid(e)))
         def _():
             sl = lax.rem(e + self.ring, self.ring)
             self.across(e).wait_recv()
             self.got[e] = (self.own[sl].astype(f32) + self.other[e].astype(f32)).astype(bf16)
+
+            @pl.when(e >= PACE)
+            def _():
+                self.to_end(e - PACE).wait_send()
             self.to_end(e).start()
+
+    def tick(self, t):
+        self.send(t)
+        self.half(t - LAG_B)
+        self.whole(t - LAG_C)
 
     def await_total(self, e):
         @pl.when(self.me.is_end)
@@ -578,22 +593,21 @@
             self.to_end(e).wait_recv()
 
     def drain(self):
-        def sent(e, carry):
-            self.to_mid(e).wait_send()
-            return carry
-        lax.fori_loop(self.experts - self.ring, self.experts, sent, 0)
-
-        @pl.when(self.me.is_mid)
-        def _():
-            def out(e, carry):
+        for e in range(self.experts - PACE, self.experts):
+            @pl.when(self.me.is_end)
+            def _():
+                self.to_mid(e).wait_send()
+
+            @pl.when(self.me.is_mid)
+            def _():
+                self.across(e).wait_send()
                 self.to_end(e).wait_send()
-                return carry
-            lax.fori_loop(0, self.experts, out, 0)
 
 
 RING = 8
 GROUP = 4
 LAG_B, LAG_C, LAG_D = 2, 4, 6
+PACE = 2
 
 
 class LineGather:
@@ -733,6 +747,11 @@
         before = before + count[:, 127:128]
 
 
+POINTS = (2, 2, 2, 2, 2, 0, 2, 2, 2, 4, 1)
+AHEAD = 4
+KEEP = 12
+
+
 class BlockRows:
     def __init__(self, ref):
         self.ref = ref
@@ -797,11 +816,11 @@
 def forward_kernel(heads, experts, capacity,
                    x_ref, gain1_ref, wq_ref, wk_ref, wv_ref, wout_ref, table_ref, wr_ref, gain2_ref, doc_row,
                    choice_row, grad_ref, wh_hbm, wb_hbm,
-                   out_ref, gh_hbm, gb_hbm,
+                   out_ref, gh_hbm, gb_hbm, nh_hbm,
                    hidden_ref, normed_ref, router_ref, gate_ref, at_ref, q_ref, kv_ref, lse_ref, xb_ref,
                    wqkv_all, wout_all, small_all,
                    slot_ref, w1_ref, w2_ref, g_ref, g_out, rows_ref, rows_out, gs_ref,
-                   own_ref, ag_ref, other_ref, xs_ref, p_ref, got_ref, other2_ref,
+                   own_ref, ag_ref, other_ref, xs_ref, got_ref, other2_ref,
                    wq_st, wo_st, sm_st, at_in, y_in, s_in, line_out, line_in,
                    nat_sem, own_sem, got_sem, other_sem, t_sem, p_sem, got2_sem, other2_sem, t2_sem, gh_sem, gb_sem,
                    wqr_s, wqr_r, wql_s, wql_r, smr_s, smr_r, sml_s, sml_r,
@@ -826,25 +845,26 @@
     give = Dispatch(me, g_out, g_ref, gz_s, gz_r, gc_s, gc_r, gp_s, gp_r)
     rows = Dispatch(me, rows_out, rows_ref, rz_s, rz_r, rc_s, rc_r, rp_s, rp_r)
     acts = LineSum(me, own_ref, ag_ref, other_ref, own_sem, got_sem, other_sem, t_sem, experts)
-    pres = LineSum(me, p_ref, got_ref, other2_ref, p_sem, got2_sem, other2_sem, t2_sem, experts)
+    pres = LineSum(me, own_ref, got_ref, other2_ref, p_sem, got2_sem, other2_sem, t2_sem, experts)
     weights = LineGather(me, lambda z: wq_st.at[core, z], wqr_s, wqr_r, wql_s, wql_r)
     smalls = LineGather(me, lambda z: sm_st.at[z], smr_s, smr_r, sml_s, sml_r)
 
-    def act_step(i, carry):
-        @pl.when(i < experts)
+    def act_step(t):
+        @pl.when(t < experts)
         def _():
-            acts.slot_free(i)
-            gs = pick_rows(slot_ref, i * capacity, capacity, BlockRows(g_ref), tokens).astype(bf16)
-            gs_ref[i] = gs
-            acts.put(i, nn(gs, w2_ref[i]).astype(bf16))
-        acts.half(i - LAG_B)
-        acts.whole(i - LAG_C)
-        return carry
+            gs = pick_rows(slot_ref, t * capacity, capacity, BlockRows(g_ref), tokens).astype(bf16)
+            gs_ref[t] = gs
+            acts.put(t, nn(gs, w2_ref[t]).astype(bf16))
+        acts.tick(t)
 
     done = [0]
 
-    def act_steps(count):
-        lax.fori_loop(done[0], done[0] + count, act_step, 0)
+    def ticks(count):
+        def body(t, carry):
+            act_step(t)
+            return carry
+        if count:
+            lax.fori_loop(done[0], done[0] + count, body, 0)
         done[0] += count
 
     def xb_plane(k):
@@ -866,6 +886,9 @@
 
     def at_plane(k):
         return remote(at_ref.at[me.chips[k]], at_in.at[chip], at_s.at[k], at_r.at[k], me.on_plane(k))
+
+    def line_copy(k):
+        return remote(line_out.at[me.line[k]], line_in.at[k], lo_s.at[k], lo_r.at[k], me.on_line(k))
 
     barrier = pltpu.get_barrier_semaphore()
     friends = [me.on_line(k) for k in range(3)] + [me.on_plane(k) for k in range(3)] + [me.pair]
@@ -881,12 +904,10 @@
     g_ref[gx * 8 + gy] = g_out[gx]
     pl.semaphore_wait(barrier, len(friends))
     give.start()
-    weights.start()
     give.spread(0)
     for k in range(3):
         xb_plane(k).start()
     wq_pair(0).start()
-    smalls.start()
 
     def front(bias_ref, nat_ref, half_ref, one_ref, two_ref):
         def load_span(source, g, q):
@@ -916,29 +937,28 @@
         fill_bias(bias_ref, table_ref, chip, heads)
         for m in (1, 2, 3):
             give.spread(m)
-        for h in range(3):
+        weights.start()
+        smalls.start()
+        for g in range(spans):
+            turn_span(wb_hbm, w2_ref, g, lambda: load_spans(wb_hbm, g + 1) if g + 1 < spans else None)
+            if g > 0:
+                weights.receive(g - 1)
+                smalls.receive(g - 1)
+        give.share(0)
+        for h in range(spans - 1, 3):
             weights.receive(h)
             smalls.receive(h)
-
-        def back_body(g, carry):
-            def following():
-                @pl.when(g + 1 < spans)
-                def _():
-                    load_spans(wb_hbm, g + 1)
-            turn_span(wb_hbm, w2_ref, g, following)
-            return carry
-        lax.fori_loop(0, spans, back_body, 0)
         load_spans(wh_hbm, 0)
         for k in (1, 2, 3):
             wq_pair(k).start()
         for z in range(4):
             wo_st[gy, z] = wq_st[core, z][:, 3 * cols:]
+        for m in (1, 2, 3):
+            give.share(m)
+        give.arrive()
         for k in range(3):
             wo_plane(k).start()
-        for m in range(4):
-            give.share(m)
-        give.arrive()
-        act_steps(4)
+        ticks(POINTS[9])
         for k in range(4):
             wq_pair(k).wait_recv()
         for z in range(4):
@@ -958,10 +978,7 @@
             q_ref[c] = (made[:, :hd].astype(bf16).astype(f32) * scale).astype(bf16)
             kv_ref[2 * c + core] = made[:, hd:].astype(bf16)
             kv_pair(c).start()
-        for k in range(3):
-            wo_plane(k).wait_recv()
-            wo_pair(k).start()
-        act_steps(2)
+        ticks(POINTS[0])
         for c in range(4):
             kv_pair(c).wait_recv()
         lanes = lax.broadcasted_iota(jnp.int32, (local, hd), 1) // HSIZE
@@ -985,12 +1002,16 @@
                 at_plane(k).start()
             else:
                 at_in[chip] = total.astype(bf16)
-            act_steps(3)
+            ticks(POINTS[1 + k])
+        for k in range(3):
+            wo_plane(k).wait_recv()
+            wo_pair(k).start()
         small_all[...] = jnp.concatenate([sm_st[z] for z in range(4)], axis=1)
         for k in range(3):
             wo_pair(k).wait_recv()
         for z in range(4):
             wout_all[z * width:(z + 1) * width, :] = jnp.concatenate([wo_st[g, z] for g in range(8)], axis=1)
+        ticks(POINTS[10])
         for k in range(3):
             at_plane(k).wait_recv()
         attended = jnp.concatenate([at_in[c] for c in range(4)], axis=1)
@@ -1020,24 +1041,23 @@
         rows.start()
         rows_ref[gx * 8 + gy] = rows_out[gx]
         rows.spread(0)
-        act_steps(2)
+        ticks(POINTS[5])
         turn_span(wh_hbm, w1_ref, 0, lambda: load_spans(wh_hbm, 1))
         for m in (1, 2, 3):
             rows.spread(m)
-        act_steps(2)
+        ticks(POINTS[6])
         for n in range(1, spans):
             turn_span(wh_hbm, w1_ref, n, lambda: load_spans(wh_hbm, n + 1) if n + 1 < spans else None)
-            act_steps(1)
+            ticks(POINTS[7])
         for m in range(4):
             rows.share(m)
-        act_steps(1)
+        ticks(POINTS[8])
         rows.arrive()
 
     V = pltpu.VMEM
     pl.run_scoped(front, V((heads, local, 16 * local), f32), V((4, width, 1024), bf16), V((8, width, 512), bf16),
                   V((1024, 1024), bf16), V((512, 512), bf16))
     first_left = done[0]
-    per_step = -(-(experts + LAG_C - first_left) // LAG_D)
 
     def experts_part(y_own, y_out, s_out, gh_st, gb_st):
         def grad_copy(stage, target, sems, e):
@@ -1082,27 +1102,27 @@
                 from_owner(j, k).wait_recv()
                 pair_total(j, k + 1).start()
 
-        def step(i, carry):
-            @pl.when(i < LAG_D)
+        def step(t, carry):
+            i = t - experts + AHEAD
+
+            @pl.when(i == experts - PACE)
             def _():
-                for n in range(per_step):
-                    act_step(first_left + per_step * i + n, 0)
-
-            @pl.when(i < experts)
+                acts.drain()
+
+            @pl.when(jnp.logical_and(i >= 0, i < experts))
             def _():
-                pres.slot_free(i)
                 xs = pick_rows(slot_ref, i * capacity, capacity, BlockRows(rows_ref), tokens).astype(bf16)
-                xs_ref[lax.rem(i, RING)] = xs
+                xs_ref[lax.rem(i, KEEP)] = xs
                 pres.put(i, nn(xs[:, :width], w1_ref[i]).astype(bf16))
-            pres.half(i - LAG_B)
-            pres.whole(i - LAG_C)
-            e = i - LAG_D
+            act_step(t)
+            pres.tick(t - experts)
+            e = t - experts - LAG_D
 
             @pl.when(e >= 0)
             def _():
                 acts.await_total(e)
                 pres.await_total(e)
-                xs = xs_ref[lax.rem(e, RING)]
+                xs = xs_ref[lax.rem(e, KEEP)]
                 pieces = xs[:, width:].astype(f32)
                 gate = pieces[:, 0:1] + pieces[:, 1:2] + pieces[:, 2:3]
                 u = got_ref[e].astype(f32)
@@ -1153,7 +1173,7 @@
                     stage_four(j - 2)
             return carry
 
-        lax.fori_loop(0, experts + LAG_D, step, 0)
+        lax.fori_loop(first_left, 2 * experts + LAG_D, step, 0)
         last = groups - 1
         stage_two(last)
         stage_four(last - 1)
@@ -1182,15 +1202,11 @@
                 pair_total(j, k).wait_recv()
         total = total + picked(experts // many - 1)
 
-        def line_copy(k):
-            return remote(line_out.at[me.line[k]], line_in.at[k], lo_s.at[k], lo_r.at[k], me.on_line(k))
-
         for z in range(4):
             line_out[z] = total[z * local:(z + 1) * local].astype(bf16)
         for k in range(3):
             line_copy(k).start()
         out_ref[gx] = line_out[gx].astype(f32)
-        acts.drain()
         pres.drain()
         for e in (experts - 2, experts - 1):
             grad_copy(gh_st, gh_hbm, gh_sem, e).wait()
@@ -1215,15 +1231,44 @@
         for k in range(4):
             for copy in (wq_pair, kv_pair):
                 copy(k).wait_send()
+
+    def turn_part(one_ref, two_ref, in_ref, half_ref, nat_ref):
+        def load(g):
+            return pltpu.make_async_copy(gh_hbm.at[:, :, g * 128:(g + 1) * 128], in_ref, gh_sem.at[0])
+
+        def store(g, q):
+            at = nh_hbm.at[:, g * 4096 + q * 1024:g * 4096 + (q + 1) * 1024]
+            return pltpu.make_async_copy(nat_ref.at[q], at, nat_sem.at[q])
+
+        load(0).start()
+        fill_moves(one_ref, two_ref, False)
+        for g in range(spans):
+            load(g).wait()
+            for r in range(8):
+                gathered = jnp.concatenate([in_ref[4 * r + n] for n in range(4)], axis=1)
+                moved = nn(gathered, two_ref[...]).astype(bf16)
+                for q in range(4):
+                    half_ref[q, :, r * 128:(r + 1) * 128] = moved[:, q * 128:(q + 1) * 128]
+            if g + 1 < spans:
+                load(g + 1).start()
+            for q in range(4):
+                if g > 0:
+                    store(g - 1, q).wait()
+                nat_ref[q] = nn(half_ref[q], one_ref[...]).astype(bf16)
+                store(g, q).start()
         for k in range(3):
             line_copy(k).wait_recv()
             out_ref[me.line_from[k]] = line_in[k].astype(f32)
         for k in range(3):
             line_copy(k).wait_send()
+        for q in range(4):
+            store(spans - 1, q).wait()
 
     block = (groups, GROUP, half, 2 * width)
     pl.run_scoped(experts_part, V(block, bf16), V(block, bf16), V(block, bf16),
                   V((2, width, units), bf16), V((2, width, units), bf16))
+    pl.run_scoped(turn_part, V((1024, 1024), bf16), V((512, 512), bf16), V((experts, width, 128), bf16),
+                  V((4, width, 1024), bf16), V((4, width, 1024), bf16))
 
 
 def forward_pass(x_in, gain1, wq, wk, wv, wout, table, wr, gain2, doc_row, choice_row, grad_out, w_hidden, w_back,
@@ -1244,13 +1289,13 @@
     dma = pltpu.SemaphoreType.DMA
     shape = jax.ShapeDtypeStruct
     V = pltpu.VMEM
-    ring = 8
     return pl.pallas_call(
         functools.partial(forward_kernel, heads, experts, capacity),
         out_shape=(
             shape((4, local, 2 * width), f32),
             shape((experts, width, units), bf16),
             shape((experts, width, units), bf16),
+            shape((width, experts * units), bf16),
             shape((local, features), f32),
             shape((local, features), f32),
             shape((local, experts), f32),
@@ -1265,21 +1310,21 @@
             shape((experts + 8, features), f32),
         ),
         in_specs=[vm] * 6 + [sm] + [vm] * 5 + [hbm] * 2,
-        out_specs=(vm, hbm, hbm) + (vm,) * 12,
+        out_specs=(vm, hbm, hbm, hbm) + (vm,) * 12,
         scratch_shapes=[
             V((1, tokens), jnp.int32),
             V((experts, width, units), bf16), V((experts, width, units), bf16),
             V((32, local, width), bf16), V((4, local, width), bf16),
             V((32, local, width + 64), bf16), V((4, local, width + 64), bf16),
             V((experts, capacity, width), bf16),
-            V((ring, capacity, units), bf16), V((experts, capacity, units), bf16), V((experts, capacity, units), bf16),
-            V((RING, capacity, width + 64), bf16),
-            V((RING, capacity, units), bf16), V((experts, capacity, units), bf16), V((experts, capacity, units), bf16),
+            V((experts, capacity, units), bf16), V((experts, capacity, units), bf16), V((experts, capacity, units), bf16),
+            V((KEEP, capacity, width + 64), bf16),
+            V((experts, capacity, units), bf16), V((experts, capacity, units), bf16),
             V((2, 4, width, 4 * cols), bf16), V((8, 4, width, cols), bf16), V((4, experts + 8, width), f32),
             V((4, local, hd), bf16),
             V((groups, GROUP, half, 2 * width), bf16), V((groups, 3, half, 2 * width), bf16),
             V((4, local, 2 * width), bf16), V((3, local, 2 * width), bf16),
-        ] + [dma((n,)) for n in (4, ring, experts, experts, experts, RING, experts, experts, experts, 2, 2)]
+        ] + [dma((n,)) for n in (4, experts, experts, experts, experts, experts, experts, experts, experts, 2, 2)]
         + [dma((3,))] * 8
         + [dma((n,)) for n in (3, 3, 4, 4, 3, 3, 3, 3, 4, 4, 3, 3, 3, 3, 3, 3, 3, 3)]
         + [dma((4, 3)), dma((4, 3)), dma((4, 4)), dma((4, 4))] * 2
@@ -1297,8 +1342,8 @@
 def back_kernel(heads, experts,
                 x_ref, gain1_ref, grad_ref, choice_row, doc_row, table_ref,
                 hidden_ref, normed_ref, router_ref, gate_ref, at_ref, q_ref, kv_ref, lse_ref, xb_ref,
-                wqkv_all, wout_all, small_all, ret_ref, gh_hbm, gb_hbm,
-                out_ref, gin_ref, wgrad_ref, small_out, tail_out, nh_hbm, nb_hbm,
+                wqkv_all, wout_all, small_all, ret_ref, gb_hbm,
+                out_ref, gin_ref, wgrad_ref, small_out, tail_out, nb_hbm,
                 bias_ref, ag_ref, dq_ref, dk_ref, dv_ref, near_ref, go_ref, fg_ref, top_ref,
                 one_ref, two_ref, in_ref, half_ref, nat_ref,
                 sp_out, sp_in, sc_out, sc_in, sz_out, sz_in,
@@ -1314,14 +1359,14 @@
     hd = q_ref.shape[2]
     cols = hd // 2
     seq = 8 * local
-    spans = gh_hbm.shape[2] // 128
+    spans = gb_hbm.shape[2] // 128
 
     barrier = pltpu.get_barrier_semaphore()
     friends = [me.on_line(k) for k in range(3)] + [me.on_plane(k) for k in range(3)] + [me.pair]
     for device in friends:
         pl.semaphore_signal(barrier, inc=1, device_id=device, device_id_type=MESH)
 
-    work = [(gh_hbm, nh_hbm, g) for g in range(spans)] + [(gb_hbm, nb_hbm, g) for g in range(spans)]
+    work = [(gb_hbm, nb_hbm, g) for g in range(spans)]
 
     def load(i):
         at = work[i][0].at[:, :, work[i][2] * 128:(work[i][2] + 1) * 128]
@@ -1550,7 +1595,6 @@
         t_plane(k).start()
     weight_line(1, own_1)
     turn_span(0)
-    turn_span(1)
     for k in range(3):
         t_plane(k).wait_recv()
     tail = jnp.zeros((40, 128), f32)
@@ -1562,8 +1606,7 @@
     tz_out[...] = tail
     for k in range(3):
         t_line(k).start()
-    turn_span(2)
-    turn_span(3)
+    turn_span(1)
 
     first = fg_ref[...]
     for k in range(3):
@@ -1580,8 +1623,7 @@
         small_line(k).wait_recv()
         total = total + sz_in[k]
     small_out[...] = total
-    turn_span(4)
-    turn_span(5)
+    turn_span(2)
     for p in range(2):
         total = wz_out[p, gx].astype(f32)
         for k in range(3):
@@ -1610,11 +1652,11 @@
             copy(k).wait_send()
 
 
-def back_pass(x_in, gain1, grad_out, choice_row, doc_row, table, saved, returned, gh, gb, collective_id):
+def back_pass(x_in, gain1, grad_out, choice_row, doc_row, table, saved, returned, gb, collective_id):
     local, features = x_in.shape
     width = features // 4
     hidden, normed, router, gate, attended, queries, keyvals, lse, xb, wqkv, wout, small = saved
-    experts, _, units = gh.shape
+    experts, _, units = gb.shape
     hd = queries.shape[2]
     cols = hd // 2
     heads = hd // HSIZE
@@ -1635,10 +1677,9 @@
             shape((rows, width), f32),
             shape((40, 128), f32),
             shape((width, experts * units), bf16),
-            shape((width, experts * units), bf16),
         ),
-        in_specs=[vm] * 5 + [sm] + [vm] * 13 + [hbm] * 2,
-        out_specs=(vm,) * 5 + (hbm,) * 2,
+        in_specs=[vm] * 5 + [sm] + [vm] * 13 + [hbm],
+        out_specs=(vm,) * 5 + (hbm,),
         scratch_shapes=[
             V((heads, local, 16 * local), f32),
             V((4, local, features), bf16), V((4, local, hd), bf16), V((hd, seq), f32), V((hd, seq), f32),
@@ -1660,7 +1701,7 @@
             collective_id=collective_id, has_side_effects=True, vmem_limit_bytes=62 * 2**20),
         cost_estimate=pl.CostEstimate(flops=20 * 10**9, bytes_accessed=40 * 10**6, transcendentals=2 * 10**6),
     )(x_in, gain1, grad_out, choice_row, doc_row, table, hidden, normed, router, gate, attended, queries, keyvals, lse,
-      xb, wqkv, wout, small, returned, gh, gb)
+      xb, wqkv, wout, small, returned, gb)
 
 
 def finish_kernel(heads, experts,
@@ -1761,7 +1802,7 @@
     gain_row = norm1_gain[None, :]
     choice_row, doc_row = expert_choice[None, :], doc_ids[None, :]
     table = relative_bias_table.T
-    returned, hidden_grads, back_grads, *saved = forward_pass(
+    returned, _, back_grads, natural_hidden, *saved = forward_pass(
         x_in,
         gain_row,
         w_query,
@@ -1778,7 +1819,7 @@
         w_back,
         1,
     )
-    results = back_pass(
+    *results, natural_back = back_pass(
         x_in,
         gain_row,
         grad_out,
@@ -1787,7 +1828,6 @@
         table,
         saved,
         returned,
-        hidden_grads,
         back_grads,
         2,
     )
@@ -1804,7 +1844,7 @@
         grad_router,
         grad_hidden,
         grad_back,
-    ) = finish(*results, table.shape[0])
+    ) = finish(*results, natural_hidden, natural_back, table.shape[0])
     return (
         out_rows,
         input_rows,

time: 340 us -> 334 us (0.982)
  Pallas kernels: 332 us -> 328 us
    pallas_call x1, Pallas kernels: 61.2 us -> 52.1 us  [back_pass(): pl.pallas_call(functools.partial(back_kernel, heads, experts), out_shape=...]
    pallas_call x1, Pallas kernels: 259 us -> 264 us  [forward_pass(): pl.pallas_call(functools.partial(forward_kernel, heads, experts, capacity...]
where the time goes in v5:
time: 334 us; the launch traced here: 331 us
  Pallas kernels  328 us (98%)
    pallas_call x1, Pallas kernels, forward_pass(): pl.pallas_call(functools.partial(forward_kernel, heads, experts, capacity...  264 us
    pallas_call x1, Pallas kernels, back_pass(): pl.pallas_call(functools.partial(back_kernel, heads, experts), out_shape=...  52.1 us
    pallas_call x1, Pallas kernels, finish(): pl.pallas_call(functools.partial(finish_kernel, heads, experts), out_shap...  12.1 us

profile of v5, /device:TPU:0, one launch (start us, length us, event | category | flops | bytes accessed | tf_op | source)
XLA Modules:
  0.0 331.4 jit_solution(5228949023124629640)
XLA Ops:
  0.6 1.3 broadcast_in_dim.12.gain1_ref
  1.9 263.9 %shard_map.229 = (f32[4,128,384]{2,1,0:T(8,128)}, bf16[32,192,384]{2,1,0:T(8,128)(2,1)}, bf16[32,192,384]{2,1,0:T(8,128)(2,1)}, bf16[192,12288]{1,0:T(8,128)(2,1...) custom-call(bf16[128,768]{1,0:T(8,128)(2,1)} %x_ref.3, ...), custom_call_target="tpu_custom_call" | custom-call | flops 24999999488 | bytes 50000000 | tf_op jit(solution)/shard_map/pallas_call | solution.py:1292
  265.8 52.1 %shard_map.230 = (f32[128,768]{1,0:T(8,128)}, f32[128,768]{1,0:T(8,128)}, f32[2,96,384]{2,1,0:T(8,128)}, f32[40,192]{1,0:T(8,128)}, f32[40,128]{1,0:T(8,128)}, /*index=5*/bf16[192,12288]{1,0:T(8,128)(2,1)}) custom-call(bf16[128,768]{1,0:T(8,128)(2,1)} %x_ref.3, f32[1,768]{1,0:T(1,128)} %broadcast_in_dim.12.gain1_ref, bf16[128,768]{1,0:T(8,128)(2,1)} %grad_ref.3, ...), custom_call_target="tpu_custom_call" | custom-call | flops 20000000000 | bytes 40000000 | tf_op jit(solution)/shard_map/pallas_call | solution.py:1671
  317.9 12.1 %shard_map.231 = (f32[128,768]{1,0:T(8,128)}, f32[128,768]{1,0:T(8,128)}, f32[1,768]{1,0:T(1,128)}, f32[192,96]{1,0:T(8,128)}, f32[192,96]{1,0:T(8,128)}, /*inde...) custom-call(f32[128,768]{1,0:T(8,128)} %get-tuple-element.59.out_ref, ...), custom_call_target="tpu_custom_call" | custom-call | flops 10000000 | bytes 30000000 | tf_op jit(solution)/shard_map/pallas_call | solution.py:1767
  330.0 1.3 reduce

commit v6 on v5

--- a/solution.py
+++ b/solution.py
@@ -973,7 +973,7 @@
                 xb_plane(k - 1).wait_recv()
             xc = xb_ref[c].astype(f32)
             r1 = lax.rsqrt(jnp.mean(xc * xc, axis=-1, keepdims=True) + epsilon)
-            xn = (xc * r1 * gain1_ref[...]).astype(bf16)
+            xn = (xc * r1 * gain1_ref[...].reshape(1, x_ref.shape[1])).astype(bf16)
             made = nn(xn, wqkv_all[...])
             q_ref[c] = (made[:, :hd].astype(bf16).astype(f32) * scale).astype(bf16)
             kv_ref[2 * c + core] = made[:, hd:].astype(bf16)
@@ -1509,7 +1509,7 @@
         return xc * lax.rsqrt(jnp.mean(xc * xc, axis=-1, keepdims=True) + epsilon)
 
     xr = [xn_block(c) for c in range(4)]
-    xn = jnp.concatenate([(v * gain1_ref[...]).astype(bf16) for v in xr], axis=0)
+    xn = jnp.concatenate([(v * gain1_ref[...].reshape(1, features)).astype(bf16) for v in xr], axis=0)
 
     def packed(value, z):
         top, mid, bottom = z * width, z * width + width // 2, (z + 1) * width
@@ -1614,7 +1614,7 @@
         first = first + fg_in[k].astype(f32)
     x = x_ref[...].astype(f32)
     r1 = lax.rsqrt(jnp.mean(x * x, axis=-1, keepdims=True) + epsilon)
-    gained1 = first * gain1_ref[...]
+    gained1 = first * gain1_ref[...].reshape(1, features)
     dot1 = jnp.sum(gained1 * x, axis=-1, keepdims=True)
     gin_ref[...] = gin_ref[...] + r1 * gained1 - x * (r1 * r1 * r1) * (dot1 / features)
 
@@ -1728,7 +1728,7 @@
     out_to[...] = out_ref[...]
     gin_to[...] = gin_ref[...]
     for n in range(6):
-        norm1_to[:, n * 128:(n + 1) * 128] = tail_ref[experts + n:experts + n + 1, :]
+        norm1_to[n * 128:(n + 1) * 128] = tail_ref[experts + n, :]
     parts = []
     for p in range(2):
         rows = wgrad_ref[p]
@@ -1767,7 +1767,7 @@
     return pl.pallas_call(
         functools.partial(finish_kernel, heads, experts),
         out_shape=(
-            shape(local, features), shape(local, features), shape(1, features),
+            shape(local, features), shape(local, features), shape(features),
             shape(width, cols), shape(width, cols), shape(width, cols), shape(heads, experts), shape(cols, width),
             shape(1, width), shape(experts, width), shape(width, natural), shape(width, natural),
         ),
@@ -1799,12 +1799,11 @@
     doc_ids,
     grad_out,
 ):
-    gain_row = norm1_gain[None, :]
     choice_row, doc_row = expert_choice[None, :], doc_ids[None, :]
     table = relative_bias_table.T
     returned, _, back_grads, natural_hidden, *saved = forward_pass(
         x_in,
-        gain_row,
+        norm1_gain,
         w_query,
         w_key,
         w_value,
@@ -1821,7 +1820,7 @@
     )
     *results, natural_back = back_pass(
         x_in,
-        gain_row,
+        norm1_gain,
         grad_out,
         choice_row,
         doc_row,
@@ -1848,7 +1847,7 @@
     return (
         out_rows,
         input_rows,
-        grad_norm1[0],
+        grad_norm1,
         grad_query,
         grad_key,
         grad_value,

time: 334 us -> 332 us (level)
  no operation moved by 1% of the time
where the time goes in v6:
time: 332 us; the launch traced here: 329 us
  Pallas kernels  328 us (99%)
    pallas_call x1, Pallas kernels, forward_pass(): pl.pallas_call(functools.partial(forward_kernel, heads, experts, capacity...  264 us
    pallas_call x1, Pallas kernels, back_pass(): pl.pallas_call(functools.partial(back_kernel, heads, experts), out_shape=...  52.1 us
    pallas_call x1, Pallas kernels, finish(): pl.pallas_call(functools.partial(finish_kernel, heads, experts), out_shap...  12.1 us

profile of v6, /device:TPU:0, one launch (start us, length us, event | category | flops | bytes accessed | tf_op | source)
XLA Modules:
  0.0 329.0 jit_solution(15026115744675163401)
XLA Ops:
  0.6 263.9 %shard_map.229 = (f32[4,128,384]{2,1,0:T(8,128)}, bf16[32,192,384]{2,1,0:T(8,128)(2,1)}, bf16[32,192,384]{2,1,0:T(8,128)(2,1)}, bf16[192,12288]{1,0:T(8,128)(2,1...) custom-call(bf16[128,768]{1,0:T(8,128)(2,1)} %x_ref.3, ...), custom_call_target="tpu_custom_call" | custom-call | flops 24999999488 | bytes 50000000 | tf_op jit(solution)/shard_map/pallas_call | solution.py:1292
  264.6 52.1 %shard_map.230 = (f32[128,768]{1,0:T(8,128)}, f32[128,768]{1,0:T(8,128)}, f32[2,96,384]{2,1,0:T(8,128)}, f32[40,192]{1,0:T(8,128)}, f32[40,128]{1,0:T(8,128)}, /*index=5*/bf16[192,12288]{1,0:T(8,128)(2,1)}) custom-call(bf16[128,768]{1,0:T(8,128)(2,1)} %x_ref.3, f32[768]{0:T(1024)} %gain1_ref.3, bf16[128,768]{1,0:T(8,128)(2,1)} %grad_ref.3, ...), custom_call_target="tpu_custom_call" | custom-call | flops 20000000000 | bytes 40000000 | tf_op jit(solution)/shard_map/pallas_call | solution.py:1671
  316.7 12.1 %shard_map.231 = (f32[128,768]{1,0:T(8,128)}, f32[128,768]{1,0:T(8,128)}, f32[768]{0:T(1024)}, f32[192,96]{1,0:T(8,128)}, f32[192,96]{1,0:T(8,128)}, /*index=5*/...) custom-call(f32[128,768]{1,0:T(8,128)} %get-tuple-element.59.out_ref, ...), custom_call_target="tpu_custom_call" | custom-call | flops 10000000 | bytes 30000000 | tf_op jit(solution)/shard_map/pallas_call | solution.py:1767
